TPU v7x, 32 devices: a whole 2x2x4 slice. The times are simulated.
32 devices in a mesh: fsdp: 4 (over y, core), ctx: 4 (over z), tp: 2 (over x).
Axes of the slice: x: 2, y: 2, z: 4, core: 2. Of those that a mesh axis runs over, the one named last changes fastest.
Arguments:
- inputs: bfloat16 [4, 1024, 1536], P('fsdp', 'ctx'), may hold values from -6 to 6
- cotangent: bfloat16 [4, 1024, 1536], P('fsdp', 'ctx'), may hold values from -6 to 6
- doc_bounds: int32 [4, 2], P('fsdp'), may hold values from 1 to 1023, as said below
- attn_gain: bfloat16 [1536], P(('fsdp', 'ctx')), may hold values from 0.5 to 1.5
- w_query: bfloat16 [1536, 1536], P(('fsdp', 'ctx'), 'tp'), may hold values from -0.15625 to 0.15625
- w_key: bfloat16 [1536, 512], P(('fsdp', 'ctx'), 'tp'), may hold values from -0.15625 to 0.15625
- w_value: bfloat16 [1536, 512], P(('fsdp', 'ctx'), 'tp'), may hold values from -0.15625 to 0.15625
- w_output: bfloat16 [1536, 1536], P('tp', ('fsdp', 'ctx')), may hold values from -2.5 to 2.5
- query_gain: bfloat16 [64], P(('fsdp', 'ctx')), may hold values from 0.099609375 to 1.8984375
- key_gain: bfloat16 [64], P(('fsdp', 'ctx')), may hold values from 0.099609375 to 1.8984375
- ffn_gain: bfloat16 [1536], P(('fsdp', 'ctx')), may hold values from 0.5 to 1.5
- w_gate: bfloat16 [1536, 6912], P(('fsdp', 'ctx'), 'tp'), may hold values from -0.15625 to 0.15625
- w_up: bfloat16 [1536, 6912], P(('fsdp', 'ctx'), 'tp'), may hold values from -0.15625 to 0.15625
- w_down: bfloat16 [6912, 1536], P('tp', ('fsdp', 'ctx')), may hold values from -0.078125 to 0.078125
Outputs:
- result: bfloat16 [4, 1024, 1536], P('fsdp', 'ctx')
- grad_inputs: float32 [4, 1024, 1536], P('fsdp', 'ctx')
- grad_attn_gain: float32 [1536], P(('fsdp', 'ctx'))
- grad_query: float32 [1536, 1536], P(('fsdp', 'ctx'), 'tp')
- grad_key: float32 [1536, 512], P(('fsdp', 'ctx'), 'tp')
- grad_value: float32 [1536, 512], P(('fsdp', 'ctx'), 'tp')
- grad_output: float32 [1536, 1536], P('tp', ('fsdp', 'ctx'))
- grad_query_gain: float32 [64], P(('fsdp', 'ctx'))
- grad_key_gain: float32 [64], P(('fsdp', 'ctx'))
- grad_ffn_gain: float32 [1536], P(('fsdp', 'ctx'))
- grad_gate: float32 [1536, 6912], P(('fsdp', 'ctx'), 'tp')
- grad_up: float32 [1536, 6912], P(('fsdp', 'ctx'), 'tp')
- grad_down: float32 [6912, 1536], P('tp', ('fsdp', 'ctx'))
Inputs may be any that keep to these rules, and one draw needn't show every extreme that they name: Each sequence holds three documents: the second begins at doc_bounds[s,0], one of the indices 1 to 255, the third at doc_bounds[s,1], one of the indices 1024 - 255 to 1023.
All inputs are finite; a program needn't handle non-finite values.
Results may differ from a plain program's by a relative error of at most 0.02.
Values may be sent and summed in bfloat16 or wider, within the bound.
No kernel may reach another device: no remote copies, remote signals or barrier semaphores. Data moves between devices by JAX's collectives and lax.ppermute only.
A program may use at most 192 MiB of HBM per device.

v0:
```python
import functools
import math

import jax
import jax.numpy as jnp
from jax import lax
from jax.experimental import pallas as pl
from jax.experimental.pallas import tpu as pltpu
from jax.sharding import PartitionSpec as P

HQ = 24
HK = 8
HEAD = 64
GROUP = HQ // HK


EPS = 1e-05
THETA = 1000000.0
LINE = 4
LOG2E = math.log2(math.e)
LOW = jnp.bfloat16
VMEM = pl.BlockSpec(memory_space=pltpu.VMEM)
SMEM = pl.BlockSpec(memory_space=pltpu.SMEM)
ANY = pl.BlockSpec(memory_space=pl.ANY)
PARAMS = pltpu.CompilerParams(vmem_limit_bytes=52 * 1024 * 1024)


def inverse_rms(values):
    return lax.rsqrt(jnp.mean(values * values, axis=-1, keepdims=True) + EPS)


def norm_back(values, inverse, gain, grads):
    scaled = grads * gain
    return inverse * scaled - values * (inverse * inverse * inverse) * jnp.mean(
        scaled * values, axis=-1, keepdims=True
    )


def contract_rows(left, right):
    return lax.dot_general(
        left, right, (((0,), (0,)), ((), ())), preferred_element_type=jnp.float32
    )


def contract_cols(left, right):
    return lax.dot_general(
        left, right, (((1,), (1,)), ((), ())), preferred_element_type=jnp.float32
    )


def tables(first, rows, bounds):
    index = first + jnp.arange(rows, dtype=jnp.int32)
    begin = jnp.where(index >= bounds[1], bounds[1], jnp.where(index >= bounds[0], bounds[0], 0))
    freq = THETA ** (-(jnp.arange(HEAD // 2, dtype=jnp.float32) * 2.0 / HEAD))
    angle = (index - begin).astype(jnp.float32)[:, None] * freq[None, :]
    cosine = jnp.cos(angle)
    sine = jnp.sin(angle)
    return (
        jnp.concatenate([cosine, cosine, cosine, cosine], axis=1),
        jnp.concatenate([-sine, sine, -sine, sine], axis=1),
    )


def shaped(shape, dtype=LOW):
    return jax.ShapeDtypeStruct(shape, dtype)


def cost(micros):
    return pl.CostEstimate(
        flops=int(micros * 9e8), bytes_accessed=int(micros * 1e6), transcendentals=0
    )


def pair_inverse(x):
    lane=lax.broadcasted_iota(jnp.int32,x.shape,1)
    left=lane<HEAD
    sq=x*x
    a=jnp.sum(jnp.where(left,sq,0.0),axis=-1,keepdims=True)
    b=jnp.sum(jnp.where(left,0.0,sq),axis=-1,keepdims=True)
    return lax.rsqrt(jnp.where(left,a,b)*(1.0/HEAD)+EPS)

def pair_mean(x):
    lane=lax.broadcasted_iota(jnp.int32,x.shape,1)
    left=lane<HEAD
    a=jnp.sum(jnp.where(left,x,0.0),axis=-1,keepdims=True)
    b=jnp.sum(jnp.where(left,0.0,x),axis=-1,keepdims=True)
    return jnp.where(left,a,b)*(1.0/HEAD)

def partner(x):
    lane=lax.broadcasted_iota(jnp.int32,x.shape,1)
    front=lax.rem(lane,HEAD)<HEAD//2
    return jnp.where(front,pltpu.roll(x,2*HEAD-HEAD//2,1),pltpu.roll(x,HEAD//2,1))

def kprep_kernel(kv_ref,gain_ref,cos_ref,sin_ref,out_ref):
    width=kv_ref.shape[1]//2
    for i in range(width//128):
        x=kv_ref[:,128*i:128*(i+1)]
        xn=x*pair_inverse(x)*gain_ref[...]
        out_ref[:,128*i:128*(i+1)]=(xn*cos_ref[...]+partner(xn)*sin_ref[...]).astype(jnp.bfloat16)
    out_ref[:,width:]=kv_ref[:,width:].astype(jnp.bfloat16)

def bias_of(first_key,first_row,bounds_ref,keys,rows):
    key=first_key+lax.broadcasted_iota(jnp.int32,(keys,rows),0)
    row=first_row+lax.broadcasted_iota(jnp.int32,(keys,rows),1)
    b0=bounds_ref[0]; b1=bounds_ref[1]
    begin=jnp.where(row>=b1,b1,jnp.where(row>=b0,b0,0))
    return jnp.where((key<=row)&(key>=begin),0.0,-1e30)

def fwd_kernel(slots, where_ref, bounds_ref, q_ref, *refs):
    kv_refs = refs[:slots]
    gain_ref, cos_ref, sin_ref, qr_ref, ob_ref, oT_ref, qs, ks, vs, bias = refs[slots:]
    rows, width = kv_refs[0].shape
    width //= 2
    heads = q_ref.shape[1] // HEAD
    kvh = width // HEAD
    me = where_ref[slots]
    for i in range(heads // 2):
        at = slice(2 * HEAD * i, 2 * HEAD * (i + 1))
        x = q_ref[:, at]
        xn = x * pair_inverse(x) * gain_ref[...]
        qr_ref[:, at] = (xn * cos_ref[...] + partner(xn) * sin_ref[...]).astype(LOW)
    for h in range(heads):
        qs[h] = qr_ref[:, HEAD * h : HEAD * (h + 1)]
    for j in range(slots):
        for k in range(kvh):
            ks[j * kvh + k] = kv_refs[j][:, HEAD * k : HEAD * (k + 1)]
            vT = kv_refs[j][:, width + HEAD * k : width + HEAD * (k + 1)].astype(jnp.float32).T
            vs[j * kvh + k] = jnp.concatenate([vT, jnp.ones_like(vT)], axis=0).astype(LOW)
    oT_ref[...] = jnp.zeros_like(oT_ref)

    def step(t, carry):
        c = where_ref[t // kvh]
        k = lax.rem(t, kvh)

        @pl.when((c <= me) & (c >= 0))
        def _():
            @pl.when(k == 0)
            def _():
                bias[...] = bias_of(c * rows, me * rows, bounds_ref, rows, rows)

            kb = ks[t]
            vaug = vs[t]
            for g in range(GROUP):
                s = contract_cols(kb, qs[k * GROUP + g])
                p = jnp.exp2(s * (0.125 * LOG2E) + bias[...]).astype(LOW)
                oT_ref[k, :, g * rows : (g + 1) * rows] += jnp.dot(
                    vaug, p, preferred_element_type=jnp.float32
                )

        return carry

    lax.fori_loop(0, slots * kvh, step, 0)
    for k in range(kvh):
        oT = oT_ref[k, :HEAD, :] * (1.0 / oT_ref[k, HEAD : HEAD + 1, :])
        oT_ref[k, :HEAD, :] = oT
        for g in range(GROUP):
            h = k * GROUP + g
            ob_ref[:, HEAD * h : HEAD * (h + 1)] = oT[:, g * rows : (g + 1) * rows].T.astype(LOW)


def bwd_kernel(slots, where_ref, bounds_ref, q_ref, qr_ref, dob_ref, oT_ref, *refs):
    kv_refs = refs[:slots]
    gain_ref, cos_ref, sin_ref, _, _, dqb_ref = refs[slots : slots + 6]
    dkv_refs = refs[slots + 6 : 2 * slots + 6]
    gg_ref, qs, ds_, ks, vs, kTs, dks, dvs, logl, delta, dqT, bias = refs[2 * slots + 6 :]
    rows, width = kv_refs[0].shape
    width //= 2
    heads = q_ref.shape[1] // HEAD
    kvh = width // HEAD
    me = where_ref[slots]
    for h in range(heads):
        k, g = h // GROUP, h % GROUP
        at = slice(g * rows, (g + 1) * rows)
        qs[h] = qr_ref[:, HEAD * h : HEAD * (h + 1)]
        d = dob_ref[:, HEAD * h : HEAD * (h + 1)]
        ds_[h] = d
        dT = d.astype(jnp.float32).T
        delta[k, :, at] = jnp.broadcast_to(
            jnp.sum(dT * oT_ref[k, :HEAD, at], axis=0, keepdims=True), (8, rows)
        )
    for k in range(kvh):
        logl[k] = jnp.broadcast_to(jnp.log2(oT_ref[k, HEAD : HEAD + 1, :]), logl.shape[1:])
    for j in range(slots):
        for k in range(kvh):
            t = j * kvh + k
            kb = kv_refs[j][:, HEAD * k : HEAD * (k + 1)]
            ks[t] = kb
            vs[t] = kv_refs[j][:, width + HEAD * k : width + HEAD * (k + 1)]
            kTs[t] = kb.astype(jnp.float32).T.astype(LOW)
    dqT[...] = jnp.zeros_like(dqT)

    def step(t, carry):
        c = where_ref[t // kvh]
        k = lax.rem(t, kvh)
        seen = (c <= me) & (c >= 0)

        @pl.when(seen)
        def _():
            @pl.when(k == 0)
            def _():
                bias[...] = bias_of(c * rows, me * rows, bounds_ref, rows, rows)

            kb = ks[t]
            vb = vs[t]
            kT = kTs[t]
            dk = jnp.zeros((rows, HEAD), jnp.float32)
            dv = jnp.zeros((rows, HEAD), jnp.float32)
            for g in range(GROUP):
                at = slice(g * rows, (g + 1) * rows)
                qh = qs[k * GROUP + g]
                dh = ds_[k * GROUP + g]
                s = contract_cols(kb, qh)
                p = jnp.exp2(s * (0.125 * LOG2E) + (bias[...] - logl[k, 0:1, at]))
                dp = contract_cols(vb, dh)
                ds = (p * (dp - delta[k, 0:1, at])).astype(LOW)
                dv += jnp.dot(p.astype(LOW), dh, preferred_element_type=jnp.float32)
                dk += jnp.dot(ds, qh, preferred_element_type=jnp.float32)
                dqT[k, :, at] += jnp.dot(kT, ds, preferred_element_type=jnp.float32)
            dks[t] = (dk * 0.125).astype(LOW)
            dvs[t] = dv.astype(LOW)

        @pl.when(jnp.logical_not(seen))
        def _():
            dks[t] = jnp.zeros((rows, HEAD), LOW)
            dvs[t] = jnp.zeros((rows, HEAD), LOW)

        return carry

    lax.fori_loop(0, slots * kvh, step, 0)
    for j in range(slots):
        for k in range(kvh):
            t = j * kvh + k
            dkv_refs[j][:, HEAD * k : HEAD * (k + 1)] = dks[t]
            dkv_refs[j][:, width + HEAD * k : width + HEAD * (k + 1)] = dvs[t]
    gg = jnp.zeros((1, 2 * HEAD), jnp.float32)
    for i in range(heads // 2):
        at = slice(2 * HEAD * i, 2 * HEAD * (i + 1))
        pair = []
        for h in (2 * i, 2 * i + 1):
            k, g = h // GROUP, h % GROUP
            pair.append(dqT[k, :, g * rows : (g + 1) * rows].T * 0.125)
        d = jnp.concatenate(pair, axis=1)
        x = q_ref[:, at]
        inv = pair_inverse(x)
        dn = d * cos_ref[...] - partner(d) * sin_ref[...]
        gg += jnp.sum(dn * x * inv, axis=0, keepdims=True)
        sc = dn * gain_ref[...]
        dqb_ref[:, at] = (inv * sc - x * (inv * inv * inv) * pair_mean(sc * x)).astype(LOW)
    gg_ref[...] = gg


def kback_kernel(kv_ref, d_ref, gain_ref, cos_ref, sin_ref, *refs):
    out_ref, gg_ref = refs[-2:]
    width = kv_ref.shape[1] // 2
    gg = jnp.zeros((1, 2 * HEAD), jnp.float32)
    for i in range(width // (2 * HEAD)):
        at = slice(2 * HEAD * i, 2 * HEAD * (i + 1))
        x = kv_ref[:, at]
        d = d_ref[:, at]
        inv = pair_inverse(x)
        dn = d * cos_ref[...] - partner(d) * sin_ref[...]
        gg += jnp.sum(dn * x * inv, axis=0, keepdims=True)
        sc = dn * gain_ref[...]
        out_ref[:, at] = (inv * sc - x * (inv * inv * inv) * pair_mean(sc * x)).astype(LOW)
    out_ref[:, width:] = d_ref[:, width:].astype(LOW)
    gg_ref[...] = gg


def prepare_keys(kv, gain, cosine, sine):
    return pl.pallas_call(
        kprep_kernel,
        out_shape=shaped(kv.shape),
        in_specs=[VMEM] * 4,
        out_specs=VMEM,
        compiler_params=PARAMS,
        name="keys",
        cost_estimate=cost(1),
    )(kv, gain, cosine, sine)


def attend(where, bounds, q, kv, gain, cosine, sine):
    slots = len(kv)
    rows, width = kv[0].shape
    heads = width // 2 // HEAD
    return pl.pallas_call(
        functools.partial(fwd_kernel, slots),
        out_shape=(
            shaped(q.shape),
            shaped(q.shape),
            shaped((heads, 2 * HEAD, GROUP * rows), jnp.float32),
        ),
        in_specs=[SMEM, SMEM] + [VMEM] * (4 + slots),
        out_specs=(VMEM,) * 3,
        scratch_shapes=[
            pltpu.VMEM((heads * GROUP, rows, HEAD), LOW),
            pltpu.VMEM((slots * heads, rows, HEAD), LOW),
            pltpu.VMEM((slots * heads, 2 * HEAD, rows), LOW),
            pltpu.VMEM((rows, rows), jnp.float32),
        ],
        compiler_params=PARAMS,
        name="attend",
        cost_estimate=cost(14),
    )(where, bounds, q, *kv, gain, cosine, sine)


def attend_back(where, bounds, q, qr, dob, mixed, kv, gain, cosine, sine, later):
    slots = len(kv)
    rows, width = kv[0].shape
    heads = width // 2 // HEAD
    return pl.pallas_call(
        functools.partial(bwd_kernel, slots),
        out_shape=(shaped(q.shape),)
        + (shaped(kv[0].shape),) * slots
        + (shaped((1, 2 * HEAD), jnp.float32),),
        in_specs=[SMEM, SMEM] + [VMEM] * (7 + slots) + [ANY] * 2,
        out_specs=(VMEM,) * (2 + slots),
        scratch_shapes=[
            pltpu.VMEM((heads * GROUP, rows, HEAD), LOW),
            pltpu.VMEM((heads * GROUP, rows, HEAD), LOW),
            pltpu.VMEM((slots * heads, rows, HEAD), LOW),
            pltpu.VMEM((slots * heads, rows, HEAD), LOW),
            pltpu.VMEM((slots * heads, HEAD, rows), LOW),
            pltpu.VMEM((slots * heads, rows, HEAD), LOW),
            pltpu.VMEM((slots * heads, rows, HEAD), LOW),
            pltpu.VMEM((heads, 8, GROUP * rows), jnp.float32),
            pltpu.VMEM((heads, 8, GROUP * rows), jnp.float32),
            pltpu.VMEM((heads, HEAD, GROUP * rows), jnp.float32),
            pltpu.VMEM((rows, rows), jnp.float32),
        ],
        compiler_params=PARAMS,
        name="attend_back",
        cost_estimate=cost(17),
    )(where, bounds, q, qr, dob, mixed, *kv, gain, cosine, sine, *later)


def keys_back(kv, grads, gain, cosine, sine, later=()):
    return pl.pallas_call(
        kback_kernel,
        out_shape=(shaped(kv.shape), shaped((1, 2 * HEAD), jnp.float32)),
        in_specs=[VMEM] * 5 + [ANY] * len(later),
        out_specs=(VMEM,) * 2,
        compiler_params=PARAMS,
        name="keys_back",
        cost_estimate=cost(1),
    )(kv, grads, gain, cosine, sine, *later)


def normed_back(grad_query, grad_kv, query, kv, tokens, inverse):
    def kernel(dq, dkv, wq, wkv, x, inv, out, gain):
        terms = contract_cols(dq[...], wq[...]) + contract_cols(dkv[...], wkv[...])
        out[...] = terms.astype(LOW)
        gain[...] = jnp.sum(
            terms * (x[...].astype(jnp.float32) * inv[...]), axis=0, keepdims=True
        )

    rows, model = tokens.shape
    return pl.pallas_call(
        kernel,
        out_shape=(shaped((rows, model)), shaped((1, model), jnp.float32)),
        in_specs=[VMEM] * 6,
        out_specs=(VMEM,) * 2,
        compiler_params=PARAMS,
        name="normed_back",
        cost_estimate=cost(4),
    )(grad_query, grad_kv, query, kv, tokens, inverse)


def begin(copies):
    for copy in copies:
        copy.start()


def finish(copies):
    for copy in copies:
        copy.wait()


def collect(parts, later=()):
    count = len(parts)

    def kernel(*refs):
        out, sems = refs[-2:]
        copies = [pltpu.make_async_copy(refs[i], out.at[i], sems.at[i]) for i in range(count)]
        begin(copies)
        finish(copies)

    return pl.pallas_call(
        kernel,
        out_shape=shaped((count,) + parts[0].shape, parts[0].dtype),
        in_specs=[ANY] * (count + len(later)),
        out_specs=VMEM,
        scratch_shapes=[pltpu.SemaphoreType.DMA((count,))],
        compiler_params=PARAMS,
        name="collect",
        cost_estimate=cost(1),
    )(*parts, *later)


def chunks_of(width):
    return ((0, width),)


def split_columns(where, weights):
    count = len(weights)
    share, width = weights[0].shape
    parts = 4
    width //= parts
    chunks = chunks_of(width)

    def kernel(where_ref, *refs):
        me = where_ref[where.shape[0] - 1]
        ins, outs = refs[:count], refs[count:]
        for column in range(parts):
            for bit in range(parts):

                @pl.when(column ^ bit == me)
                def _():
                    for j, (begin, end) in enumerate(chunks):
                        at = slice(column * width + begin, column * width + end)
                        for i in range(count):
                            outs[j * parts + bit][i] = ins[i][:, at]

    outs = pl.pallas_call(
        kernel,
        out_shape=tuple(
            shaped((count, share, end - begin)) for begin, end in chunks for _ in range(parts)
        ),
        in_specs=[SMEM] + [VMEM] * count,
        out_specs=(VMEM,) * (parts * len(chunks)),
        compiler_params=PARAMS,
        name="split_columns",
        cost_estimate=cost(3),
    )(where, *weights)
    return [outs[j * parts : (j + 1) * parts] for j in range(len(chunks))]


def join_columns(where, slots):
    parts = len(slots[0])
    count, share, _ = slots[0][0].shape
    width = sum(chunk[0].shape[-1] for chunk in slots)
    chunks = chunks_of(width)

    def kernel(where_ref, *refs):
        me = where_ref[where.shape[0] - 1]
        ins, outs = refs[: parts * len(chunks)], refs[parts * len(chunks) :]
        for column in range(parts):
            for bit in range(parts):

                @pl.when(column ^ bit == me)
                def _():
                    for j, (begin, end) in enumerate(chunks):
                        at = slice(column * width + begin, column * width + end)
                        for i in range(count):
                            outs[i][:, at] = ins[j * parts + bit][i].astype(jnp.float32)

    return pl.pallas_call(
        kernel,
        out_shape=(shaped((share, width * parts), jnp.float32),) * count,
        in_specs=[SMEM] + [VMEM] * (parts * len(chunks)),
        out_specs=(VMEM,) * count,
        compiler_params=PARAMS,
        name="join_columns",
        cost_estimate=cost(4),
    )(where, *[part for chunk in slots for part in chunk])


def arrange(where, slots, share, pieces):
    own, both, across = slots
    size, rows, width = own.shape
    parts = 4
    more = rows - share
    piece = width // pieces

    def kernel(where_ref, *refs):
        me = where_ref[size + 1]
        own, both, across = refs[:3]
        outs, sems = refs[3:-1], refs[-1]
        ins = [own, both.at[0], across, both.at[1]]
        copies = []
        for bit in range(parts):
            for step in range(size):
                index = (me ^ bit) * size + where_ref[step]
                row = pl.multiple_of(index * share, share)
                for i in range(pieces):
                    copies.append(
                        pltpu.make_async_copy(
                            ins[bit].at[step, pl.ds(0, share), pl.ds(i * piece, piece)],
                            outs[i].at[pl.ds(row, share)],
                            sems.at[i, bit, step],
                        )
                    )
                if more:
                    copies.append(
                        pltpu.make_async_copy(
                            ins[bit].at[step, pl.ds(share, more)],
                            outs[pieces].at[index],
                            sems.at[pieces, bit, step],
                        )
                    )
        begin(copies)
        finish(copies)

    shapes = [shaped((parts * size * share, piece))] * pieces
    if more:
        shapes.append(shaped((parts * size, more, width)))
    return pl.pallas_call(
        kernel,
        out_shape=tuple(shapes),
        in_specs=[SMEM] + [ANY] * 3,
        out_specs=(VMEM,) * len(shapes),
        scratch_shapes=[pltpu.SemaphoreType.DMA((pieces + 1, parts, size))],
        compiler_params=PARAMS,
        name="arrange",
        cost_estimate=cost(2),
    )(where, *slots)


def token_copies(refs, whole, sems):
    own, both, across = refs
    rows = own.shape[0]
    pairs = ((own, 0), (both.at[0], 1), (across, 2), (both.at[1], 3))
    return [
        pltpu.make_async_copy(ref, whole.at[pl.ds(i * rows, rows)], sems.at[i]) for ref, i in pairs
    ]


def weight_copies(where_ref, ref, m, whole, sems):
    size, parts, _, share, _ = ref.shape
    me = where_ref[size + 1]
    copies = []
    for c in range(size):
        for bit in range(parts):
            row = pl.multiple_of(((me ^ bit) * size + c) * share, share)
            copies.append(
                pltpu.make_async_copy(
                    ref.at[c, bit, m], whole.at[pl.ds(row, share)], sems.at[c * parts + bit]
                )
            )
    return copies


def ffn(where, tokens, pulled, weights, before=(), later=()):
    rows, model = tokens[0].shape
    size, parts, _, _, width = weights.shape
    total = rows * parts

    def kernel(where_ref, *refs):
        weights_ref = refs[6]
        more = len(before)
        sums = refs[7 : 7 + more]
        refs = refs[: 7 + more] + refs[7 + more + len(later) :]
        keep, send, middle, d_gate, d_up = refs[7 + more : 12 + more]
        hn, cot, w_gate, w_up, w_down, sem_h, sem_c, sem_g, sem_u, sem_d = refs[12 + more :]
        gates = weight_copies(where_ref, weights_ref, 0, w_gate, sem_g)
        reads = token_copies(refs[:3], hn, sem_h)
        ups = weight_copies(where_ref, weights_ref, 1, w_up, sem_u)
        pulls = token_copies(refs[3:6], cot, sem_c)
        downs = weight_copies(where_ref, weights_ref, 2, w_down, sem_d)
        for copies in (gates, reads, ups, pulls, downs):
            begin(copies)

        def token_part(i, carry):
            at = pl.ds(pl.multiple_of(i * rows, rows), rows)

            @pl.when(i == 0)
            def _():
                finish(gates)
                finish(reads)

            g = jnp.dot(hn[at], w_gate[...], preferred_element_type=jnp.float32)

            @pl.when(i == 0)
            def _():
                finish(ups)

            u = jnp.dot(hn[at], w_up[...], preferred_element_type=jnp.float32)
            sigma = jax.nn.sigmoid(g)
            active = g * sigma
            middle[at] = (active * u).astype(LOW)

            @pl.when(i == 0)
            def _():
                finish(pulls)
                finish(downs)

            d = jnp.dot(cot[at], w_down[...], preferred_element_type=jnp.float32)
            d_gate[at] = (d * u * sigma * (1.0 + g * (1.0 - sigma))).astype(LOW)
            d_up[at] = (d * active).astype(LOW)
            back = contract_cols(d_gate[at], w_gate[...]) + contract_cols(d_up[at], w_up[...])
            index = i // 2
            for j, out in enumerate((keep, send)):

                @pl.when(lax.rem(i, 2) == j)
                def _():
                    if more:
                        out[index] = (back + sums[j][index].astype(jnp.float32)).astype(LOW)
                    else:
                        out[index] = back.astype(LOW)

            return carry

        lax.fori_loop(0, parts, token_part, 0)

    return pl.pallas_call(
        kernel,
        out_shape=(shaped((2, rows, model)),) * 2 + (shaped((total, width)),) * 3,
        in_specs=[SMEM] + [ANY] * 7 + [VMEM] * len(before) + [ANY] * len(later),
        out_specs=(VMEM,) * 5,
        scratch_shapes=[pltpu.VMEM((total, model), LOW)] * 2
        + [pltpu.VMEM((model, width), LOW)] * 3
        + [pltpu.SemaphoreType.DMA((4,))] * 2
        + [pltpu.SemaphoreType.DMA((size * parts,))] * 3,
        compiler_params=PARAMS,
        name="ffn",
        cost_estimate=cost(15),
    )(where, *tokens, *pulled, weights, *before, *later)


def ffn_out(where, middles, weights, later):
    count = len(weights)
    size, parts, _, share, _ = weights[0].shape
    model = parts * size * share
    rows = middles[0].shape[0] // parts

    def kernel(where_ref, *refs):
        mids, weight_refs = refs[:count], refs[count : 2 * count]
        keep, send = refs[2 * count + 1 : 2 * count + 3]
        downs, sems = refs[2 * count + 3 : 3 * count + 3], refs[3 * count + 3 :]
        copies = [
            weight_copies(where_ref, weight_refs[j], 2, downs[j], sems[j]) for j in range(count)
        ]
        for each in copies:
            begin(each)
        for each in copies:
            finish(each)

        def token_part(i, carry):
            at = pl.ds(pl.multiple_of(i * rows, rows), rows)
            d = sum(contract_cols(mids[j][at], downs[j][...]) for j in range(count)).astype(LOW)
            index = i // 2

            @pl.when(lax.rem(i, 2) == 0)
            def _():
                keep[index] = d

            @pl.when(lax.rem(i, 2) == 1)
            def _():
                send[index] = d

            return carry

        lax.fori_loop(0, parts, token_part, 0)

    return pl.pallas_call(
        kernel,
        out_shape=(shaped((2, rows, model)), shaped((2, rows, model))),
        in_specs=[SMEM] + [VMEM] * count + [ANY] * (count + 1),
        out_specs=(VMEM,) * 2,
        scratch_shapes=[pltpu.VMEM((model, each.shape[-1]), LOW) for each in weights]
        + [pltpu.SemaphoreType.DMA((size * parts,))] * count,
        compiler_params=PARAMS,
        name="ffn_out",
        cost_estimate=cost(9),
    )(where, *middles, *weights, later)


def hidden_grads(where, tokens, rights, pulled, lasts, later=()):
    rows, model = tokens[0].shape
    lefts = len(rights)
    rights = rights + lasts
    count = len(rights)
    size = where.shape[0] - 2
    total, width = rights[0].shape
    parts = total // rows
    tall = model // parts
    share = tall // size

    def kernel(where_ref, *refs):
        refs = refs[: 6 + count] + refs[6 + count + len(later) :]
        out = refs[6 + count]
        left, right, stage, sem_h, sem_c, sem_r, sem_o = refs[7 + count :]
        me = where_ref[size + 1]
        reads = token_copies(refs[:3], left.at[0], sem_h)
        pulls = token_copies(refs[3:6], left.at[1], sem_c)
        operands = [
            pltpu.make_async_copy(refs[6 + m], right.at[m], sem_r.at[m]) for m in range(count)
        ]
        begin(reads)
        begin(operands)
        begin(pulls)

        def write(i, c):
            m, part = i // parts, lax.rem(i, parts)
            return pltpu.make_async_copy(
                stage.at[i, pl.ds(c * share, share)], out.at[c, me ^ part, m], sem_o.at[i, c]
            )

        def block(i, carry):
            m, part = i // parts, lax.rem(i, parts)

            @pl.when(i == 0)
            def _():
                finish(reads)

            for k in range(count):

                @pl.when(i == k * parts)
                def _():
                    operands[k].wait()

            @pl.when(i == lefts * parts)
            def _():
                finish(pulls)

            column = pl.multiple_of(part * tall, tall)
            which = (m >= lefts).astype(jnp.int32)
            stage[i] = contract_rows(left[which, :, pl.ds(column, tall)], right[m]).astype(LOW)
            for c in range(size):
                write(i, c).start()
            return carry

        lax.fori_loop(0, count * parts, block, 0)

        def drain(i, carry):
            for c in range(size):
                write(i, c).wait()
            return carry

        lax.fori_loop(0, count * parts, drain, 0)

    return pl.pallas_call(
        kernel,
        out_shape=shaped((size, parts, count, share, width)),
        in_specs=[SMEM] + [ANY] * (6 + count + len(later)),
        out_specs=ANY,
        scratch_shapes=[
            pltpu.VMEM((2, total, model), LOW),
            pltpu.VMEM((count, total, width), LOW),
            pltpu.VMEM((count * parts, tall, width), LOW),
            pltpu.SemaphoreType.DMA((4,)),
            pltpu.SemaphoreType.DMA((4,)),
            pltpu.SemaphoreType.DMA((count,)),
            pltpu.SemaphoreType.DMA((count * parts, size)),
        ],
        compiler_params=PARAMS,
        name="hidden_grads",
        cost_estimate=cost(3 * count),
    )(where, *tokens, *pulled, *rights, *later)


def head_grads(where, lefts, rights, gains=None, small=0, later=()):
    count = len(lefts)
    model = lefts[0].shape[1]
    each = rights[0].shape[1]
    width = each * count
    size = where.shape[0] - 2
    parts = 4
    tall = model // parts
    share = tall // size
    pad = 16 if gains else 0
    gains = gains or []

    def kernel(where_ref, *refs):
        left_refs, right_refs, refs = refs[:count], refs[count : 2 * count], refs[2 * count :]
        keep, send = refs[-2:]
        me = where_ref[size + 1]
        here = where_ref[size]

        def place(bit, c):
            return bit // 2, lax.rem(here - c + size, size) if size <= LINE else c

        def block(part, carry):
            column = pl.multiple_of(part * tall, tall)
            bit = me ^ part
            for m in range(count):
                grads = contract_rows(
                    left_refs[m][:, pl.ds(column, tall)], right_refs[m][...]
                ).astype(LOW)
                for out, odd in ((keep, 0), (send, 1)):

                    @pl.when(lax.rem(bit, 2) == odd)
                    def _():
                        for c in range(size):
                            index, step = place(bit, c)
                            out[index, step, :share, m * each : (m + 1) * each] = grads[
                                c * share : (c + 1) * share
                            ]

            return carry

        lax.fori_loop(0, parts, block, 0)
        if pad:
            pairs = [gain[:, :HEAD] + gain[:, HEAD:] for gain in refs[2:4]]
            for part in range(parts):
                bit = me ^ part
                for c in range(size):
                    i = part * size + c
                    index, step = place(bit, c)
                    pieces = [gain[:, i * share : (i + 1) * share] for gain in refs[:2]]
                    pieces += [pair[:, i * small : (i + 1) * small] for pair in pairs]
                    row = jnp.concatenate(
                        [
                            jnp.concatenate(
                                [piece, jnp.zeros((1, 128 - piece.shape[1]), jnp.float32)], axis=1
                            )
                            for piece in pieces
                        ],
                        axis=1,
                    )
                    tile = jnp.broadcast_to(row, (pad, width)).astype(LOW)
                    for out, odd in ((keep, 0), (send, 1)):

                        @pl.when(lax.rem(bit, 2) == odd)
                        def _():
                            out[index, step, share:] = tile

    return pl.pallas_call(
        kernel,
        out_shape=(shaped((2, size, share + pad, width)),) * 2,
        in_specs=[SMEM] + [VMEM] * (2 * count + len(gains)) + [ANY] * len(later),
        out_specs=(VMEM,) * 2,
        compiler_params=PARAMS,
        name="head_grads",
        cost_estimate=cost(3),
    )(where, *lefts, *rights, *gains, *later)


def flip(part, bit):
    size = lax.axis_size("fsdp")
    return lax.ppermute(part, "fsdp", [(i, i ^ bit) for i in range(size)])


def swap(part):
    return lax.ppermute(part, "tp", [(0, 1), (1, 0)])


def turn(part):
    size = lax.axis_size("ctx")
    return lax.ppermute(part, "ctx", [(i, (i + 1) % size) for i in range(size)])


def ctx_slots(part):
    size = lax.axis_size("ctx")
    if size > LINE:
        whole = lax.all_gather(part, "ctx", axis=0)
        return [whole[i] for i in range(size)]
    slots = [part]
    for _ in range(1, size):
        slots.append(turn(slots[-1]))
    return slots


def ctx_sum(terms):
    size = lax.axis_size("ctx")
    if size > LINE:
        return lax.psum_scatter(terms, "ctx", scatter_dimension=0, tiled=False).astype(jnp.float32)
    moving = terms[1]
    for step in range(1, size):
        total = turn(moving).astype(jnp.float32) + terms[(step + 1) % size].astype(jnp.float32)
        moving = total.astype(LOW)
    return total


def back_slots(part):
    size = lax.axis_size("ctx")
    if size > LINE:
        whole = lax.all_gather(part, "ctx", axis=0)
        return [whole[i] for i in range(size)]
    slots = [part]
    for step in range(1, size):
        slots.append(lax.ppermute(part, "ctx", [(i, i + step) for i in range(size - step)]))
    return slots


def back_sum(terms):
    size = lax.axis_size("ctx")
    if size > LINE:
        total = lax.psum_scatter(jnp.stack(terms), "ctx", scatter_dimension=0, tiled=False)
        return total.astype(jnp.float32), total
    parts = [terms[0]] + [
        lax.ppermute(terms[step], "ctx", [(i, i - step) for i in range(step, size)])
        for step in range(1, size)
    ]
    return sum(part.astype(jnp.float32) for part in parts), parts[1]


def group_tokens(part):
    across = flip(part, 2)
    return (part, flip(collect([part, across]), 1), across)


def chip_sum(keep, send):
    beside = flip(send, 1)
    far = keep[1].astype(jnp.float32) + beside[1].astype(jnp.float32)
    near = keep[0].astype(jnp.float32) + beside[0].astype(jnp.float32)
    return near, far.astype(LOW)


def pair_sum(near, far):
    return near + flip(far, 2).astype(jnp.float32)


def group_sum(keep, send):
    return pair_sum(*chip_sum(keep, send))


def gather_all(where, slots, share, later=()):
    own = collect(slots, later)
    across = flip(own, 2)
    both = flip(collect([own, across]), 1)
    return arrange(where, [own, both, across], share, 1), across


def scatter_hidden(terms):
    size, parts, count, share, width = terms.shape
    own = lax.psum_scatter(terms.reshape(-1, width), "ctx", scatter_dimension=0, tiled=True)
    own = own.reshape(parts, count, share, width)
    return [own[0]] + [flip(own[bit], bit) for bit in range(1, parts)]


def body(
    inputs,
    cotangent,
    doc_bounds,
    attn_gain,
    w_query,
    w_key,
    w_value,
    w_output,
    query_gain,
    key_gain,
    ffn_gain,
    w_gate,
    w_up,
    w_down,
):
    parts = lax.axis_size("fsdp")
    size = lax.axis_size("ctx")
    tensor = lax.axis_size("tp")
    me = lax.axis_index("ctx")
    share = w_query.shape[0]
    model = share * parts * size
    width = HQ // tensor * HEAD
    kv_width = HK // tensor * HEAD
    small = query_gain.shape[0]
    shards = parts * size
    steps = jnp.arange(size, dtype=jnp.int32)
    slots_at = lax.rem(me - steps + size, size) if size <= LINE else steps
    where = jnp.concatenate(
        [slots_at, jnp.stack([me, lax.axis_index("fsdp")]).astype(jnp.int32)]
    )
    bounds = doc_bounds[0]

    split = split_columns(where, [w_gate, w_up, w_down.T])
    gains = jnp.concatenate([attn_gain, ffn_gain, query_gain, key_gain])
    pad = 16
    gain_rows = jnp.zeros((pad, 2 * kv_width), LOW).at[0, : gains.shape[0]].set(gains)
    kv_block = jnp.concatenate([jnp.concatenate([w_key, w_value], axis=1), gain_rows], axis=0)
    traded = [
        [part[0]] + [flip(part[bit], bit) for bit in range(1, parts)] for part in split
    ]
    kv_slots = ctx_slots(kv_block)
    query_slots = ctx_slots(w_query)
    output_slots = ctx_slots(w_output.T)
    (full_kv, gain_rows), kv_across = gather_all(where, kv_slots, share)
    (full_query,), query_across = gather_all(where, query_slots, share, [kv_across])
    (full_output,), output_across = gather_all(where, output_slots, share, [query_across])
    weights = []
    for chunk in traded:
        block = collect(chunk, [kv_slots[-1]])
        weights.append(
            lax.all_gather(
                block.reshape(-1, block.shape[-1]), "ctx", axis=0, tiled=True
            ).reshape(size, *block.shape)
        )
    pulled_all = group_tokens(collect([cotangent[0]], [output_across])[0])
    all_gains = gain_rows[:, 0].astype(jnp.float32)
    gain_attn = all_gains[:, :share].reshape(model)
    gain_ffn = all_gains[:, share : 2 * share].reshape(model)
    gain_query = jnp.tile(all_gains[:, 2 * share : 2 * share + small].reshape(HEAD), 2)[None]
    gain_key = jnp.tile(
        all_gains[:, 2 * share + small : 2 * share + 2 * small].reshape(HEAD), 2
    )[None]

    pulled = cotangent[0]

    tokens = inputs[0].astype(jnp.float32)
    rows = tokens.shape[0]
    cosine, sine = tables(me * rows, rows, bounds)
    first_inv = inverse_rms(tokens)
    normed = (tokens * first_inv * gain_attn).astype(LOW)
    keys_values = jnp.dot(normed, full_kv, preferred_element_type=jnp.float32)
    own_kv = prepare_keys(keys_values, gain_key, cosine, sine)
    kv = back_slots(own_kv)
    queries = jnp.dot(normed, full_query, preferred_element_type=jnp.float32)
    query_rot, mixed_low, mixed = attend(where, bounds, queries, kv, gain_query, cosine, sine)
    branch_part = contract_cols(mixed_low, full_output).astype(LOW)
    branch = branch_part.astype(jnp.float32) + swap(branch_part).astype(jnp.float32)
    hidden = tokens + branch
    second_inv = inverse_rms(hidden)
    hidden_normed = (hidden * second_inv * gain_ffn).astype(LOW)

    hidden_all = group_tokens(hidden_normed)
    keep, send, middle, grad_gate_low, grad_up_low = ffn(
        where, hidden_all, pulled_all, weights[0]
    )
    near, far = chip_sum(keep, send)
    normed_part = pair_sum(near, far).astype(LOW)
    terms = hidden_grads(
        where, hidden_all, [grad_gate_low, grad_up_low], pulled_all, [middle], [far]
    )
    grad_gate, grad_up, grad_down = join_columns(where, [scatter_hidden(terms)])
    grad_down = grad_down.T
    feed_terms = ffn_out(where, [middle], weights, normed_part)
    grad_normed_ffn = normed_part.astype(jnp.float32) + swap(normed_part).astype(jnp.float32)

    ffn_gain_part = jnp.sum(grad_normed_ffn * hidden * second_inv, axis=0) * 0.5
    grad_hidden = pulled.astype(jnp.float32) + norm_back(
        hidden, second_inv, gain_ffn, grad_normed_ffn
    )
    grad_hidden_low = grad_hidden.astype(LOW)
    grad_mixed = jnp.dot(
        grad_hidden_low, full_output, preferred_element_type=jnp.float32
    ).astype(LOW)
    grad_query_low, *key_terms, query_gain_pair = attend_back(
        where, bounds, queries, query_rot, grad_mixed, mixed, kv, gain_query, cosine, sine,
        [terms, feed_terms[0]],
    )
    near, far = chip_sum(
        *head_grads(where, [normed, grad_hidden_low], [grad_query_low, mixed_low])
    )
    heads_sum = ctx_sum(pair_sum(near, far).astype(LOW))
    moved = collect(key_terms[1:], [far])
    own_terms, _ = back_sum([key_terms[0]] + [moved[i] for i in range(size - 1)])
    grad_query = heads_sum[:, :width]
    grad_output = heads_sum[:, width:].T
    feed_part = group_sum(*feed_terms).astype(LOW)
    feed = feed_part.astype(jnp.float32) + swap(feed_part).astype(jnp.float32)
    result = (hidden + feed).astype(LOW)[None]
    grad_kv_low, key_gain_pair = keys_back(
        keys_values,
        own_terms,
        gain_key,
        cosine,
        sine,
    )
    normed_low, attn_gain_part = normed_back(
        grad_query_low, grad_kv_low, full_query, full_kv, inputs[0], first_inv
    )
    own_kv = ctx_sum(
        group_sum(
            *head_grads(
                where,
                [normed],
                [grad_kv_low],
                [attn_gain_part, ffn_gain_part[None], query_gain_pair, key_gain_pair],
                small,
            )
        ).astype(LOW)
    )
    grad_key = own_kv[:share, :kv_width]
    grad_value = own_kv[:share, kv_width:]
    grad_normed = normed_low.astype(jnp.float32) + swap(normed_low).astype(jnp.float32)
    own_gains = own_kv[share].astype(LOW)
    grad_gains = own_gains.astype(jnp.float32) + swap(own_gains).astype(jnp.float32)
    grad_inputs = grad_hidden + norm_back(tokens, first_inv, gain_attn, grad_normed)
    return (
        result,
        grad_inputs[None],
        grad_gains[:share],
        grad_query,
        grad_key,
        grad_value,
        grad_output,
        grad_gains[256 : 256 + small],
        grad_gains[384 : 384 + small],
        grad_gains[128 : 128 + share],
        grad_gate,
        grad_up,
        grad_down,
    )


def solution(mesh):
    vector = P(("fsdp", "ctx"))
    columns = P(("fsdp", "ctx"), "tp")
    tall = P("tp", ("fsdp", "ctx"))
    act = P("fsdp", "ctx", None)
    return jax.shard_map(
        body,
        mesh=mesh,
        in_specs=(
            act,
            act,
            P("fsdp", None),
            vector,
            columns,
            columns,
            columns,
            tall,
            vector,
            vector,
            vector,
            columns,
            columns,
            tall,
        ),
        out_specs=(
            act,
            act,
            vector,
            columns,
            columns,
            columns,
            tall,
            vector,
            vector,
            vector,
            columns,
            columns,
            tall,
        ),
        check_vma=False,
    )
```

profile of v0, /device:TPU:0, one launch (start us, length us, event | category | flops | bytes accessed | tf_op | source)
XLA Modules:
  0.0 542.3 jit_solution(10248110434371428513)
XLA Ops:
  7.4 3.1 split_columns.1
  15.5 5.6 %collective-permute-done.refs_1_ = bf16[112,512]{1,0:T(8,128)(2,1)S(1)} collective-permute-done((bf16[112,512]{1,0:T(8,128)(2,1)S(1)}, bf16[112,512]{1,0:T(8,128)(2,1)S(1)}, u32[]{:S(2)}, u32[]{:S(2)}) %collective-permute-start) | collective-permute-done | bytes 114720 | tf_op jit(solution)/shard_map/ppermute | solution.py:839
  21.1 6.6 %collective-permute-done.1.refs_2_ = bf16[112,512]{1,0:T(8,128)(2,1)S(1)} collective-permute-done((bf16[112,512]{1,0:T(8,128)(2,1)S(1)}, bf16[112,512]{1,0:T(8,128)(2,1)S(1)}, u32[]{:S(2)}, u32[]{:S(2)}) %collective-permute-start.1) | collective-permute-done | bytes 114720 | tf_op jit(solution)/shard_map/ppermute | solution.py:839
  27.8 6.6 %collective-permute-done.2.refs_3_.refs_4_ = bf16[112,512]{1,0:T(8,128)(2,1)S(1)} collective-permute-done((bf16[112,512]{1,0:T(8,128)(2,1)S(1)}, bf16[112,512]{1,0:T(8,128)(2,1)S(1)}, u32[]{:S(2)}, u32[]{:S(2)}) %collective-permute-start.2) | collective-permute-done | bytes 114720 | tf_op jit(solution)/shard_map/ppermute | solution.py:839
  37.4 3.4 collect.20
  47.1 2.5 collective-permute-done.5.refs_1_
  51.6 6.3 %collective-permute-done.6.refs_2_ = bf16[96,768]{1,0:T(8,128)(2,1)S(1)} collective-permute-done((bf16[96,768]{1,0:T(8,128)(2,1)S(1)}, bf16[96,768]{1,0:T(8,128)(2,1)S(1)}, u32[]{:S(2)}, u32[]{:S(2)}) %collective-permute-start.6) | collective-permute-done | bytes 147488 | tf_op jit(solution)/shard_map/ppermute | solution.py:839
  60.0 8.4 %collective-permute-done.7.refs_3_ = bf16[96,768]{1,0:T(8,128)(2,1)S(1)} collective-permute-done((bf16[96,768]{1,0:T(8,128)(2,1)S(1)}, bf16[96,768]{1,0:T(8,128)(2,1)S(1)}, u32[]{:S(2)}, u32[]{:S(2)}) %collective-permute-start.7) | collective-permute-done | bytes 147488 | tf_op jit(solution)/shard_map/ppermute | solution.py:839
  69.2 2.6 collective-permute-start.8
  72.7 14.1 %collective-permute-done.14.refs_2_ = bf16[96,768]{1,0:T(8,128)(2,1)S(1)} collective-permute-done((bf16[96,768]{1,0:T(8,128)(2,1)S(1)}, bf16[96,768]{1,0:T(8,128)(2,1)S(1)}, u32[]{:S(2)}, u32[]{:S(2)}) %collective-permute-start.14) | collective-permute-done | bytes 147488 | tf_op jit(solution)/shard_map/ppermute | solution.py:839
  88.4 9.6 %collective-permute-done.15.refs_3_ = bf16[96,768]{1,0:T(8,128)(2,1)S(1)} collective-permute-done((bf16[96,768]{1,0:T(8,128)(2,1)S(1)}, bf16[96,768]{1,0:T(8,128)(2,1)S(1)}, u32[]{:S(2)}, u32[]{:S(2)}) %collective-permute-start.15) | collective-permute-done | bytes 147488 | tf_op jit(solution)/shard_map/ppermute | solution.py:839
  101.5 4.4 arrange.3
  112.2 8.8 %collective-permute-start.11 = (bf16[256,512]{1,0:T(8,128)(2,1)S(1)}, bf16[256,512]{1,0:T(8,128)(2,1)}, u32[]{:S(2)}, u32[]{:S(2)}) collective-permute-start(bf16[256,512]{1,0:T(8,128)(2,1)S(1)} %keys.1.refs_0_), channel_id=1, source_target_pairs={{0,4},{2,6},{1,5},{3,7},{8,12},{10,14},{9,13},{11,15},{16,20},{18,... | collective-permute-start | bytes 786440 | tf_op jit(solution)/shard_map/ppermute | solution.py:871
  125.7 5.0 arrange.4.wq
  130.8 3.3 fusion.37.q_ref
  135.0 9.9 %collective-permute-done.12.refs_3_ = bf16[256,512]{1,0:T(8,128)(2,1)} collective-permute-done((bf16[256,512]{1,0:T(8,128)(2,1)S(1)}, bf16[256,512]{1,0:T(8,128)(2,1)}, u32[]{:S(2)}, u32[]{:S(2)}) %collective-permute-start.12) | collective-permute-done | bytes 262176 | tf_op jit(solution)/shard_map/ppermute | solution.py:871
  144.9 8.9 %attend.1 = (bf16[256,768]{1,0:T(8,128)(2,1)S(1)}, bf16[256,768]{1,0:T(8,128)(2,1)}, f32[4,128,768]{2,1,0:T(8,128)}) custom-call(s32[6]{0:T(128)S(1)} %pad_add_fusion.where_ref, s32[2]{0:T(128)S(1)} %bitcast.109, f32[256,768]{1,0:T(8,128)} %fusion.37.q_ref, bf16[256,512]{1,0:T(8,128)(2,1)S(1)} %keys.1.refs_0_, ...), custom_call_target="tpu_custom_call" | custom-call | flops 12600000512 | bytes 14000000 | tf_op jit(solution)/shard_map/attend/pallas_call | solution.py:285
  155.6 4.0 arrange.5
  166.1 11.9 %collective-permute-done.18 = bf16[256,1536]{1,0:T(8,128)(2,1)} collective-permute-done((bf16[256,1536]{1,0:T(8,128)(2,1)S(1)}, bf16[256,1536]{1,0:T(8,128)(2,1)}, u32[]{:S(2)}, u32[]{:S(2)}) %collective-permute-start.18) | collective-permute-done | bytes 786464 | tf_op jit(solution)/shard_map/ppermute | solution.py:834
  183.9 13.6 %collective-permute-done.19.refs_1_.refs_2_ = bf16[256,1536]{1,0:T(8,128)(2,1)S(1)} collective-permute-done((bf16[256,1536]{1,0:T(8,128)(2,1)S(1)}, bf16[256,1536]{1,0:T(8,128)(2,1)S(1)}, u32[]{:S(2)}, u32[]{:S(2)}) %collective-permute-start.19) | collective-permute-done | bytes 786464 | tf_op jit(solution)/shard_map/ppermute | solution.py:830
  199.1 3.7 collective-permute-done.20.refs_1_
  202.8 10.0 %all-gather.2.cloned.1.call-done = bf16[4608,864]{1,0:T(8,128)(2,1)} async-done(((bf16[1152,864]{1,0:T(8,128)(2,1)}), bf16[4608,864]{1,0:T(8,128)(2,1)}) %all-gather.2.cloned.1.call-update) | async-done | bytes 7962640 | tf_op jit(solution)/shard_map/all_gather | solution.py:972
  213.9 28.4 %ffn.1 = (bf16[2,256,1536]{2,1,0:T(8,128)(2,1)}, bf16[2,256,1536]{2,1,0:T(8,128)(2,1)}, bf16[1024,864]{1,0:T(8,128)(2,1)}, bf16[1024,864]{1,0:T(8,128)(2,1)}, bf16[1024,864]{1,0:T(8,128)(2,1)}) custom-call(s32[6]{0:T(128)S(1)} %pad_add_fusion.where_ref, bf16[256,1536]{1,0:T(8,128)(2,1)S(1)} %multiply_convert_fusion.refs_0_, ...), custom_call_target="tpu_custom_call" | custom-call | flops 13500000256 | bytes 15000000 | tf_op jit(solution)/shard_map/ffn/pallas_call | solution.py:604
  242.5 3.5 collective-permute-done.26
  248.9 18.2 %collective-permute-done.27 = bf16[256,1536]{1,0:T(8,128)(2,1)S(1)} collective-permute-done((bf16[256,1536]{1,0:T(8,128)(2,1)S(1)}, bf16[256,1536]{1,0:T(8,128)(2,1)S(1)}, u32[]{:S(2)}, u32[]{:S(2)}) %collective-permute-start.27) | collective-permute-done | bytes 786464 | tf_op jit(solution)/shard_map/ppermute | solution.py:830
  267.4 9.6 %ffn_out.1 = (bf16[2,256,1536]{2,1,0:T(8,128)(2,1)}, bf16[2,256,1536]{2,1,0:T(8,128)(2,1)}) custom-call(s32[6]{0:T(128)S(1)} %pad_add_fusion.where_ref, bf16[1024,864]{1,0:T(8,128)(2,1)} %get-tuple-element.65.refs_0_.refs_8_, bf16[4,4,3,96,864]{4,3,2,1,0:T(8,128)(2,1)} %bitcast.128, bf16[256,1536]{1,0:T(8,128)(2,1)S(1)} %fusion.10.refs_2_), custom_call_target="tpu_custom_call" | custom-call | flops 8099999744 | bytes 9000000 | tf_op jit(solution)/shard_map/ffn_out/pallas_call | solution.py:654
  277.1 16.7 %hidden_grads.1.refs_7_ = bf16[4,4,3,96,864]{4,3,2,1,0:T(8,128)(2,1)} custom-call(s32[6]{0:T(128)S(1)} %pad_add_fusion.where_ref, bf16[256,1536]{1,0:T(8,128)(2,1)S(1)} %multiply_convert_fusion.refs_0_, bf16[2,256,1536]{2,1,0:T(8,128)(2,1)} %collective-permute-done.20.refs_1_, bf16[256,1536]{1,0:T(8,128)(2,1)S(1)} %copy-done.4, bf16[256,1536]{1,0:T(8,128)(2,1)} %bitcast.114, ...), custom_call_target="tpu_custom_call" | custom-call | flops 8099999744 | bytes 9000000 | tf_op jit(solution)/shard_map/hidden_grads/pallas_call | solution.py:731
  298.5 17.1 %collective-permute-done.29 = bf16[256,1536]{1,0:T(8,128)(2,1)S(1)} collective-permute-done((bf16[256,1536]{1,0:T(8,128)(2,1)S(1)}, bf16[256,1536]{1,0:T(8,128)(2,1)S(1)}, u32[]{:S(2)}, u32[]{:S(2)}) %collective-permute-start.29) | collective-permute-done | bytes 786464 | tf_op jit(solution)/shard_map/ppermute | solution.py:830
  319.3 17.0 %collective-permute-done.30 = bf16[256,1536]{1,0:T(8,128)(2,1)S(1)} collective-permute-done((bf16[256,1536]{1,0:T(8,128)(2,1)S(1)}, bf16[256,1536]{1,0:T(8,128)(2,1)S(1)}, u32[]{:S(2)}, u32[]{:S(2)}) %collective-permute-start.30) | collective-permute-done | bytes 786464 | tf_op jit(solution)/shard_map/ppermute | solution.py:834
  340.0 11.9 %attend_back.1 = (bf16[256,768]{1,0:T(8,128)(2,1)}, bf16[256,512]{1,0:T(8,128)(2,1)S(1)}, bf16[256,512]{1,0:T(8,128)(2,1)S(1)}, bf16[256,512]{1,0:T(8,128)(2,1)S...) custom-call(s32[6]{0:T(128)S(1)} %pad_add_fusion.where_ref, s32[2]{0:T(128)S(1)} %bitcast.110, ...), custom_call_target="tpu_custom_call" | custom-call | flops 15299999744 | bytes 17000000 | tf_op jit(solution)/shard_map/attend_back/pallas_call | solution.py:310
  352.9 6.9 %head_grads.2 = (bf16[2,4,96,1536]{3,2,1,0:T(8,128)(2,1)}, bf16[2,4,96,1536]{3,2,1,0:T(8,128)(2,1)}) custom-call(s32[6]{0:T(128)S(1)} %pad_add_fusion.where_ref, bf16[256,1536]{1,0:T(8,128)(2,1)S(1)} %fusion.3.refs_0_, bf16[256,1536]{1,0:T(8,128)(2,1)} %copy-done.23, bf16[256,768]{1,0:T(8,128)(2,1)S(1)} %copy-done.9, bf16[256,768]{1,0:T(8,128)(2,1)S(1)} %copy-done.8), custom_call_target="tpu_custom_call" | custom-call | flops 2700000000 | bytes 3000000 | tf_op jit(solution)/shard_map/head_grads/pallas_call | solution.py:817
  359.8 4.7 collective-permute-done.32
  364.5 3.5 fusion.12.refs_3_
  373.1 41.5 %collective-permute-done.35 = bf16[256,512]{1,0:T(8,128)(2,1)S(1)} collective-permute-done((bf16[256,512]{1,0:T(8,128)(2,1)}, bf16[256,512]{1,0:T(8,128)(2,1)S(1)}, u32[]{:S(2)}, u32[]{:S(2)}) %collective-permute-start.35) | collective-permute-done | bytes 262176 | tf_op jit(solution)/shard_map/ppermute | solution.py:881
  414.6 5.5 %collective-permute-done.33 = bf16[256,512]{1,0:T(8,128)(2,1)} collective-permute-done((bf16[256,512]{1,0:T(8,128)(2,1)S(1)}, bf16[256,512]{1,0:T(8,128)(2,1)}, u32[]{:S(2)}, u32[]{:S(2)}) %collective-permute-start.33) | collective-permute-done | bytes 262176 | tf_op jit(solution)/shard_map/ppermute | solution.py:881
  421.9 3.6 normed_back.1
  427.3 4.0 head_grads.3
  431.3 13.8 %collective-permute-done.36 = bf16[256,1536]{1,0:T(8,128)(2,1)S(1)} collective-permute-done((bf16[256,1536]{1,0:T(8,128)(2,1)S(1)}, bf16[256,1536]{1,0:T(8,128)(2,1)S(1)}, u32[]{:S(2)}, u32[]{:S(2)}) %collective-permute-start.36) | collective-permute-done | bytes 786464 | tf_op jit(solution)/shard_map/ppermute | solution.py:834
  446.5 8.6 %collective-permute-done.43 = bf16[4,96,1536]{2,1,0:T(8,128)(2,1)S(1)} collective-permute-done((bf16[4,96,1536]{2,1,0:T(8,128)(2,1)}, bf16[4,96,1536]{2,1,0:T(8,128)(2,1)S(1)}, u32[]{:S(2)}, u32[]{:S(2)}) %collective-permute-start.43) | collective-permute-done | bytes 1179680 | tf_op jit(solution)/shard_map/ppermute | solution.py:830
  455.6 11.8 %collective-permute-start.44 = (bf16[96,1536]{1,0:T(8,128)(2,1)S(1)}, bf16[96,1536]{1,0:T(8,128)(2,1)S(1)}, u32[]{:S(2)}, u32[]{:S(2)}) collective-permute-start(bf16[96,1536]{1,0:T(8,128)(2,1)S(1)} %slice_bitcast_fusion.4), channel_id=1, source_target_pairs={{0,2},{2,4},{4,6},{6,0},{1,3},{3,5},{5,7},{7,1},{8,10},{10,12},{12... | collective-permute-start | bytes 884744 | tf_op jit(solution)/shard_map/ppermute | solution.py:839
  467.7 7.8 %collective-permute-start.39 = (bf16[112,512]{1,0:T(8,128)(2,1)S(1)}, bf16[112,512]{1,0:T(8,128)(2,1)S(1)}, u32[]{:S(2)}, u32[]{:S(2)}) collective-permute-start(bf16[112,512]{1,0:T(8,128)(2,1)S(1)} %slice_bitcast_fusion.11), channel_id=1, source_target_pairs={{0,2},{2,4},{4,6},{6,0},{1,3},{3,5},{5,7},{7,1},{8,10},{10,12},{12... | collective-permute-start | bytes 344072 | tf_op jit(solution)/shard_map/ppermute | solution.py:839
  475.5 2.9 collective-permute-done.44
  478.5 3.3 collective-permute-start.45
  487.0 4.3 collective-permute-done.40
  494.1 5.2 collective-permute-done.41
  508.6 11.8 %collective-permute-done.48.refs_2_ = bf16[3,96,864]{2,1,0:T(8,128)(2,1)S(1)} collective-permute-done((bf16[3,96,864]{2,1,0:T(8,128)(2,1)S(1)}, bf16[3,96,864]{2,1,0:T(8,128)(2,1)S(1)}, u32[]{:S(2)}, u32[]{:S(2)}) %collective-permute-start.48) | collective-permute-done | bytes 497696 | tf_op jit(solution)/shard_map/ppermute | solution.py:830
  520.4 10.2 %collective-permute-done.49.refs_3_ = bf16[3,96,864]{2,1,0:T(8,128)(2,1)S(1)} collective-permute-done((bf16[3,96,864]{2,1,0:T(8,128)(2,1)S(1)}, bf16[3,96,864]{2,1,0:T(8,128)(2,1)S(1)}, u32[]{:S(2)}, u32[]{:S(2)}) %collective-permute-start.49) | collective-permute-done | bytes 497696 | tf_op jit(solution)/shard_map/ppermute | solution.py:830
  531.3 3.7 join_columns.1
  (222 shorter events, 99.1 us)
Async XLA Ops:
  7.2 205.6 %all-gather.2.cloned.1.call-start = ((), (), s32[]{:S(2)}) async-start(), calls=%async_computation.1 | async-start | bytes 10321920 | tf_op jit(solution)/shard_map/all_gather | solution.py:972
  10.4 23.9 %collective-permute-start.23 = (bf16[3,96,864]{2,1,0:T(8,128)(2,1)S(1)}, bf16[3,96,864]{2,1,0:T(8,128)(2,1)S(1)}, u32[]{:S(2)}, u32[]{:S(2)}) collective-permute-start(bf16[3,96,864]{2,1,0:T(8,128)(2,1)S(1)} %get-tuple-element.62), channel_id=1, source_target_pairs={{0,8},{8,0},{16,24},{24,16},{1,9},{9,1},{17,25},{25,17},{2,10},{10... | collective-permute-start | bytes 1493000 | tf_op jit(solution)/shard_map/ppermute | solution.py:830
  10.9 23.5 %collective-permute-start.24 = (bf16[3,96,864]{2,1,0:T(8,128)(2,1)S(1)}, bf16[3,96,864]{2,1,0:T(8,128)(2,1)S(1)}, u32[]{:S(2)}, u32[]{:S(2)}) collective-permute-start(bf16[3,96,864]{2,1,0:T(8,128)(2,1)S(1)} %get-tuple-element.63), channel_id=1, source_target_pairs={{0,16},{8,24},{16,0},{24,8},{1,17},{9,25},{17,1},{25,9},{2,18},{10... | collective-permute-start | bytes 1493000 | tf_op jit(solution)/shard_map/ppermute | solution.py:830
  13.4 23.3 %collective-permute-start.25 = (bf16[3,96,864]{2,1,0:T(8,128)(2,1)}, bf16[3,96,864]{2,1,0:T(8,128)(2,1)S(1)}, u32[]{:S(2)}, u32[]{:S(2)}) collective-permute-start(bf16[3,96,864]{2,1,0:T(8,128)(2,1)} %get-tuple-element.64), channel_id=1, source_target_pairs={{0,24},{8,16},{16,8},{24,0},{1,25},{9,17},{17,9},{25,1},{2,26},{10... | collective-permute-start | bytes 1493000 | tf_op jit(solution)/shard_map/ppermute | solution.py:830
  13.6 7.5 %collective-permute-start = (bf16[112,512]{1,0:T(8,128)(2,1)S(1)}, bf16[112,512]{1,0:T(8,128)(2,1)S(1)}, u32[]{:S(2)}, u32[]{:S(2)}) collective-permute-start(bf16[112,512]{1,0:T(8,128)(2,1)S(1)} %fusion.23.refs_0_), channel_id=1, source_target_pairs={{0,2},{2,4},{4,6},{6,0},{1,3},{3,5},{5,7},{7,1},{8,10},{10,12},{12... | collective-permute-start | bytes 344072 | tf_op jit(solution)/shard_map/ppermute | solution.py:839
  21.1 6.6 %collective-permute-start.1 = (bf16[112,512]{1,0:T(8,128)(2,1)S(1)}, bf16[112,512]{1,0:T(8,128)(2,1)S(1)}, u32[]{:S(2)}, u32[]{:S(2)}) collective-permute-start(bf16[112,512]{1,0:T(8,128)(2,1)S(1)} %collective-permute-done.refs_1_), channel_id=1, source_target_pairs={{0,2},{2,4},{4,6},{6,0},{1,3},{3,5},{5,7},{7,1},{8,10},{10,12},{12... | collective-permute-start | bytes 344072 | tf_op jit(solution)/shard_map/ppermute | solution.py:839
  27.8 6.6 %collective-permute-start.2 = (bf16[112,512]{1,0:T(8,128)(2,1)S(1)}, bf16[112,512]{1,0:T(8,128)(2,1)S(1)}, u32[]{:S(2)}, u32[]{:S(2)}) collective-permute-start(bf16[112,512]{1,0:T(8,128)(2,1)S(1)} %collective-permute-done.1.refs_2_), channel_id=1, source_target_pairs={{0,2},{2,4},{4,6},{6,0},{1,3},{3,5},{5,7},{7,1},{8,10},{10,12},{12... | collective-permute-start | bytes 344072 | tf_op jit(solution)/shard_map/ppermute | solution.py:839
  40.9 463.1 %reduce-scatter.2.cloned.1.call-start = ((), (), s32[]{:S(2)}) async-start(), calls=%async_computation.2 | async-start | bytes 10321920 | tf_op jit(solution)/shard_map/reduce_scatter | solution.py:916
  41.8 7.9 %collective-permute-start.5 = (bf16[96,768]{1,0:T(8,128)(2,1)S(1)}, bf16[96,768]{1,0:T(8,128)(2,1)S(1)}, u32[]{:S(2)}, u32[]{:S(2)}) collective-permute-start(bf16[96,768]{1,0:T(8,128)(2,1)S(1)} %copy-done.5), channel_id=1, source_target_pairs={{0,2},{2,4},{4,6},{6,0},{1,3},{3,5},{5,7},{7,1},{8,10},{10,12},{12... | collective-permute-start | bytes 442376 | tf_op jit(solution)/shard_map/ppermute | solution.py:839
  44.0 15.3 %collective-permute-start.3 = (bf16[4,112,512]{2,1,0:T(8,128)(2,1)S(1)}, bf16[4,112,512]{2,1,0:T(8,128)(2,1)S(1)}, u32[]{:S(2)}, u32[]{:S(2)}) collective-permute-start(bf16[4,112,512]{2,1,0:T(8,128)(2,1)S(1)} %collect.11.refs_0_), channel_id=1, source_target_pairs={{0,16},{8,24},{16,0},{24,8},{1,17},{9,25},{17,1},{25,9},{2,18},{10... | collective-permute-start | bytes 1376264 | tf_op jit(solution)/shard_map/ppermute | solution.py:830
  45.5 27.0 %collective-permute-start.13 = (bf16[96,768]{1,0:T(8,128)(2,1)S(1)}, bf16[96,768]{1,0:T(8,128)(2,1)S(1)}, u32[]{:S(2)}, u32[]{:S(2)}) collective-permute-start(bf16[96,768]{1,0:T(8,128)(2,1)S(1)} %bitcast.115), channel_id=1, source_target_pairs={{0,2},{2,4},{4,6},{6,0},{1,3},{3,5},{5,7},{7,1},{8,10},{10,12},{12... | collective-permute-start | bytes 442376 | tf_op jit(solution)/shard_map/ppermute | solution.py:839
  49.7 8.2 %collective-permute-start.6 = (bf16[96,768]{1,0:T(8,128)(2,1)S(1)}, bf16[96,768]{1,0:T(8,128)(2,1)S(1)}, u32[]{:S(2)}, u32[]{:S(2)}) collective-permute-start(bf16[96,768]{1,0:T(8,128)(2,1)S(1)} %collective-permute-done.5.refs_1_), channel_id=1, source_target_pairs={{0,2},{2,4},{4,6},{6,0},{1,3},{3,5},{5,7},{7,1},{8,10},{10,12},{12... | collective-permute-start | bytes 442376 | tf_op jit(solution)/shard_map/ppermute | solution.py:839
  57.9 10.5 %collective-permute-start.7 = (bf16[96,768]{1,0:T(8,128)(2,1)S(1)}, bf16[96,768]{1,0:T(8,128)(2,1)S(1)}, u32[]{:S(2)}, u32[]{:S(2)}) collective-permute-start(bf16[96,768]{1,0:T(8,128)(2,1)S(1)} %collective-permute-done.6.refs_2_), channel_id=1, source_target_pairs={{0,2},{2,4},{4,6},{6,0},{1,3},{3,5},{5,7},{7,1},{8,10},{10,12},{12... | collective-permute-start | bytes 442376 | tf_op jit(solution)/shard_map/ppermute | solution.py:839
  59.9 40.6 %collective-permute-start.4 = (bf16[2,4,112,512]{3,2,1,0:T(8,128)(2,1)S(1)}, bf16[2,4,112,512]{3,2,1,0:T(8,128)(2,1)S(1)}, u32[]{:S(2)}, u32[]{:S(2)}) collective-permute-start(bf16[2,4,112,512]{3,2,1,0:T(8,128)(2,1)S(1)} %collect.12), channel_id=1, source_target_pairs={{0,8},{8,0},{16,24},{24,16},{1,9},{9,1},{17,25},{25,17},{2,10},{10... | collective-permute-start | bytes 2752520 | tf_op jit(solution)/shard_map/ppermute | solution.py:830
  69.2 17.9 %collective-permute-start.8 = (bf16[4,96,768]{2,1,0:T(8,128)(2,1)S(1)}, bf16[4,96,768]{2,1,0:T(8,128)(2,1)S(1)}, u32[]{:S(2)}, u32[]{:S(2)}) collective-permute-start(bf16[4,96,768]{2,1,0:T(8,128)(2,1)S(1)} %collect.13.refs_0_), channel_id=1, source_target_pairs={{0,16},{8,24},{16,0},{24,8},{1,17},{9,25},{17,1},{25,9},{2,18},{10... | collective-permute-start | bytes 1769480 | tf_op jit(solution)/shard_map/ppermute | solution.py:830
  72.6 14.2 %collective-permute-start.14 = (bf16[96,768]{1,0:T(8,128)(2,1)S(1)}, bf16[96,768]{1,0:T(8,128)(2,1)S(1)}, u32[]{:S(2)}, u32[]{:S(2)}) collective-permute-start(bf16[96,768]{1,0:T(8,128)(2,1)S(1)} %collective-permute-done.13.refs_1_), channel_id=1, source_target_pairs={{0,2},{2,4},{4,6},{6,0},{1,3},{3,5},{5,7},{7,1},{8,10},{10,12},{12... | collective-permute-start | bytes 442376 | tf_op jit(solution)/shard_map/ppermute | solution.py:839
  86.8 11.3 %collective-permute-start.15 = (bf16[96,768]{1,0:T(8,128)(2,1)S(1)}, bf16[96,768]{1,0:T(8,128)(2,1)S(1)}, u32[]{:S(2)}, u32[]{:S(2)}) collective-permute-start(bf16[96,768]{1,0:T(8,128)(2,1)S(1)} %collective-permute-done.14.refs_2_), channel_id=1, source_target_pairs={{0,2},{2,4},{4,6},{6,0},{1,3},{3,5},{5,7},{7,1},{8,10},{10,12},{12... | collective-permute-start | bytes 442376 | tf_op jit(solution)/shard_map/ppermute | solution.py:839
  88.4 37.3 %collective-permute-start.9 = (bf16[2,4,96,768]{3,2,1,0:T(8,128)(2,1)}, bf16[2,4,96,768]{3,2,1,0:T(8,128)(2,1)}, u32[]{:S(2)}, u32[]{:S(2)}) collective-permute-start(bf16[2,4,96,768]{3,2,1,0:T(8,128)(2,1)} %collect.14), channel_id=1, source_target_pairs={{0,8},{8,0},{16,24},{24,16},{1,9},{9,1},{17,25},{25,17},{2,10},{10... | collective-permute-start | bytes 3538952 | tf_op jit(solution)/shard_map/ppermute | solution.py:830
  99.6 23.7 %collective-permute-start.16 = (bf16[4,96,768]{2,1,0:T(8,128)(2,1)}, bf16[4,96,768]{2,1,0:T(8,128)(2,1)}, u32[]{:S(2)}, u32[]{:S(2)}) collective-permute-start(bf16[4,96,768]{2,1,0:T(8,128)(2,1)} %collect.15.refs_0_), channel_id=1, source_target_pairs={{0,16},{8,24},{16,0},{24,8},{1,17},{9,25},{17,1},{25,9},{2,18},{10... | collective-permute-start | bytes 1769480 | tf_op jit(solution)/shard_map/ppermute | solution.py:830
  110.2 23.9 %collective-permute-start.10 = (bf16[256,512]{1,0:T(8,128)(2,1)S(1)}, bf16[256,512]{1,0:T(8,128)(2,1)}, u32[]{:S(2)}, u32[]{:S(2)}) collective-permute-start(bf16[256,512]{1,0:T(8,128)(2,1)S(1)} %keys.1.refs_0_), channel_id=1, source_target_pairs={{0,2},{2,4},{4,6},{1,3},{3,5},{5,7},{8,10},{10,12},{12,14},{9,11},... | collective-permute-start | bytes 786440 | tf_op jit(solution)/shard_map/ppermute | solution.py:871
  112.2 22.8 %collective-permute-start.11 = (bf16[256,512]{1,0:T(8,128)(2,1)S(1)}, bf16[256,512]{1,0:T(8,128)(2,1)}, u32[]{:S(2)}, u32[]{:S(2)}) collective-permute-start(bf16[256,512]{1,0:T(8,128)(2,1)S(1)} %keys.1.refs_0_), channel_id=1, source_target_pairs={{0,4},{2,6},{1,5},{3,7},{8,12},{10,14},{9,13},{11,15},{16,20},{18,... | collective-permute-start | bytes 786440 | tf_op jit(solution)/shard_map/ppermute | solution.py:871
  121.0 23.9 %collective-permute-start.12 = (bf16[256,512]{1,0:T(8,128)(2,1)S(1)}, bf16[256,512]{1,0:T(8,128)(2,1)}, u32[]{:S(2)}, u32[]{:S(2)}) collective-permute-start(bf16[256,512]{1,0:T(8,128)(2,1)S(1)} %keys.1.refs_0_), channel_id=1, source_target_pairs={{0,6},{1,7},{8,14},{9,15},{16,22},{17,23},{24,30},{25,31}} | collective-permute-start | bytes 786440 | tf_op jit(solution)/shard_map/ppermute | solution.py:871
  125.6 29.0 %collective-permute-start.17 = (bf16[2,4,96,768]{3,2,1,0:T(8,128)(2,1)}, bf16[2,4,96,768]{3,2,1,0:T(8,128)(2,1)S(1)}, u32[]{:S(2)}, u32[]{:S(2)}) collective-permute-start(bf16[2,4,96,768]{3,2,1,0:T(8,128)(2,1)} %collect.16), channel_id=1, source_target_pairs={{0,8},{8,0},{16,24},{24,16},{1,9},{9,1},{17,25},{25,17},{2,10},{10... | collective-permute-start | bytes 3538952 | tf_op jit(solution)/shard_map/ppermute | solution.py:830
  162.1 15.9 %collective-permute-start.18 = (bf16[256,1536]{1,0:T(8,128)(2,1)S(1)}, bf16[256,1536]{1,0:T(8,128)(2,1)}, u32[]{:S(2)}, u32[]{:S(2)}) collective-permute-start(bf16[256,1536]{1,0:T(8,128)(2,1)S(1)} %convolution_convert_fusion), channel_id=1, source_target_pairs={{0,1},{1,0},{2,3},{3,2},{4,5},{5,4},{6,7},{7,6},{8,9},{9,8},{10,11... | collective-permute-start | bytes 2359304 | tf_op jit(solution)/shard_map/ppermute | solution.py:834
  165.1 17.4 %collective-permute-start.21 = (bf16[256,1536]{1,0:T(8,128)(2,1)S(1)}, bf16[256,1536]{1,0:T(8,128)(2,1)S(1)}, u32[]{:S(2)}, u32[]{:S(2)}) collective-permute-start(bf16[256,1536]{1,0:T(8,128)(2,1)S(1)} %bitcast.111), channel_id=1, source_target_pairs={{0,16},{8,24},{16,0},{24,8},{1,17},{9,25},{17,1},{25,9},{2,18},{10... | collective-permute-start | bytes 2359304 | tf_op jit(solution)/shard_map/ppermute | solution.py:830
  180.9 16.6 %collective-permute-start.19 = (bf16[256,1536]{1,0:T(8,128)(2,1)S(1)}, bf16[256,1536]{1,0:T(8,128)(2,1)S(1)}, u32[]{:S(2)}, u32[]{:S(2)}) collective-permute-start(bf16[256,1536]{1,0:T(8,128)(2,1)S(1)} %multiply_convert_fusion.refs_0_), channel_id=1, source_target_pairs={{0,16},{8,24},{16,0},{24,8},{1,17},{9,25},{17,1},{25,9},{2,18},{10... | collective-permute-start | bytes 2359304 | tf_op jit(solution)/shard_map/ppermute | solution.py:830
  183.9 15.2 %collective-permute-start.22 = (bf16[2,256,1536]{2,1,0:T(8,128)(2,1)}, bf16[2,256,1536]{2,1,0:T(8,128)(2,1)}, u32[]{:S(2)}, u32[]{:S(2)}) collective-permute-start(bf16[2,256,1536]{2,1,0:T(8,128)(2,1)} %collect.19), channel_id=1, source_target_pairs={{0,8},{8,0},{16,24},{24,16},{1,9},{9,1},{17,25},{25,17},{2,10},{10... | collective-permute-start | bytes 4718600 | tf_op jit(solution)/shard_map/ppermute | solution.py:830
  247.4 19.6 %collective-permute-start.27 = (bf16[256,1536]{1,0:T(8,128)(2,1)S(1)}, bf16[256,1536]{1,0:T(8,128)(2,1)S(1)}, u32[]{:S(2)}, u32[]{:S(2)}) collective-permute-start(bf16[256,1536]{1,0:T(8,128)(2,1)S(1)} %fusion.14.refs_9_), channel_id=1, source_target_pairs={{0,16},{8,24},{16,0},{24,8},{1,17},{9,25},{17,1},{25,9},{2,18},{10... | collective-permute-start | bytes 2359304 | tf_op jit(solution)/shard_map/ppermute | solution.py:830
  277.0 16.8 %collective-permute-start.28 = (bf16[2,256,1536]{2,1,0:T(8,128)(2,1)}, bf16[2,256,1536]{2,1,0:T(8,128)(2,1)}, u32[]{:S(2)}, u32[]{:S(2)}) collective-permute-start(bf16[2,256,1536]{2,1,0:T(8,128)(2,1)} %get-tuple-element.69), channel_id=1, source_target_pairs={{0,8},{8,0},{16,24},{24,16},{1,9},{9,1},{17,25},{25,17},{2,10},{10... | collective-permute-start | bytes 4718600 | tf_op jit(solution)/shard_map/ppermute | solution.py:830
  295.5 20.0 %collective-permute-start.29 = (bf16[256,1536]{1,0:T(8,128)(2,1)S(1)}, bf16[256,1536]{1,0:T(8,128)(2,1)S(1)}, u32[]{:S(2)}, u32[]{:S(2)}) collective-permute-start(bf16[256,1536]{1,0:T(8,128)(2,1)S(1)} %fusion.15), channel_id=1, source_target_pairs={{0,16},{8,24},{16,0},{24,8},{1,17},{9,25},{17,1},{25,9},{2,18},{10... | collective-permute-start | bytes 2359304 | tf_op jit(solution)/shard_map/ppermute | solution.py:830
  296.9 21.6 %collective-permute-start.31 = (bf16[256,1536]{1,0:T(8,128)(2,1)S(1)}, bf16[256,1536]{1,0:T(8,128)(2,1)S(1)}, u32[]{:S(2)}, u32[]{:S(2)}) collective-permute-start(bf16[256,1536]{1,0:T(8,128)(2,1)S(1)} %fusion.10.refs_2_), channel_id=1, source_target_pairs={{0,1},{1,0},{2,3},{3,2},{4,5},{5,4},{6,7},{7,6},{8,9},{9,8},{10,11... | collective-permute-start | bytes 2359304 | tf_op jit(solution)/shard_map/ppermute | solution.py:834
  317.0 19.3 %collective-permute-start.30 = (bf16[256,1536]{1,0:T(8,128)(2,1)S(1)}, bf16[256,1536]{1,0:T(8,128)(2,1)S(1)}, u32[]{:S(2)}, u32[]{:S(2)}) collective-permute-start(bf16[256,1536]{1,0:T(8,128)(2,1)S(1)} %fusion.9), channel_id=1, source_target_pairs={{0,1},{1,0},{2,3},{3,2},{4,5},{5,4},{6,7},{7,6},{8,9},{9,8},{10,11... | collective-permute-start | bytes 2359304 | tf_op jit(solution)/shard_map/ppermute | solution.py:834
  359.8 4.7 collective-permute-start.32
  368.9 45.8 %collective-permute-start.35 = (bf16[256,512]{1,0:T(8,128)(2,1)}, bf16[256,512]{1,0:T(8,128)(2,1)S(1)}, u32[]{:S(2)}, u32[]{:S(2)}) collective-permute-start(bf16[256,512]{1,0:T(8,128)(2,1)} %get-tuple-element.103), channel_id=1, source_target_pairs={{6,0},{7,1},{14,8},{15,9},{22,16},{23,17},{30,24},{31,25}} | collective-permute-start | bytes 786440 | tf_op jit(solution)/shard_map/ppermute | solution.py:881
  370.1 44.5 %collective-permute-start.34 = (bf16[256,512]{1,0:T(8,128)(2,1)S(1)}, bf16[256,512]{1,0:T(8,128)(2,1)S(1)}, u32[]{:S(2)}, u32[]{:S(2)}) collective-permute-start(bf16[256,512]{1,0:T(8,128)(2,1)S(1)} %get-tuple-element.104), channel_id=1, source_target_pairs={{4,0},{6,2},{5,1},{7,3},{12,8},{14,10},{13,9},{15,11},{20,16},{22,... | collective-permute-start | bytes 786440 | tf_op jit(solution)/shard_map/ppermute | solution.py:881
  371.4 48.7 %collective-permute-start.33 = (bf16[256,512]{1,0:T(8,128)(2,1)S(1)}, bf16[256,512]{1,0:T(8,128)(2,1)}, u32[]{:S(2)}, u32[]{:S(2)}) collective-permute-start(bf16[256,512]{1,0:T(8,128)(2,1)S(1)} %get-tuple-element.102), channel_id=1, source_target_pairs={{2,0},{4,2},{6,4},{3,1},{5,3},{7,5},{10,8},{12,10},{14,12},{11,9},... | collective-permute-start | bytes 786440 | tf_op jit(solution)/shard_map/ppermute | solution.py:881
  425.5 19.6 %collective-permute-start.36 = (bf16[256,1536]{1,0:T(8,128)(2,1)S(1)}, bf16[256,1536]{1,0:T(8,128)(2,1)S(1)}, u32[]{:S(2)}, u32[]{:S(2)}) collective-permute-start(bf16[256,1536]{1,0:T(8,128)(2,1)S(1)} %get-tuple-element.82), channel_id=1, source_target_pairs={{0,1},{1,0},{2,3},{3,2},{4,5},{5,4},{6,7},{7,6},{8,9},{9,8},{10,11... | collective-permute-start | bytes 2359304 | tf_op jit(solution)/shard_map/ppermute | solution.py:834
  426.0 29.2 %collective-permute-start.43 = (bf16[4,96,1536]{2,1,0:T(8,128)(2,1)}, bf16[4,96,1536]{2,1,0:T(8,128)(2,1)S(1)}, u32[]{:S(2)}, u32[]{:S(2)}) collective-permute-start(bf16[4,96,1536]{2,1,0:T(8,128)(2,1)} %fusion.12.refs_3_), channel_id=1, source_target_pairs={{0,16},{8,24},{16,0},{24,8},{1,17},{9,25},{17,1},{25,9},{2,18},{10... | collective-permute-start | bytes 3538952 | tf_op jit(solution)/shard_map/ppermute | solution.py:830
  431.3 14.2 %collective-permute-start.37 = (bf16[2,4,112,512]{3,2,1,0:T(8,128)(2,1)}, bf16[2,4,112,512]{3,2,1,0:T(8,128)(2,1)S(1)}, u32[]{:S(2)}, u32[]{:S(2)}) collective-permute-start(bf16[2,4,112,512]{3,2,1,0:T(8,128)(2,1)} %get-tuple-element.87), channel_id=1, source_target_pairs={{0,8},{8,0},{16,24},{24,16},{1,9},{9,1},{17,25},{25,17},{2,10},{10... | collective-permute-start | bytes 2752520 | tf_op jit(solution)/shard_map/ppermute | solution.py:830
  445.6 21.8 %collective-permute-start.38 = (bf16[4,112,512]{2,1,0:T(8,128)(2,1)S(1)}, bf16[4,112,512]{2,1,0:T(8,128)(2,1)S(1)}, u32[]{:S(2)}, u32[]{:S(2)}) collective-permute-start(bf16[4,112,512]{2,1,0:T(8,128)(2,1)S(1)} %fusion.19), channel_id=1, source_target_pairs={{0,16},{8,24},{16,0},{24,8},{1,17},{9,25},{17,1},{25,9},{2,18},{10... | collective-permute-start | bytes 1376264 | tf_op jit(solution)/shard_map/ppermute | solution.py:830
  455.6 22.8 %collective-permute-start.44 = (bf16[96,1536]{1,0:T(8,128)(2,1)S(1)}, bf16[96,1536]{1,0:T(8,128)(2,1)S(1)}, u32[]{:S(2)}, u32[]{:S(2)}) collective-permute-start(bf16[96,1536]{1,0:T(8,128)(2,1)S(1)} %slice_bitcast_fusion.4), channel_id=1, source_target_pairs={{0,2},{2,4},{4,6},{6,0},{1,3},{3,5},{5,7},{7,1},{8,10},{10,12},{12... | collective-permute-start | bytes 884744 | tf_op jit(solution)/shard_map/ppermute | solution.py:839
  467.7 16.4 %collective-permute-start.39 = (bf16[112,512]{1,0:T(8,128)(2,1)S(1)}, bf16[112,512]{1,0:T(8,128)(2,1)S(1)}, u32[]{:S(2)}, u32[]{:S(2)}) collective-permute-start(bf16[112,512]{1,0:T(8,128)(2,1)S(1)} %slice_bitcast_fusion.11), channel_id=1, source_target_pairs={{0,2},{2,4},{4,6},{6,0},{1,3},{3,5},{5,7},{7,1},{8,10},{10,12},{12... | collective-permute-start | bytes 344072 | tf_op jit(solution)/shard_map/ppermute | solution.py:839
  478.5 13.0 %collective-permute-start.45 = (bf16[96,1536]{1,0:T(8,128)(2,1)S(1)}, bf16[96,1536]{1,0:T(8,128)(2,1)S(1)}, u32[]{:S(2)}, u32[]{:S(2)}) collective-permute-start(bf16[96,1536]{1,0:T(8,128)(2,1)S(1)} %fusion.18), channel_id=1, source_target_pairs={{0,2},{2,4},{4,6},{6,0},{1,3},{3,5},{5,7},{7,1},{8,10},{10,12},{12... | collective-permute-start | bytes 884744 | tf_op jit(solution)/shard_map/ppermute | solution.py:839
  484.1 7.2 %collective-permute-start.40 = (bf16[112,512]{1,0:T(8,128)(2,1)S(1)}, bf16[112,512]{1,0:T(8,128)(2,1)S(1)}, u32[]{:S(2)}, u32[]{:S(2)}) collective-permute-start(bf16[112,512]{1,0:T(8,128)(2,1)S(1)} %fusion.21), channel_id=1, source_target_pairs={{0,2},{2,4},{4,6},{6,0},{1,3},{3,5},{5,7},{7,1},{8,10},{10,12},{12... | collective-permute-start | bytes 344072 | tf_op jit(solution)/shard_map/ppermute | solution.py:839
  491.4 7.9 %collective-permute-start.41 = (bf16[112,512]{1,0:T(8,128)(2,1)S(1)}, bf16[112,512]{1,0:T(8,128)(2,1)S(1)}, u32[]{:S(2)}, u32[]{:S(2)}) collective-permute-start(bf16[112,512]{1,0:T(8,128)(2,1)S(1)} %fusion.20), channel_id=1, source_target_pairs={{0,2},{2,4},{4,6},{6,0},{1,3},{3,5},{5,7},{7,1},{8,10},{10,12},{12... | collective-permute-start | bytes 344072 | tf_op jit(solution)/shard_map/ppermute | solution.py:839
  491.5 16.1 %collective-permute-start.46 = (bf16[96,1536]{1,0:T(8,128)(2,1)S(1)}, bf16[96,1536]{1,0:T(8,128)(2,1)S(1)}, u32[]{:S(2)}, u32[]{:S(2)}) collective-permute-start(bf16[96,1536]{1,0:T(8,128)(2,1)S(1)} %fusion.17), channel_id=1, source_target_pairs={{0,2},{2,4},{4,6},{6,0},{1,3},{3,5},{5,7},{7,1},{8,10},{10,12},{12... | collective-permute-start | bytes 884744 | tf_op jit(solution)/shard_map/ppermute | solution.py:839
  505.8 14.6 %collective-permute-start.48 = (bf16[3,96,864]{2,1,0:T(8,128)(2,1)S(1)}, bf16[3,96,864]{2,1,0:T(8,128)(2,1)S(1)}, u32[]{:S(2)}, u32[]{:S(2)}) collective-permute-start(bf16[3,96,864]{2,1,0:T(8,128)(2,1)S(1)} %bitcast.122), channel_id=1, source_target_pairs={{0,16},{8,24},{16,0},{24,8},{1,17},{9,25},{17,1},{25,9},{2,18},{10... | collective-permute-start | bytes 1493000 | tf_op jit(solution)/shard_map/ppermute | solution.py:830
  507.1 23.4 %collective-permute-start.49 = (bf16[3,96,864]{2,1,0:T(8,128)(2,1)S(1)}, bf16[3,96,864]{2,1,0:T(8,128)(2,1)S(1)}, u32[]{:S(2)}, u32[]{:S(2)}) collective-permute-start(bf16[3,96,864]{2,1,0:T(8,128)(2,1)S(1)} %bitcast.121), channel_id=1, source_target_pairs={{0,24},{8,16},{16,8},{24,0},{1,25},{9,17},{17,9},{25,1},{2,26},{10... | collective-permute-start | bytes 1493000 | tf_op jit(solution)/shard_map/ppermute | solution.py:830
  (40 other events, 352.3 us)
Sparse Core Ops, SparseCore 0:
  41.0 171.7 all-gather.1
  293.9 176.9 reduce-scatter.1
where the time goes:
time: 548 us; the launch traced here: 542 us
  waiting for transfers between devices  281 us (51%)
  Pallas kernels  126 us (23%)
  starting transfers between devices  74.3 us (14%)
  other arithmetic  21.2 us (4%)
  between operations  15.2 us (3%)
  local copies, waits for them, and re-layouts  14.9 us (3%)
  matrix products  9.3 us (2%)
    ppermute x24, waiting for transfers between devices, flip(): return lax.ppermute(part, 'fsdp', [(i, i ^ bit) for i in range(size)])  95 us
    ppermute x15, waiting for transfers between devices, turn(): return lax.ppermute(part, 'ctx', [(i, (i + 1) % size) for i in range(size)])  74.6 us
    ppermute x3, waiting for transfers between devices, back_sum(): lax.ppermute(terms[step], 'ctx', [(i, i - step) for i in range(step, size)])  47 us
    ppermute x5, waiting for transfers between devices, swap(): return lax.ppermute(part, 'tp', [(0, 1), (1, 0)])  44 us
    ppermute x15, starting transfers between devices, turn(): return lax.ppermute(part, 'ctx', [(i, (i + 1) % size) for i in range(size)])  33.4 us
    pallas_call x1, Pallas kernels, ffn(): pl.pallas_call(kernel, out_shape=(shaped((2, rows, model)),) * 2 + (shape...  28.4 us
    ppermute x24, starting transfers between devices, flip(): return lax.ppermute(part, 'fsdp', [(i, i ^ bit) for i in range(size)])  17 us
    pallas_call x1, Pallas kernels, hidden_grads(): pl.pallas_call(kernel, out_shape=shaped((size, parts, count, share, width...  16.7 us
  transfers between devices with their start and end apart: 52, of which 32 were waited for; matrix products, arithmetic and copies ran while one was open for 6% of the time, Pallas kernels for 14%

commit v1 on v0

--- a/solution.py
+++ b/solution.py
@@ -67,7 +67,7 @@
 
 def cost(micros):
     return pl.CostEstimate(
-        flops=int(micros * 9e8), bytes_accessed=int(micros * 1e6), transcendentals=0
+        flops=int(micros * 900000000.0), bytes_accessed=int(micros * 1000000.0), transcendentals=0
     )
 
 
@@ -120,7 +120,9 @@
         xn = x * pair_inverse(x) * gain_ref[...]
         qr_ref[:, at] = (xn * cos_ref[...] + partner(xn) * sin_ref[...]).astype(LOW)
     for h in range(heads):
-        qs[h] = qr_ref[:, HEAD * h : HEAD * (h + 1)]
+        qs[h // GROUP, (h % GROUP) * rows : (h % GROUP + 1) * rows] = qr_ref[
+            :, HEAD * h : HEAD * (h + 1)
+        ]
     for j in range(slots):
         for k in range(kvh):
             ks[j * kvh + k] = kv_refs[j][:, HEAD * k : HEAD * (k + 1)]
@@ -128,28 +130,22 @@
             vs[j * kvh + k] = jnp.concatenate([vT, jnp.ones_like(vT)], axis=0).astype(LOW)
     oT_ref[...] = jnp.zeros_like(oT_ref)
 
-    def step(t, carry):
-        c = where_ref[t // kvh]
-        k = lax.rem(t, kvh)
+    def step(j, carry):
+        c = where_ref[j]
 
         @pl.when((c <= me) & (c >= 0))
         def _():
-            @pl.when(k == 0)
-            def _():
-                bias[...] = bias_of(c * rows, me * rows, bounds_ref, rows, rows)
-
-            kb = ks[t]
-            vaug = vs[t]
+            mask = bias_of(c * rows, me * rows, bounds_ref, rows, rows)
             for g in range(GROUP):
-                s = contract_cols(kb, qs[k * GROUP + g])
+                bias[:, g * rows : (g + 1) * rows] = mask
+            for k in range(kvh):
+                s = contract_cols(ks[j * kvh + k], qs[k])
                 p = jnp.exp2(s * (0.125 * LOG2E) + bias[...]).astype(LOW)
-                oT_ref[k, :, g * rows : (g + 1) * rows] += jnp.dot(
-                    vaug, p, preferred_element_type=jnp.float32
-                )
+                oT_ref[k] += jnp.dot(vs[j * kvh + k], p, preferred_element_type=jnp.float32)
 
         return carry
 
-    lax.fori_loop(0, slots * kvh, step, 0)
+    lax.fori_loop(0, slots, step, 0)
     for k in range(kvh):
         oT = oT_ref[k, :HEAD, :] * (1.0 / oT_ref[k, HEAD : HEAD + 1, :])
         oT_ref[k, :HEAD, :] = oT
@@ -160,9 +156,9 @@
 
 def bwd_kernel(slots, where_ref, bounds_ref, q_ref, qr_ref, dob_ref, oT_ref, *refs):
     kv_refs = refs[:slots]
-    gain_ref, cos_ref, sin_ref, _, _, dqb_ref = refs[slots : slots + 6]
-    dkv_refs = refs[slots + 6 : 2 * slots + 6]
-    gg_ref, qs, ds_, ks, vs, kTs, dks, dvs, logl, delta, dqT, bias = refs[2 * slots + 6 :]
+    gain_ref, cos_ref, sin_ref, _, dqb_ref = refs[slots : slots + 5]
+    dkv_refs = refs[slots + 5 : 2 * slots + 5]
+    gg_ref, qs, ds_, ks, vs, kTs, dks, dvs, logl, delta, dqT, bias = refs[2 * slots + 5 :]
     rows, width = kv_refs[0].shape
     width //= 2
     heads = q_ref.shape[1] // HEAD
@@ -171,9 +167,9 @@
     for h in range(heads):
         k, g = h // GROUP, h % GROUP
         at = slice(g * rows, (g + 1) * rows)
-        qs[h] = qr_ref[:, HEAD * h : HEAD * (h + 1)]
+        qs[k, at] = qr_ref[:, HEAD * h : HEAD * (h + 1)]
         d = dob_ref[:, HEAD * h : HEAD * (h + 1)]
-        ds_[h] = d
+        ds_[k, at] = d
         dT = d.astype(jnp.float32).T
         delta[k, :, at] = jnp.broadcast_to(
             jnp.sum(dT * oT_ref[k, :HEAD, at], axis=0, keepdims=True), (8, rows)
@@ -189,44 +185,35 @@
             kTs[t] = kb.astype(jnp.float32).T.astype(LOW)
     dqT[...] = jnp.zeros_like(dqT)
 
-    def step(t, carry):
-        c = where_ref[t // kvh]
-        k = lax.rem(t, kvh)
+    def step(j, carry):
+        c = where_ref[j]
         seen = (c <= me) & (c >= 0)
 
         @pl.when(seen)
         def _():
-            @pl.when(k == 0)
-            def _():
-                bias[...] = bias_of(c * rows, me * rows, bounds_ref, rows, rows)
-
-            kb = ks[t]
-            vb = vs[t]
-            kT = kTs[t]
-            dk = jnp.zeros((rows, HEAD), jnp.float32)
-            dv = jnp.zeros((rows, HEAD), jnp.float32)
+            mask = bias_of(c * rows, me * rows, bounds_ref, rows, rows)
             for g in range(GROUP):
-                at = slice(g * rows, (g + 1) * rows)
-                qh = qs[k * GROUP + g]
-                dh = ds_[k * GROUP + g]
-                s = contract_cols(kb, qh)
-                p = jnp.exp2(s * (0.125 * LOG2E) + (bias[...] - logl[k, 0:1, at]))
-                dp = contract_cols(vb, dh)
-                ds = (p * (dp - delta[k, 0:1, at])).astype(LOW)
-                dv += jnp.dot(p.astype(LOW), dh, preferred_element_type=jnp.float32)
-                dk += jnp.dot(ds, qh, preferred_element_type=jnp.float32)
-                dqT[k, :, at] += jnp.dot(kT, ds, preferred_element_type=jnp.float32)
-            dks[t] = (dk * 0.125).astype(LOW)
-            dvs[t] = dv.astype(LOW)
+                bias[:, g * rows : (g + 1) * rows] = mask
+            for k in range(kvh):
+                t = j * kvh + k
+                s = contract_cols(ks[t], qs[k])
+                dp = contract_cols(vs[t], ds_[k])
+                p = jnp.exp2(s * (0.125 * LOG2E) + (bias[...] - logl[k, 0:1]))
+                ds = (p * (dp - delta[k, 0:1])).astype(LOW)
+                dvs[t] = jnp.dot(p.astype(LOW), ds_[k], preferred_element_type=jnp.float32).astype(LOW)
+                dk = jnp.dot(ds, qs[k], preferred_element_type=jnp.float32)
+                dks[t] = (dk * 0.125).astype(LOW)
+                dqT[k] += jnp.dot(kTs[t], ds, preferred_element_type=jnp.float32)
 
         @pl.when(jnp.logical_not(seen))
         def _():
-            dks[t] = jnp.zeros((rows, HEAD), LOW)
-            dvs[t] = jnp.zeros((rows, HEAD), LOW)
+            for k in range(kvh):
+                dks[j * kvh + k] = jnp.zeros((rows, HEAD), LOW)
+                dvs[j * kvh + k] = jnp.zeros((rows, HEAD), LOW)
 
         return carry
 
-    lax.fori_loop(0, slots * kvh, step, 0)
+    lax.fori_loop(0, slots, step, 0)
     for j in range(slots):
         for k in range(kvh):
             t = j * kvh + k
@@ -292,10 +279,10 @@
         in_specs=[SMEM, SMEM] + [VMEM] * (4 + slots),
         out_specs=(VMEM,) * 3,
         scratch_shapes=[
-            pltpu.VMEM((heads * GROUP, rows, HEAD), LOW),
+            pltpu.VMEM((heads, GROUP * rows, HEAD), LOW),
             pltpu.VMEM((slots * heads, rows, HEAD), LOW),
             pltpu.VMEM((slots * heads, 2 * HEAD, rows), LOW),
-            pltpu.VMEM((rows, rows), jnp.float32),
+            pltpu.VMEM((rows, GROUP * rows), jnp.float32),
         ],
         compiler_params=PARAMS,
         name="attend",
@@ -312,11 +299,11 @@
         out_shape=(shaped(q.shape),)
         + (shaped(kv[0].shape),) * slots
         + (shaped((1, 2 * HEAD), jnp.float32),),
-        in_specs=[SMEM, SMEM] + [VMEM] * (7 + slots) + [ANY] * 2,
+        in_specs=[SMEM, SMEM] + [VMEM] * (7 + slots) + [ANY],
         out_specs=(VMEM,) * (2 + slots),
         scratch_shapes=[
-            pltpu.VMEM((heads * GROUP, rows, HEAD), LOW),
-            pltpu.VMEM((heads * GROUP, rows, HEAD), LOW),
+            pltpu.VMEM((heads, GROUP * rows, HEAD), LOW),
+            pltpu.VMEM((heads, GROUP * rows, HEAD), LOW),
             pltpu.VMEM((slots * heads, rows, HEAD), LOW),
             pltpu.VMEM((slots * heads, rows, HEAD), LOW),
             pltpu.VMEM((slots * heads, HEAD, rows), LOW),
@@ -325,7 +312,7 @@
             pltpu.VMEM((heads, 8, GROUP * rows), jnp.float32),
             pltpu.VMEM((heads, 8, GROUP * rows), jnp.float32),
             pltpu.VMEM((heads, HEAD, GROUP * rows), jnp.float32),
-            pltpu.VMEM((rows, rows), jnp.float32),
+            pltpu.VMEM((rows, GROUP * rows), jnp.float32),
         ],
         compiler_params=PARAMS,
         name="attend_back",
@@ -539,182 +526,84 @@
     return copies
 
 
-def ffn(where, tokens, pulled, weights, before=(), later=()):
+def ffn(where, tokens, pulled, weights):
     rows, model = tokens[0].shape
-    size, parts, _, _, width = weights.shape
+    size, parts, count, share, width = weights.shape
     total = rows * parts
+    tall = model // parts
 
     def kernel(where_ref, *refs):
         weights_ref = refs[6]
-        more = len(before)
-        sums = refs[7 : 7 + more]
-        refs = refs[: 7 + more] + refs[7 + more + len(later) :]
-        keep, send, middle, d_gate, d_up = refs[7 + more : 12 + more]
-        hn, cot, w_gate, w_up, w_down, sem_h, sem_c, sem_g, sem_u, sem_d = refs[12 + more :]
+        sums, grads = refs[7:11], refs[11]
+        left, w_gate, w_up, w_down, right, back, stage = refs[12:19]
+        sem_h, sem_c, sem_g, sem_u, sem_d, sem_s, sem_o = refs[19:]
+        me = where_ref[size + 1]
         gates = weight_copies(where_ref, weights_ref, 0, w_gate, sem_g)
-        reads = token_copies(refs[:3], hn, sem_h)
+        reads = token_copies(refs[:3], left.at[0], sem_h)
         ups = weight_copies(where_ref, weights_ref, 1, w_up, sem_u)
-        pulls = token_copies(refs[3:6], cot, sem_c)
+        pulls = token_copies(refs[3:6], left.at[1], sem_c)
         downs = weight_copies(where_ref, weights_ref, 2, w_down, sem_d)
         for copies in (gates, reads, ups, pulls, downs):
             begin(copies)
 
+        def sum_copies(i):
+            return [
+                pltpu.make_async_copy(
+                    back.at[j, pl.ds((2 * i + odd) * rows, rows)],
+                    sums[2 * j + odd].at[i],
+                    sem_s.at[j, 2 * i + odd],
+                )
+                for j in (0, 1)
+                for odd in (0, 1)
+            ]
+
         def token_part(i, carry):
-            at = pl.ds(pl.multiple_of(i * rows, rows), rows)
+            at = pl.ds(pl.multiple_of(i * 2 * rows, 2 * rows), 2 * rows)
 
             @pl.when(i == 0)
             def _():
                 finish(gates)
                 finish(reads)
 
-            g = jnp.dot(hn[at], w_gate[...], preferred_element_type=jnp.float32)
+            g = jnp.dot(left[0, at], w_gate[...], preferred_element_type=jnp.float32)
 
             @pl.when(i == 0)
             def _():
                 finish(ups)
 
-            u = jnp.dot(hn[at], w_up[...], preferred_element_type=jnp.float32)
+            u = jnp.dot(left[0, at], w_up[...], preferred_element_type=jnp.float32)
             sigma = jax.nn.sigmoid(g)
             active = g * sigma
-            middle[at] = (active * u).astype(LOW)
+            right[2, at] = (active * u).astype(LOW)
 
             @pl.when(i == 0)
             def _():
                 finish(pulls)
                 finish(downs)
 
-            d = jnp.dot(cot[at], w_down[...], preferred_element_type=jnp.float32)
-            d_gate[at] = (d * u * sigma * (1.0 + g * (1.0 - sigma))).astype(LOW)
-            d_up[at] = (d * active).astype(LOW)
-            back = contract_cols(d_gate[at], w_gate[...]) + contract_cols(d_up[at], w_up[...])
-            index = i // 2
-            for j, out in enumerate((keep, send)):
-
-                @pl.when(lax.rem(i, 2) == j)
-                def _():
-                    if more:
-                        out[index] = (back + sums[j][index].astype(jnp.float32)).astype(LOW)
-                    else:
-                        out[index] = back.astype(LOW)
-
+            d = jnp.dot(left[1, at], w_down[...], preferred_element_type=jnp.float32)
+            right[0, at] = (d * u * sigma * (1.0 + g * (1.0 - sigma))).astype(LOW)
+            right[1, at] = (d * active).astype(LOW)
+            back[0, at] = (
+                contract_cols(right[0, at], w_gate[...]) + contract_cols(right[1, at], w_up[...])
+            ).astype(LOW)
+            back[1, at] = contract_cols(right[2, at], w_down[...]).astype(LOW)
+            begin(sum_copies(i))
             return carry
 
-        lax.fori_loop(0, parts, token_part, 0)
-
-    return pl.pallas_call(
-        kernel,
-        out_shape=(shaped((2, rows, model)),) * 2 + (shaped((total, width)),) * 3,
-        in_specs=[SMEM] + [ANY] * 7 + [VMEM] * len(before) + [ANY] * len(later),
-        out_specs=(VMEM,) * 5,
-        scratch_shapes=[pltpu.VMEM((total, model), LOW)] * 2
-        + [pltpu.VMEM((model, width), LOW)] * 3
-        + [pltpu.SemaphoreType.DMA((4,))] * 2
-        + [pltpu.SemaphoreType.DMA((size * parts,))] * 3,
-        compiler_params=PARAMS,
-        name="ffn",
-        cost_estimate=cost(15),
-    )(where, *tokens, *pulled, weights, *before, *later)
-
-
-def ffn_out(where, middles, weights, later):
-    count = len(weights)
-    size, parts, _, share, _ = weights[0].shape
-    model = parts * size * share
-    rows = middles[0].shape[0] // parts
-
-    def kernel(where_ref, *refs):
-        mids, weight_refs = refs[:count], refs[count : 2 * count]
-        keep, send = refs[2 * count + 1 : 2 * count + 3]
-        downs, sems = refs[2 * count + 3 : 3 * count + 3], refs[3 * count + 3 :]
-        copies = [
-            weight_copies(where_ref, weight_refs[j], 2, downs[j], sems[j]) for j in range(count)
-        ]
-        for each in copies:
-            begin(each)
-        for each in copies:
-            finish(each)
-
-        def token_part(i, carry):
-            at = pl.ds(pl.multiple_of(i * rows, rows), rows)
-            d = sum(contract_cols(mids[j][at], downs[j][...]) for j in range(count)).astype(LOW)
-            index = i // 2
-
-            @pl.when(lax.rem(i, 2) == 0)
-            def _():
-                keep[index] = d
-
-            @pl.when(lax.rem(i, 2) == 1)
-            def _():
-                send[index] = d
-
-            return carry
-
-        lax.fori_loop(0, parts, token_part, 0)
-
-    return pl.pallas_call(
-        kernel,
-        out_shape=(shaped((2, rows, model)), shaped((2, rows, model))),
-        in_specs=[SMEM] + [VMEM] * count + [ANY] * (count + 1),
-        out_specs=(VMEM,) * 2,
-        scratch_shapes=[pltpu.VMEM((model, each.shape[-1]), LOW) for each in weights]
-        + [pltpu.SemaphoreType.DMA((size * parts,))] * count,
-        compiler_params=PARAMS,
-        name="ffn_out",
-        cost_estimate=cost(9),
-    )(where, *middles, *weights, later)
-
-
-def hidden_grads(where, tokens, rights, pulled, lasts, later=()):
-    rows, model = tokens[0].shape
-    lefts = len(rights)
-    rights = rights + lasts
-    count = len(rights)
-    size = where.shape[0] - 2
-    total, width = rights[0].shape
-    parts = total // rows
-    tall = model // parts
-    share = tall // size
-
-    def kernel(where_ref, *refs):
-        refs = refs[: 6 + count] + refs[6 + count + len(later) :]
-        out = refs[6 + count]
-        left, right, stage, sem_h, sem_c, sem_r, sem_o = refs[7 + count :]
-        me = where_ref[size + 1]
-        reads = token_copies(refs[:3], left.at[0], sem_h)
-        pulls = token_copies(refs[3:6], left.at[1], sem_c)
-        operands = [
-            pltpu.make_async_copy(refs[6 + m], right.at[m], sem_r.at[m]) for m in range(count)
-        ]
-        begin(reads)
-        begin(operands)
-        begin(pulls)
+        lax.fori_loop(0, parts // 2, token_part, 0)
 
         def write(i, c):
-            m, part = i // parts, lax.rem(i, parts)
             return pltpu.make_async_copy(
-                stage.at[i, pl.ds(c * share, share)], out.at[c, me ^ part, m], sem_o.at[i, c]
+                stage.at[i, pl.ds(c * share, share)],
+                grads.at[c, me ^ lax.rem(i, parts), i // parts],
+                sem_o.at[i, c],
             )
 
         def block(i, carry):
             m, part = i // parts, lax.rem(i, parts)
-
-            @pl.when(i == 0)
-            def _():
-                finish(reads)
-
-            for k in range(count):
-
-                @pl.when(i == k * parts)
-                def _():
-                    operands[k].wait()
-
-            @pl.when(i == lefts * parts)
-            def _():
-                finish(pulls)
-
             column = pl.multiple_of(part * tall, tall)
-            which = (m >= lefts).astype(jnp.int32)
-            stage[i] = contract_rows(left[which, :, pl.ds(column, tall)], right[m]).astype(LOW)
+            stage[i] = contract_rows(left[m // 2, :, pl.ds(column, tall)], right[m]).astype(LOW)
             for c in range(size):
                 write(i, c).start()
             return carry
@@ -728,24 +617,31 @@
 
         lax.fori_loop(0, count * parts, drain, 0)
 
+        def drain_sums(i, carry):
+            finish(sum_copies(i))
+            return carry
+
+        lax.fori_loop(0, parts // 2, drain_sums, 0)
+
     return pl.pallas_call(
         kernel,
-        out_shape=shaped((size, parts, count, share, width)),
-        in_specs=[SMEM] + [ANY] * (6 + count + len(later)),
-        out_specs=ANY,
-        scratch_shapes=[
+        out_shape=(shaped((2, rows, model)),) * 4 + (shaped((size, parts, count, share, width)),),
+        in_specs=[SMEM] + [ANY] * 7,
+        out_specs=(ANY,) * 5,
+        scratch_shapes=[pltpu.VMEM((2, total, model), LOW)]
+        + [pltpu.VMEM((model, width), LOW)] * 3
+        + [
+            pltpu.VMEM((3, total, width), LOW),
             pltpu.VMEM((2, total, model), LOW),
-            pltpu.VMEM((count, total, width), LOW),
             pltpu.VMEM((count * parts, tall, width), LOW),
-            pltpu.SemaphoreType.DMA((4,)),
-            pltpu.SemaphoreType.DMA((4,)),
-            pltpu.SemaphoreType.DMA((count,)),
-            pltpu.SemaphoreType.DMA((count * parts, size)),
-        ],
+        ]
+        + [pltpu.SemaphoreType.DMA((4,))] * 2
+        + [pltpu.SemaphoreType.DMA((size * parts,))] * 3
+        + [pltpu.SemaphoreType.DMA((2, parts)), pltpu.SemaphoreType.DMA((count * parts, size))],
         compiler_params=PARAMS,
-        name="hidden_grads",
-        cost_estimate=cost(3 * count),
-    )(where, *tokens, *pulled, *rights, *later)
+        name="ffn",
+        cost_estimate=cost(37),
+    )(where, *tokens, *pulled, weights)
 
 
 def head_grads(where, lefts, rights, gains=None, small=0, later=()):
@@ -762,63 +658,67 @@
 
     def kernel(where_ref, *refs):
         left_refs, right_refs, refs = refs[:count], refs[count : 2 * count], refs[2 * count :]
-        keep, send = refs[-2:]
+        *gain_refs, keep, send, stage, sems = refs[: len(gains)] + refs[len(gains) + len(later) :]
         me = where_ref[size + 1]
         here = where_ref[size]
 
-        def place(bit, c):
-            return bit // 2, lax.rem(here - c + size, size) if size <= LINE else c
-
         def block(part, carry):
             column = pl.multiple_of(part * tall, tall)
-            bit = me ^ part
             for m in range(count):
                 grads = contract_rows(
                     left_refs[m][:, pl.ds(column, tall)], right_refs[m][...]
                 ).astype(LOW)
-                for out, odd in ((keep, 0), (send, 1)):
+                for c in range(size):
+                    stage[part * size + c, :share, m * each : (m + 1) * each] = grads[
+                        c * share : (c + 1) * share
+                    ]
+            return carry
+
+        lax.fori_loop(0, parts, block, 0)
+        if pad:
+            pairs = [gain[:, :HEAD] + gain[:, HEAD:] for gain in gain_refs[2:4]]
+            for i in range(parts * size):
+                pieces = [gain[:, i * share : (i + 1) * share] for gain in gain_refs[:2]]
+                pieces += [pair[:, i * small : (i + 1) * small] for pair in pairs]
+                row = jnp.concatenate(
+                    [
+                        jnp.concatenate(
+                            [piece, jnp.zeros((1, 128 - piece.shape[1]), jnp.float32)], axis=1
+                        )
+                        for piece in pieces
+                    ],
+                    axis=1,
+                )
+                stage[i, share:] = jnp.broadcast_to(row, (pad, width)).astype(LOW)
+
+        def each_copy(do):
+            for part in range(parts):
+                bit = me ^ part
+                for odd, out in ((0, keep), (1, send)):
 
                     @pl.when(lax.rem(bit, 2) == odd)
                     def _():
                         for c in range(size):
-                            index, step = place(bit, c)
-                            out[index, step, :share, m * each : (m + 1) * each] = grads[
-                                c * share : (c + 1) * share
-                            ]
-
-            return carry
-
-        lax.fori_loop(0, parts, block, 0)
-        if pad:
-            pairs = [gain[:, :HEAD] + gain[:, HEAD:] for gain in refs[2:4]]
-            for part in range(parts):
-                bit = me ^ part
-                for c in range(size):
-                    i = part * size + c
-                    index, step = place(bit, c)
-                    pieces = [gain[:, i * share : (i + 1) * share] for gain in refs[:2]]
-                    pieces += [pair[:, i * small : (i + 1) * small] for pair in pairs]
-                    row = jnp.concatenate(
-                        [
-                            jnp.concatenate(
-                                [piece, jnp.zeros((1, 128 - piece.shape[1]), jnp.float32)], axis=1
+                            step = lax.rem(here - c + size, size) if size <= LINE else c
+                            i = part * size + c
+                            do(
+                                pltpu.make_async_copy(
+                                    stage.at[i], out.at[bit // 2, step], sems.at[i]
+                                )
                             )
-                            for piece in pieces
-                        ],
-                        axis=1,
-                    )
-                    tile = jnp.broadcast_to(row, (pad, width)).astype(LOW)
-                    for out, odd in ((keep, 0), (send, 1)):
-
-                        @pl.when(lax.rem(bit, 2) == odd)
-                        def _():
-                            out[index, step, share:] = tile
+
+        each_copy(lambda copy: copy.start())
+        each_copy(lambda copy: copy.wait())
 
     return pl.pallas_call(
         kernel,
         out_shape=(shaped((2, size, share + pad, width)),) * 2,
         in_specs=[SMEM] + [VMEM] * (2 * count + len(gains)) + [ANY] * len(later),
-        out_specs=(VMEM,) * 2,
+        out_specs=(ANY,) * 2,
+        scratch_shapes=[
+            pltpu.VMEM((parts * size, share + pad, width), LOW),
+            pltpu.SemaphoreType.DMA((parts * size,)),
+        ],
         compiler_params=PARAMS,
         name="head_grads",
         cost_estimate=cost(3),
@@ -858,6 +758,17 @@
     for step in range(1, size):
         total = turn(moving).astype(jnp.float32) + terms[(step + 1) % size].astype(jnp.float32)
         moving = total.astype(LOW)
+    return total
+
+
+def ctx_sum_direct(terms):
+    size = lax.axis_size("ctx")
+    if size > LINE:
+        return ctx_sum(terms)
+    total = terms[0].astype(jnp.float32)
+    for step in range(1, size):
+        part = lax.ppermute(terms[step], "ctx", [(i, (i - step) % size) for i in range(size)])
+        total = total + part.astype(jnp.float32)
     return total
 
 
@@ -915,7 +826,7 @@
     size, parts, count, share, width = terms.shape
     own = lax.psum_scatter(terms.reshape(-1, width), "ctx", scatter_dimension=0, tiled=True)
     own = own.reshape(parts, count, share, width)
-    return [own[0]] + [flip(own[bit], bit) for bit in range(1, parts)]
+    return own, [own[0]] + [flip(own[bit], bit) for bit in range(1, parts)]
 
 
 def body(
@@ -1001,17 +912,12 @@
     hidden_normed = (hidden * second_inv * gain_ffn).astype(LOW)
 
     hidden_all = group_tokens(hidden_normed)
-    keep, send, middle, grad_gate_low, grad_up_low = ffn(
-        where, hidden_all, pulled_all, weights[0]
-    )
+    keep, send, keep_out, send_out, terms = ffn(where, hidden_all, pulled_all, weights[0])
     near, far = chip_sum(keep, send)
     normed_part = pair_sum(near, far).astype(LOW)
-    terms = hidden_grads(
-        where, hidden_all, [grad_gate_low, grad_up_low], pulled_all, [middle], [far]
-    )
-    grad_gate, grad_up, grad_down = join_columns(where, [scatter_hidden(terms)])
+    hidden_sum, traded_back = scatter_hidden(terms)
+    grad_gate, grad_up, grad_down = join_columns(where, [traded_back])
     grad_down = grad_down.T
-    feed_terms = ffn_out(where, [middle], weights, normed_part)
     grad_normed_ffn = normed_part.astype(jnp.float32) + swap(normed_part).astype(jnp.float32)
 
     ffn_gain_part = jnp.sum(grad_normed_ffn * hidden * second_inv, axis=0) * 0.5
@@ -1024,7 +930,7 @@
     ).astype(LOW)
     grad_query_low, *key_terms, query_gain_pair = attend_back(
         where, bounds, queries, query_rot, grad_mixed, mixed, kv, gain_query, cosine, sine,
-        [terms, feed_terms[0]],
+        [terms],
     )
     near, far = chip_sum(
         *head_grads(where, [normed, grad_hidden_low], [grad_query_low, mixed_low])
@@ -1034,7 +940,7 @@
     own_terms, _ = back_sum([key_terms[0]] + [moved[i] for i in range(size - 1)])
     grad_query = heads_sum[:, :width]
     grad_output = heads_sum[:, width:].T
-    feed_part = group_sum(*feed_terms).astype(LOW)
+    feed_part = group_sum(keep_out, collect([send_out], [grad_hidden_low])[0]).astype(LOW)
     feed = feed_part.astype(jnp.float32) + swap(feed_part).astype(jnp.float32)
     result = (hidden + feed).astype(LOW)[None]
     grad_kv_low, key_gain_pair = keys_back(
@@ -1047,19 +953,20 @@
     normed_low, attn_gain_part = normed_back(
         grad_query_low, grad_kv_low, full_query, full_kv, inputs[0], first_inv
     )
-    own_kv = ctx_sum(
-        group_sum(
-            *head_grads(
-                where,
-                [normed],
-                [grad_kv_low],
-                [attn_gain_part, ffn_gain_part[None], query_gain_pair, key_gain_pair],
-                small,
-            )
-        ).astype(LOW)
-    )
+    near, far = chip_sum(
+        *head_grads(
+            where,
+            [normed],
+            [grad_kv_low],
+            [attn_gain_part, ffn_gain_part[None], query_gain_pair, key_gain_pair],
+            small,
+        )
+    )
+    kv_sum = pair_sum(near, far).astype(LOW)
+    own_kv = ctx_sum_direct(collect([kv_sum], [hidden_sum])[0])
     grad_key = own_kv[:share, :kv_width]
     grad_value = own_kv[:share, kv_width:]
+    normed_low = collect([normed_low], [far])[0]
     grad_normed = normed_low.astype(jnp.float32) + swap(normed_low).astype(jnp.float32)
     own_gains = own_kv[share].astype(LOW)
     grad_gains = own_gains.astype(jnp.float32) + swap(own_gains).astype(jnp.float32)

time: 548 us -> 495 us (0.903)
  starting transfers between devices: 74.3 us -> 51.1 us
  Pallas kernels: 126 us -> 110 us
  waiting for transfers between devices: 281 us -> 267 us
    ppermute x15 -> x12, starting transfers between devices: 33.4 us -> 7.08 us  [turn(): return lax.ppermute(part, 'ctx', [(i, (i + 1) % size) for i in range(size)])]
    ppermute x24, waiting for transfers between devices: 95 us -> 71.6 us  [flip(): return lax.ppermute(part, 'fsdp', [(i, i ^ bit) for i in range(size)])]
    ppermute x15 -> x12, waiting for transfers between devices: 74.6 us -> 90.8 us  [turn(): return lax.ppermute(part, 'ctx', [(i, (i + 1) % size) for i in range(size)])]
    pallas_call x3 -> x1, Pallas kernels: 54.7 us -> 39.6 us  [ffn(): pl.pallas_call(kernel, out_shape=(shaped((2, rows, model)),) * 4 + (shape...]
    ppermute x5, waiting for transfers between devices: 44 us -> 30.9 us  [swap(): return lax.ppermute(part, 'tp', [(0, 1), (1, 0)])]
    ppermute x0 -> x3, waiting for transfers between devices: none -> 6.36 us  [ctx_sum_direct(): lax.ppermute(terms[step], 'ctx', [(i, (i - step) % size) for i in range(s...]
    pallas_call x11 -> x14, Pallas kernels: 14.6 us -> 17.6 us  [collect(): pl.pallas_call(kernel, out_shape=shaped((count,) + parts[0].shape, parts[...]
  transfers between devices with their start and end apart: 52 -> 52, of which waited for: 32 -> 32; matrix products, arithmetic and copies ran while one was open for 6% -> 7% of each run, Pallas kernels for 14% -> 12%
where the time goes in v1:
time: 495 us; the launch traced here: 489 us
  waiting for transfers between devices  267 us (54%)
  Pallas kernels  110 us (22%)
  starting transfers between devices  51.1 us (10%)
  other arithmetic  22.5 us (5%)
  between operations  15.2 us (3%)
  local copies, waits for them, and re-layouts  13.1 us (3%)
  matrix products  9.39 us (2%)
    ppermute x12, waiting for transfers between devices, turn(): return lax.ppermute(part, 'ctx', [(i, (i + 1) % size) for i in range(size)])  90.8 us
    ppermute x24, waiting for transfers between devices, flip(): return lax.ppermute(part, 'fsdp', [(i, i ^ bit) for i in range(size)])  71.6 us
    ppermute x3, waiting for transfers between devices, back_sum(): lax.ppermute(terms[step], 'ctx', [(i, i - step) for i in range(step, size)])  46 us
    pallas_call x1, Pallas kernels, ffn(): pl.pallas_call(kernel, out_shape=(shaped((2, rows, model)),) * 4 + (shape...  39.6 us
    ppermute x5, waiting for transfers between devices, swap(): return lax.ppermute(part, 'tp', [(0, 1), (1, 0)])  30.9 us
    pallas_call x14, Pallas kernels, collect(): pl.pallas_call(kernel, out_shape=shaped((count,) + parts[0].shape, parts[...  17.6 us
    ppermute x24, starting transfers between devices, flip(): return lax.ppermute(part, 'fsdp', [(i, i ^ bit) for i in range(size)])  17.1 us
    pallas_call x3, Pallas kernels, arrange(): pl.pallas_call(kernel, out_shape=tuple(shapes), in_specs=[SMEM] + [ANY] *...  13.6 us
  transfers between devices with their start and end apart: 52, of which 32 were waited for; matrix products, arithmetic and copies ran while one was open for 7% of the time, Pallas kernels for 12%

profile of v1, /device:TPU:0, one launch (start us, length us, event | category | flops | bytes accessed | tf_op | source)
XLA Modules:
  0.0 488.8 jit_solution(12168652544517606272)
XLA Ops:
  7.4 3.1 split_columns.1
  10.9 2.5 collective-permute-start.24
  15.5 5.6 %collective-permute-done.refs_1_ = bf16[112,512]{1,0:T(8,128)(2,1)S(1)} collective-permute-done((bf16[112,512]{1,0:T(8,128)(2,1)S(1)}, bf16[112,512]{1,0:T(8,128)(2,1)S(1)}, u32[]{:S(2)}, u32[]{:S(2)}) %collective-permute-start) | collective-permute-done | bytes 114720 | tf_op jit(solution)/shard_map/ppermute | solution.py:739
  21.1 6.6 %collective-permute-done.1.refs_2_ = bf16[112,512]{1,0:T(8,128)(2,1)S(1)} collective-permute-done((bf16[112,512]{1,0:T(8,128)(2,1)S(1)}, bf16[112,512]{1,0:T(8,128)(2,1)S(1)}, u32[]{:S(2)}, u32[]{:S(2)}) %collective-permute-start.1) | collective-permute-done | bytes 114720 | tf_op jit(solution)/shard_map/ppermute | solution.py:739
  27.8 6.6 %collective-permute-done.2.refs_3_.refs_4_ = bf16[112,512]{1,0:T(8,128)(2,1)S(1)} collective-permute-done((bf16[112,512]{1,0:T(8,128)(2,1)S(1)}, bf16[112,512]{1,0:T(8,128)(2,1)S(1)}, u32[]{:S(2)}, u32[]{:S(2)}) %collective-permute-start.2) | collective-permute-done | bytes 114720 | tf_op jit(solution)/shard_map/ppermute | solution.py:739
  34.4 2.3 collective-permute-done.25.refs_3_
  37.4 3.5 collect.23
  47.2 2.5 collective-permute-done.5.refs_1_
  51.7 6.3 %collective-permute-done.6.refs_2_ = bf16[96,768]{1,0:T(8,128)(2,1)S(1)} collective-permute-done((bf16[96,768]{1,0:T(8,128)(2,1)S(1)}, bf16[96,768]{1,0:T(8,128)(2,1)S(1)}, u32[]{:S(2)}, u32[]{:S(2)}) %collective-permute-start.6) | collective-permute-done | bytes 147488 | tf_op jit(solution)/shard_map/ppermute | solution.py:739
  60.1 8.4 %collective-permute-done.7.refs_3_ = bf16[96,768]{1,0:T(8,128)(2,1)S(1)} collective-permute-done((bf16[96,768]{1,0:T(8,128)(2,1)S(1)}, bf16[96,768]{1,0:T(8,128)(2,1)S(1)}, u32[]{:S(2)}, u32[]{:S(2)}) %collective-permute-start.7) | collective-permute-done | bytes 147488 | tf_op jit(solution)/shard_map/ppermute | solution.py:739
  69.3 2.6 collective-permute-start.8
  72.8 14.1 %collective-permute-done.14.refs_2_ = bf16[96,768]{1,0:T(8,128)(2,1)S(1)} collective-permute-done((bf16[96,768]{1,0:T(8,128)(2,1)S(1)}, bf16[96,768]{1,0:T(8,128)(2,1)S(1)}, u32[]{:S(2)}, u32[]{:S(2)}) %collective-permute-start.14) | collective-permute-done | bytes 147488 | tf_op jit(solution)/shard_map/ppermute | solution.py:739
  88.5 9.6 %collective-permute-done.15.refs_3_ = bf16[96,768]{1,0:T(8,128)(2,1)S(1)} collective-permute-done((bf16[96,768]{1,0:T(8,128)(2,1)S(1)}, bf16[96,768]{1,0:T(8,128)(2,1)S(1)}, u32[]{:S(2)}, u32[]{:S(2)}) %collective-permute-start.15) | collective-permute-done | bytes 147488 | tf_op jit(solution)/shard_map/ppermute | solution.py:739
  101.6 4.4 arrange.3
  113.0 8.7 %collective-permute-start.11 = (bf16[256,512]{1,0:T(8,128)(2,1)}, bf16[256,512]{1,0:T(8,128)(2,1)}, u32[]{:S(2)}, u32[]{:S(2)}) collective-permute-start(bf16[256,512]{1,0:T(8,128)(2,1)} %keys.1.refs_0_), channel_id=1, source_target_pairs={{0,4},{2,6},{1,5},{3,7},{8,12},{10,14},{9,13},{11,15},{16,20},{18,... | collective-permute-start | bytes 786440 | tf_op jit(solution)/shard_map/ppermute | solution.py:782
  121.7 2.5 collective-permute-start.12
  124.4 2.3 collect.19
  126.8 5.0 %arrange.4.wq = bf16[1536,768]{1,0:T(8,128)(2,1)} custom-call(s32[6]{0:T(128)S(1)} %pad_add_fusion.where_ref, bf16[4,96,768]{2,1,0:T(8,128)(2,1)S(1)} %collect.16.refs_0_, bf16[2,4,96,768]{3,2,1,0:T(8,128)(2,1)} %collective-permute-done.9.refs_1_, bf16[4,96,768]{2,1,0:T(8,128)(2,1)S(1)} %collective-permute-done.8.refs_1_.refs_2_.refs_4_), custom_call_target="tpu_custom_call" | custom-call | flops 1800000000 | bytes 2000000 | tf_op jit(solution)/shard_map/arrange/pallas_call | solution.py:493
  131.9 3.3 fusion.37.q_ref
  136.1 9.9 %collective-permute-done.12.refs_3_ = bf16[256,512]{1,0:T(8,128)(2,1)} collective-permute-done((bf16[256,512]{1,0:T(8,128)(2,1)}, bf16[256,512]{1,0:T(8,128)(2,1)}, u32[]{:S(2)}, u32[]{:S(2)}) %collective-permute-start.12) | collective-permute-done | bytes 262176 | tf_op jit(solution)/shard_map/ppermute | solution.py:782
  146.0 6.6 %attend.1 = (bf16[256,768]{1,0:T(8,128)(2,1)S(1)}, bf16[256,768]{1,0:T(8,128)(2,1)}, f32[4,128,768]{2,1,0:T(8,128)}) custom-call(s32[6]{0:T(128)S(1)} %pad_add_fusion.where_ref, s32[2]{0:T(128)S(1)} %bitcast.109, f32[256,768]{1,0:T(8,128)} %fusion.37.q_ref, bf16[256,512]{1,0:T(8,128)(2,1)} %keys.1.refs_0_, bf16[256,512]{1,0:T(8,128)(2,1)} %collective-permute-done.10.refs_1_, ...), custom_call_target="tpu_custom_call" | custom-call | flops 12600000512 | bytes 14000000 | tf_op jit(solution)/shard_map/attend/pallas_call | solution.py:272
  154.4 4.2 arrange.5
  158.6 2.6 convolution_convert_fusion
  165.1 11.9 %collective-permute-done.18 = bf16[256,1536]{1,0:T(8,128)(2,1)} collective-permute-done((bf16[256,1536]{1,0:T(8,128)(2,1)S(1)}, bf16[256,1536]{1,0:T(8,128)(2,1)}, u32[]{:S(2)}, u32[]{:S(2)}) %collective-permute-start.18) | collective-permute-done | bytes 786464 | tf_op jit(solution)/shard_map/ppermute | solution.py:734
  183.0 13.6 %collective-permute-done.19.refs_1_.refs_2_ = bf16[256,1536]{1,0:T(8,128)(2,1)S(1)} collective-permute-done((bf16[256,1536]{1,0:T(8,128)(2,1)S(1)}, bf16[256,1536]{1,0:T(8,128)(2,1)S(1)}, u32[]{:S(2)}, u32[]{:S(2)}) %collective-permute-start.19) | collective-permute-done | bytes 786464 | tf_op jit(solution)/shard_map/ppermute | solution.py:730
  198.2 3.7 collective-permute-done.20.refs_1_
  201.9 10.9 %all-gather.2.cloned.1.call-done = bf16[4608,864]{1,0:T(8,128)(2,1)} async-done(((bf16[1152,864]{1,0:T(8,128)(2,1)}), bf16[4608,864]{1,0:T(8,128)(2,1)}) %all-gather.2.cloned.1.call-update) | async-done | bytes 7962640 | tf_op jit(solution)/shard_map/all_gather | solution.py:883
  214.0 39.6 %ffn.1 = (bf16[2,256,1536]{2,1,0:T(8,128)(2,1)}, bf16[2,256,1536]{2,1,0:T(8,128)(2,1)}, bf16[2,256,1536]{2,1,0:T(8,128)(2,1)}, bf16[2,256,1536]{2,1,0:T(8,128)(2,1)}, bf16[4,4,3,96,864]{4,3,2,1,0:T(8,128)(2,1)}) custom-call(s32[6]{0:T(128)S(1)} %pad_add_fusion.where_ref, bf16[256,1536]{1,0:T(8,128)(2,1)S(1)} %multiply_convert_fusion.refs_0_, ...), custom_call_target="tpu_custom_call" | custom-call | flops 33300000768 | bytes 37000000 | tf_op jit(solution)/shard_map/ffn/pallas_call | solution.py:626
  253.8 3.6 collective-permute-done.26
  260.3 18.1 %collective-permute-done.27 = bf16[256,1536]{1,0:T(8,128)(2,1)S(1)} collective-permute-done((bf16[256,1536]{1,0:T(8,128)(2,1)S(1)}, bf16[256,1536]{1,0:T(8,128)(2,1)S(1)}, u32[]{:S(2)}, u32[]{:S(2)}) %collective-permute-start.27) | collective-permute-done | bytes 786464 | tf_op jit(solution)/shard_map/ppermute | solution.py:730
  281.4 17.4 %collective-permute-done.28 = bf16[256,1536]{1,0:T(8,128)(2,1)S(1)} collective-permute-done((bf16[256,1536]{1,0:T(8,128)(2,1)S(1)}, bf16[256,1536]{1,0:T(8,128)(2,1)S(1)}, u32[]{:S(2)}, u32[]{:S(2)}) %collective-permute-start.28) | collective-permute-done | bytes 786464 | tf_op jit(solution)/shard_map/ppermute | solution.py:734
  302.9 10.7 %attend_back.1 = (bf16[256,768]{1,0:T(8,128)(2,1)}, bf16[256,512]{1,0:T(8,128)(2,1)S(1)}, bf16[256,512]{1,0:T(8,128)(2,1)S(1)}, bf16[256,512]{1,0:T(8,128)(2,1)S...) custom-call(s32[6]{0:T(128)S(1)} %pad_add_fusion.where_ref, s32[2]{0:T(128)S(1)} %bitcast.110, ...), custom_call_target="tpu_custom_call" | custom-call | flops 15299999744 | bytes 17000000 | tf_op jit(solution)/shard_map/attend_back/pallas_call | solution.py:297
  314.6 5.6 %head_grads.2 = (bf16[2,4,96,1536]{3,2,1,0:T(8,128)(2,1)}, bf16[2,4,96,1536]{3,2,1,0:T(8,128)(2,1)}) custom-call(s32[6]{0:T(128)S(1)} %pad_add_fusion.where_ref, bf16[256,1536]{1,0:T(8,128)(2,1)S(1)} %fusion.3.refs_0_, bf16[256,1536]{1,0:T(8,128)(2,1)} %copy-done, bf16[256,768]{1,0:T(8,128)(2,1)S(1)} %copy-done.13, bf16[256,768]{1,0:T(8,128)(2,1)S(1)} %copy-done.12), custom_call_target="tpu_custom_call" | custom-call | flops 2700000000 | bytes 3000000 | tf_op jit(solution)/shard_map/head_grads/pallas_call | solution.py:713
  320.2 2.6 collect.24
  323.5 3.8 collective-permute-done.29
  327.4 2.5 fusion.15
  338.2 12.2 %collective-permute-done.30 = bf16[256,1536]{1,0:T(8,128)(2,1)S(1)} collective-permute-done((bf16[256,1536]{1,0:T(8,128)(2,1)}, bf16[256,1536]{1,0:T(8,128)(2,1)S(1)}, u32[]{:S(2)}, u32[]{:S(2)}) %collective-permute-start.30) | collective-permute-done | bytes 786464 | tf_op jit(solution)/shard_map/ppermute | solution.py:730
  353.4 12.4 %collective-permute-done.33 = bf16[256,512]{1,0:T(8,128)(2,1)S(1)} collective-permute-done((bf16[256,512]{1,0:T(8,128)(2,1)S(1)}, bf16[256,512]{1,0:T(8,128)(2,1)S(1)}, u32[]{:S(2)}, u32[]{:S(2)}) %collective-permute-start.33) | collective-permute-done | bytes 262176 | tf_op jit(solution)/shard_map/ppermute | solution.py:792
  365.8 33.6 %collective-permute-done.34 = bf16[256,512]{1,0:T(8,128)(2,1)S(1)} collective-permute-done((bf16[256,512]{1,0:T(8,128)(2,1)S(1)}, bf16[256,512]{1,0:T(8,128)(2,1)S(1)}, u32[]{:S(2)}, u32[]{:S(2)}) %collective-permute-start.34) | collective-permute-done | bytes 262176 | tf_op jit(solution)/shard_map/ppermute | solution.py:792
  400.2 3.6 normed_back.1
  403.8 4.1 head_grads.3
  413.7 14.0 %collective-permute-done.44 = bf16[96,1536]{1,0:T(8,128)(2,1)S(1)} collective-permute-done((bf16[96,1536]{1,0:T(8,128)(2,1)S(1)}, bf16[96,1536]{1,0:T(8,128)(2,1)S(1)}, u32[]{:S(2)}, u32[]{:S(2)}) %collective-permute-start.44) | collective-permute-done | bytes 294944 | tf_op jit(solution)/shard_map/ppermute | solution.py:739
  429.3 9.3 %collective-permute-done.45 = bf16[96,1536]{1,0:T(8,128)(2,1)S(1)} collective-permute-done((bf16[96,1536]{1,0:T(8,128)(2,1)S(1)}, bf16[96,1536]{1,0:T(8,128)(2,1)S(1)}, u32[]{:S(2)}, u32[]{:S(2)}) %collective-permute-start.45) | collective-permute-done | bytes 294944 | tf_op jit(solution)/shard_map/ppermute | solution.py:739
  441.2 7.7 %collective-permute-done.46 = bf16[96,1536]{1,0:T(8,128)(2,1)S(1)} collective-permute-done((bf16[96,1536]{1,0:T(8,128)(2,1)S(1)}, bf16[96,1536]{1,0:T(8,128)(2,1)S(1)}, u32[]{:S(2)}, u32[]{:S(2)}) %collective-permute-start.46) | collective-permute-done | bytes 294944 | tf_op jit(solution)/shard_map/ppermute | solution.py:739
  453.8 2.8 collective-permute-done.39
  456.5 3.6 collective-permute-done.40
  467.0 10.2 %collective-permute-done.49.refs_3_ = bf16[3,96,864]{2,1,0:T(8,128)(2,1)S(1)} collective-permute-done((bf16[3,96,864]{2,1,0:T(8,128)(2,1)S(1)}, bf16[3,96,864]{2,1,0:T(8,128)(2,1)S(1)}, u32[]{:S(2)}, u32[]{:S(2)}) %collective-permute-start.49) | collective-permute-done | bytes 497696 | tf_op jit(solution)/shard_map/ppermute | solution.py:730
  478.0 3.7 join_columns.1
  (232 shorter events, 89.1 us)
Async XLA Ops:
  7.2 205.6 %all-gather.2.cloned.1.call-start = ((), (), s32[]{:S(2)}) async-start(), calls=%async_computation.1 | async-start | bytes 10321920 | tf_op jit(solution)/shard_map/all_gather | solution.py:883
  10.4 23.9 %collective-permute-start.23 = (bf16[3,96,864]{2,1,0:T(8,128)(2,1)S(1)}, bf16[3,96,864]{2,1,0:T(8,128)(2,1)S(1)}, u32[]{:S(2)}, u32[]{:S(2)}) collective-permute-start(bf16[3,96,864]{2,1,0:T(8,128)(2,1)S(1)} %get-tuple-element.60), channel_id=1, source_target_pairs={{0,8},{8,0},{16,24},{24,16},{1,9},{9,1},{17,25},{25,17},{2,10},{10... | collective-permute-start | bytes 1493000 | tf_op jit(solution)/shard_map/ppermute | solution.py:730
  10.9 23.5 %collective-permute-start.24 = (bf16[3,96,864]{2,1,0:T(8,128)(2,1)S(1)}, bf16[3,96,864]{2,1,0:T(8,128)(2,1)S(1)}, u32[]{:S(2)}, u32[]{:S(2)}) collective-permute-start(bf16[3,96,864]{2,1,0:T(8,128)(2,1)S(1)} %get-tuple-element.61), channel_id=1, source_target_pairs={{0,16},{8,24},{16,0},{24,8},{1,17},{9,25},{17,1},{25,9},{2,18},{10... | collective-permute-start | bytes 1493000 | tf_op jit(solution)/shard_map/ppermute | solution.py:730
  13.4 23.3 %collective-permute-start.25 = (bf16[3,96,864]{2,1,0:T(8,128)(2,1)}, bf16[3,96,864]{2,1,0:T(8,128)(2,1)S(1)}, u32[]{:S(2)}, u32[]{:S(2)}) collective-permute-start(bf16[3,96,864]{2,1,0:T(8,128)(2,1)} %get-tuple-element.62), channel_id=1, source_target_pairs={{0,24},{8,16},{16,8},{24,0},{1,25},{9,17},{17,9},{25,1},{2,26},{10... | collective-permute-start | bytes 1493000 | tf_op jit(solution)/shard_map/ppermute | solution.py:730
  13.6 7.5 %collective-permute-start = (bf16[112,512]{1,0:T(8,128)(2,1)S(1)}, bf16[112,512]{1,0:T(8,128)(2,1)S(1)}, u32[]{:S(2)}, u32[]{:S(2)}) collective-permute-start(bf16[112,512]{1,0:T(8,128)(2,1)S(1)} %fusion.23.refs_0_), channel_id=1, source_target_pairs={{0,2},{2,4},{4,6},{6,0},{1,3},{3,5},{5,7},{7,1},{8,10},{10,12},{12... | collective-permute-start | bytes 344072 | tf_op jit(solution)/shard_map/ppermute | solution.py:739
  21.1 6.6 %collective-permute-start.1 = (bf16[112,512]{1,0:T(8,128)(2,1)S(1)}, bf16[112,512]{1,0:T(8,128)(2,1)S(1)}, u32[]{:S(2)}, u32[]{:S(2)}) collective-permute-start(bf16[112,512]{1,0:T(8,128)(2,1)S(1)} %collective-permute-done.refs_1_), channel_id=1, source_target_pairs={{0,2},{2,4},{4,6},{6,0},{1,3},{3,5},{5,7},{7,1},{8,10},{10,12},{12... | collective-permute-start | bytes 344072 | tf_op jit(solution)/shard_map/ppermute | solution.py:739
  27.8 6.6 %collective-permute-start.2 = (bf16[112,512]{1,0:T(8,128)(2,1)S(1)}, bf16[112,512]{1,0:T(8,128)(2,1)S(1)}, u32[]{:S(2)}, u32[]{:S(2)}) collective-permute-start(bf16[112,512]{1,0:T(8,128)(2,1)S(1)} %collective-permute-done.1.refs_2_), channel_id=1, source_target_pairs={{0,2},{2,4},{4,6},{6,0},{1,3},{3,5},{5,7},{7,1},{8,10},{10,12},{12... | collective-permute-start | bytes 344072 | tf_op jit(solution)/shard_map/ppermute | solution.py:739
  41.0 408.8 %reduce-scatter.2.cloned.1.call-start = ((), (), s32[]{:S(2)}) async-start(), calls=%async_computation.2 | async-start | bytes 10321920 | tf_op jit(solution)/shard_map/reduce_scatter | solution.py:827
  41.8 7.9 %collective-permute-start.5 = (bf16[96,768]{1,0:T(8,128)(2,1)S(1)}, bf16[96,768]{1,0:T(8,128)(2,1)S(1)}, u32[]{:S(2)}, u32[]{:S(2)}) collective-permute-start(bf16[96,768]{1,0:T(8,128)(2,1)S(1)} %copy-done.9), channel_id=1, source_target_pairs={{0,2},{2,4},{4,6},{6,0},{1,3},{3,5},{5,7},{7,1},{8,10},{10,12},{12... | collective-permute-start | bytes 442376 | tf_op jit(solution)/shard_map/ppermute | solution.py:739
  44.1 15.3 %collective-permute-start.3 = (bf16[4,112,512]{2,1,0:T(8,128)(2,1)S(1)}, bf16[4,112,512]{2,1,0:T(8,128)(2,1)S(1)}, u32[]{:S(2)}, u32[]{:S(2)}) collective-permute-start(bf16[4,112,512]{2,1,0:T(8,128)(2,1)S(1)} %collect.14.refs_0_), channel_id=1, source_target_pairs={{0,16},{8,24},{16,0},{24,8},{1,17},{9,25},{17,1},{25,9},{2,18},{10... | collective-permute-start | bytes 1376264 | tf_op jit(solution)/shard_map/ppermute | solution.py:730
  45.6 27.0 %collective-permute-start.13 = (bf16[96,768]{1,0:T(8,128)(2,1)S(1)}, bf16[96,768]{1,0:T(8,128)(2,1)S(1)}, u32[]{:S(2)}, u32[]{:S(2)}) collective-permute-start(bf16[96,768]{1,0:T(8,128)(2,1)S(1)} %bitcast.114), channel_id=1, source_target_pairs={{0,2},{2,4},{4,6},{6,0},{1,3},{3,5},{5,7},{7,1},{8,10},{10,12},{12... | collective-permute-start | bytes 442376 | tf_op jit(solution)/shard_map/ppermute | solution.py:739
  49.7 8.2 %collective-permute-start.6 = (bf16[96,768]{1,0:T(8,128)(2,1)S(1)}, bf16[96,768]{1,0:T(8,128)(2,1)S(1)}, u32[]{:S(2)}, u32[]{:S(2)}) collective-permute-start(bf16[96,768]{1,0:T(8,128)(2,1)S(1)} %collective-permute-done.5.refs_1_), channel_id=1, source_target_pairs={{0,2},{2,4},{4,6},{6,0},{1,3},{3,5},{5,7},{7,1},{8,10},{10,12},{12... | collective-permute-start | bytes 442376 | tf_op jit(solution)/shard_map/ppermute | solution.py:739
  57.9 10.5 %collective-permute-start.7 = (bf16[96,768]{1,0:T(8,128)(2,1)S(1)}, bf16[96,768]{1,0:T(8,128)(2,1)S(1)}, u32[]{:S(2)}, u32[]{:S(2)}) collective-permute-start(bf16[96,768]{1,0:T(8,128)(2,1)S(1)} %collective-permute-done.6.refs_2_), channel_id=1, source_target_pairs={{0,2},{2,4},{4,6},{6,0},{1,3},{3,5},{5,7},{7,1},{8,10},{10,12},{12... | collective-permute-start | bytes 442376 | tf_op jit(solution)/shard_map/ppermute | solution.py:739
  60.0 40.6 %collective-permute-start.4 = (bf16[2,4,112,512]{3,2,1,0:T(8,128)(2,1)S(1)}, bf16[2,4,112,512]{3,2,1,0:T(8,128)(2,1)S(1)}, u32[]{:S(2)}, u32[]{:S(2)}) collective-permute-start(bf16[2,4,112,512]{3,2,1,0:T(8,128)(2,1)S(1)} %collect.15), channel_id=1, source_target_pairs={{0,8},{8,0},{16,24},{24,16},{1,9},{9,1},{17,25},{25,17},{2,10},{10... | collective-permute-start | bytes 2752520 | tf_op jit(solution)/shard_map/ppermute | solution.py:730
  69.3 17.9 %collective-permute-start.8 = (bf16[4,96,768]{2,1,0:T(8,128)(2,1)S(1)}, bf16[4,96,768]{2,1,0:T(8,128)(2,1)S(1)}, u32[]{:S(2)}, u32[]{:S(2)}) collective-permute-start(bf16[4,96,768]{2,1,0:T(8,128)(2,1)S(1)} %collect.16.refs_0_), channel_id=1, source_target_pairs={{0,16},{8,24},{16,0},{24,8},{1,17},{9,25},{17,1},{25,9},{2,18},{10... | collective-permute-start | bytes 1769480 | tf_op jit(solution)/shard_map/ppermute | solution.py:730
  72.7 14.2 %collective-permute-start.14 = (bf16[96,768]{1,0:T(8,128)(2,1)S(1)}, bf16[96,768]{1,0:T(8,128)(2,1)S(1)}, u32[]{:S(2)}, u32[]{:S(2)}) collective-permute-start(bf16[96,768]{1,0:T(8,128)(2,1)S(1)} %collective-permute-done.13.refs_1_), channel_id=1, source_target_pairs={{0,2},{2,4},{4,6},{6,0},{1,3},{3,5},{5,7},{7,1},{8,10},{10,12},{12... | collective-permute-start | bytes 442376 | tf_op jit(solution)/shard_map/ppermute | solution.py:739
  86.9 11.3 %collective-permute-start.15 = (bf16[96,768]{1,0:T(8,128)(2,1)S(1)}, bf16[96,768]{1,0:T(8,128)(2,1)S(1)}, u32[]{:S(2)}, u32[]{:S(2)}) collective-permute-start(bf16[96,768]{1,0:T(8,128)(2,1)S(1)} %collective-permute-done.14.refs_2_), channel_id=1, source_target_pairs={{0,2},{2,4},{4,6},{6,0},{1,3},{3,5},{5,7},{7,1},{8,10},{10,12},{12... | collective-permute-start | bytes 442376 | tf_op jit(solution)/shard_map/ppermute | solution.py:739
  88.4 38.4 %collective-permute-start.9 = (bf16[2,4,96,768]{3,2,1,0:T(8,128)(2,1)}, bf16[2,4,96,768]{3,2,1,0:T(8,128)(2,1)}, u32[]{:S(2)}, u32[]{:S(2)}) collective-permute-start(bf16[2,4,96,768]{3,2,1,0:T(8,128)(2,1)} %collect.17), channel_id=1, source_target_pairs={{0,8},{8,0},{16,24},{24,16},{1,9},{9,1},{17,25},{25,17},{2,10},{10... | collective-permute-start | bytes 3538952 | tf_op jit(solution)/shard_map/ppermute | solution.py:730
  99.7 24.7 %collective-permute-start.16 = (bf16[4,96,768]{2,1,0:T(8,128)(2,1)}, bf16[4,96,768]{2,1,0:T(8,128)(2,1)S(1)}, u32[]{:S(2)}, u32[]{:S(2)}) collective-permute-start(bf16[4,96,768]{2,1,0:T(8,128)(2,1)} %collect.18.refs_0_), channel_id=1, source_target_pairs={{0,16},{8,24},{16,0},{24,8},{1,17},{9,25},{17,1},{25,9},{2,18},{10... | collective-permute-start | bytes 1769480 | tf_op jit(solution)/shard_map/ppermute | solution.py:730
  111.0 24.2 %collective-permute-start.10 = (bf16[256,512]{1,0:T(8,128)(2,1)}, bf16[256,512]{1,0:T(8,128)(2,1)}, u32[]{:S(2)}, u32[]{:S(2)}) collective-permute-start(bf16[256,512]{1,0:T(8,128)(2,1)} %keys.1.refs_0_), channel_id=1, source_target_pairs={{0,2},{2,4},{4,6},{1,3},{3,5},{5,7},{8,10},{10,12},{12,14},{9,11},... | collective-permute-start | bytes 786440 | tf_op jit(solution)/shard_map/ppermute | solution.py:782
  113.0 23.1 %collective-permute-start.11 = (bf16[256,512]{1,0:T(8,128)(2,1)}, bf16[256,512]{1,0:T(8,128)(2,1)}, u32[]{:S(2)}, u32[]{:S(2)}) collective-permute-start(bf16[256,512]{1,0:T(8,128)(2,1)} %keys.1.refs_0_), channel_id=1, source_target_pairs={{0,4},{2,6},{1,5},{3,7},{8,12},{10,14},{9,13},{11,15},{16,20},{18,... | collective-permute-start | bytes 786440 | tf_op jit(solution)/shard_map/ppermute | solution.py:782
  121.7 24.2 %collective-permute-start.12 = (bf16[256,512]{1,0:T(8,128)(2,1)}, bf16[256,512]{1,0:T(8,128)(2,1)}, u32[]{:S(2)}, u32[]{:S(2)}) collective-permute-start(bf16[256,512]{1,0:T(8,128)(2,1)} %keys.1.refs_0_), channel_id=1, source_target_pairs={{0,6},{1,7},{8,14},{9,15},{16,22},{17,23},{24,30},{25,31}} | collective-permute-start | bytes 786440 | tf_op jit(solution)/shard_map/ppermute | solution.py:782
  126.7 26.7 %collective-permute-start.17 = (bf16[2,4,96,768]{3,2,1,0:T(8,128)(2,1)}, bf16[2,4,96,768]{3,2,1,0:T(8,128)(2,1)S(1)}, u32[]{:S(2)}, u32[]{:S(2)}) collective-permute-start(bf16[2,4,96,768]{3,2,1,0:T(8,128)(2,1)} %collect.19), channel_id=1, source_target_pairs={{0,8},{8,0},{16,24},{24,16},{1,9},{9,1},{17,25},{25,17},{2,10},{10... | collective-permute-start | bytes 3538952 | tf_op jit(solution)/shard_map/ppermute | solution.py:730
  161.1 15.9 %collective-permute-start.18 = (bf16[256,1536]{1,0:T(8,128)(2,1)S(1)}, bf16[256,1536]{1,0:T(8,128)(2,1)}, u32[]{:S(2)}, u32[]{:S(2)}) collective-permute-start(bf16[256,1536]{1,0:T(8,128)(2,1)S(1)} %convolution_convert_fusion), channel_id=1, source_target_pairs={{0,1},{1,0},{2,3},{3,2},{4,5},{5,4},{6,7},{7,6},{8,9},{9,8},{10,11... | collective-permute-start | bytes 2359304 | tf_op jit(solution)/shard_map/ppermute | solution.py:734
  164.1 17.3 %collective-permute-start.21 = (bf16[256,1536]{1,0:T(8,128)(2,1)S(1)}, bf16[256,1536]{1,0:T(8,128)(2,1)S(1)}, u32[]{:S(2)}, u32[]{:S(2)}) collective-permute-start(bf16[256,1536]{1,0:T(8,128)(2,1)S(1)} %bitcast.111), channel_id=1, source_target_pairs={{0,16},{8,24},{16,0},{24,8},{1,17},{9,25},{17,1},{25,9},{2,18},{10... | collective-permute-start | bytes 2359304 | tf_op jit(solution)/shard_map/ppermute | solution.py:730
  180.0 16.6 %collective-permute-start.19 = (bf16[256,1536]{1,0:T(8,128)(2,1)S(1)}, bf16[256,1536]{1,0:T(8,128)(2,1)S(1)}, u32[]{:S(2)}, u32[]{:S(2)}) collective-permute-start(bf16[256,1536]{1,0:T(8,128)(2,1)S(1)} %multiply_convert_fusion.refs_0_), channel_id=1, source_target_pairs={{0,16},{8,24},{16,0},{24,8},{1,17},{9,25},{17,1},{25,9},{2,18},{10... | collective-permute-start | bytes 2359304 | tf_op jit(solution)/shard_map/ppermute | solution.py:730
  182.9 15.3 %collective-permute-start.22 = (bf16[2,256,1536]{2,1,0:T(8,128)(2,1)}, bf16[2,256,1536]{2,1,0:T(8,128)(2,1)}, u32[]{:S(2)}, u32[]{:S(2)}) collective-permute-start(bf16[2,256,1536]{2,1,0:T(8,128)(2,1)} %collect.22), channel_id=1, source_target_pairs={{0,8},{8,0},{16,24},{24,16},{1,9},{9,1},{17,25},{25,17},{2,10},{10... | collective-permute-start | bytes 4718600 | tf_op jit(solution)/shard_map/ppermute | solution.py:730
  258.7 19.6 %collective-permute-start.27 = (bf16[256,1536]{1,0:T(8,128)(2,1)S(1)}, bf16[256,1536]{1,0:T(8,128)(2,1)S(1)}, u32[]{:S(2)}, u32[]{:S(2)}) collective-permute-start(bf16[256,1536]{1,0:T(8,128)(2,1)S(1)} %fusion.14), channel_id=1, source_target_pairs={{0,16},{8,24},{16,0},{24,8},{1,17},{9,25},{17,1},{25,9},{2,18},{10... | collective-permute-start | bytes 2359304 | tf_op jit(solution)/shard_map/ppermute | solution.py:730
  279.8 18.9 %collective-permute-start.28 = (bf16[256,1536]{1,0:T(8,128)(2,1)S(1)}, bf16[256,1536]{1,0:T(8,128)(2,1)S(1)}, u32[]{:S(2)}, u32[]{:S(2)}) collective-permute-start(bf16[256,1536]{1,0:T(8,128)(2,1)S(1)} %fusion.10), channel_id=1, source_target_pairs={{0,1},{1,0},{2,3},{3,2},{4,5},{5,4},{6,7},{7,6},{8,9},{9,8},{10,11... | collective-permute-start | bytes 2359304 | tf_op jit(solution)/shard_map/ppermute | solution.py:734
  320.2 11.1 %collective-permute-start.32 = (bf16[2,4,96,1536]{3,2,1,0:T(8,128)(2,1)}, bf16[2,4,96,1536]{3,2,1,0:T(8,128)(2,1)}, u32[]{:S(2)}, u32[]{:S(2)}) collective-permute-start(bf16[2,4,96,1536]{3,2,1,0:T(8,128)(2,1)} %get-tuple-element.76), channel_id=1, source_target_pairs={{0,8},{8,0},{16,24},{24,16},{1,9},{9,1},{17,25},{25,17},{2,10},{10... | collective-permute-start | bytes 7077896 | tf_op jit(solution)/shard_map/ppermute | solution.py:730
  322.8 4.5 collective-permute-start.29
  329.8 20.6 %collective-permute-start.30 = (bf16[256,1536]{1,0:T(8,128)(2,1)}, bf16[256,1536]{1,0:T(8,128)(2,1)S(1)}, u32[]{:S(2)}, u32[]{:S(2)}) collective-permute-start(bf16[256,1536]{1,0:T(8,128)(2,1)} %fusion.15), channel_id=1, source_target_pairs={{0,16},{8,24},{16,0},{24,8},{1,17},{9,25},{17,1},{25,9},{2,18},{10... | collective-permute-start | bytes 2359304 | tf_op jit(solution)/shard_map/ppermute | solution.py:730
  333.0 75.0 %collective-permute-start.43 = (bf16[4,96,1536]{2,1,0:T(8,128)(2,1)S(1)}, bf16[4,96,1536]{2,1,0:T(8,128)(2,1)S(1)}, u32[]{:S(2)}, u32[]{:S(2)}) collective-permute-start(bf16[4,96,1536]{2,1,0:T(8,128)(2,1)S(1)} %fusion.12.refs_3_), channel_id=1, source_target_pairs={{0,16},{8,24},{16,0},{24,8},{1,17},{9,25},{17,1},{25,9},{2,18},{10... | collective-permute-start | bytes 3538952 | tf_op jit(solution)/shard_map/ppermute | solution.py:730
  334.1 31.7 %collective-permute-start.33 = (bf16[256,512]{1,0:T(8,128)(2,1)S(1)}, bf16[256,512]{1,0:T(8,128)(2,1)S(1)}, u32[]{:S(2)}, u32[]{:S(2)}) collective-permute-start(bf16[256,512]{1,0:T(8,128)(2,1)S(1)} %get-tuple-element.97), channel_id=1, source_target_pairs={{2,0},{4,2},{6,4},{3,1},{5,3},{7,5},{10,8},{12,10},{14,12},{11,9},... | collective-permute-start | bytes 786440 | tf_op jit(solution)/shard_map/ppermute | solution.py:792
  335.6 63.9 %collective-permute-start.34 = (bf16[256,512]{1,0:T(8,128)(2,1)S(1)}, bf16[256,512]{1,0:T(8,128)(2,1)S(1)}, u32[]{:S(2)}, u32[]{:S(2)}) collective-permute-start(bf16[256,512]{1,0:T(8,128)(2,1)S(1)} %get-tuple-element.99), channel_id=1, source_target_pairs={{4,0},{6,2},{5,1},{7,3},{12,8},{14,10},{13,9},{15,11},{20,16},{22,... | collective-permute-start | bytes 786440 | tf_op jit(solution)/shard_map/ppermute | solution.py:792
  336.9 62.6 %collective-permute-start.35 = (bf16[256,512]{1,0:T(8,128)(2,1)S(1)}, bf16[256,512]{1,0:T(8,128)(2,1)S(1)}, u32[]{:S(2)}, u32[]{:S(2)}) collective-permute-start(bf16[256,512]{1,0:T(8,128)(2,1)S(1)} %get-tuple-element.98), channel_id=1, source_target_pairs={{6,0},{7,1},{14,8},{15,9},{22,16},{23,17},{30,24},{31,25}} | collective-permute-start | bytes 786440 | tf_op jit(solution)/shard_map/ppermute | solution.py:792
  351.9 76.0 %collective-permute-start.31 = (bf16[256,1536]{1,0:T(8,128)(2,1)S(1)}, bf16[256,1536]{1,0:T(8,128)(2,1)S(1)}, u32[]{:S(2)}, u32[]{:S(2)}) collective-permute-start(bf16[256,1536]{1,0:T(8,128)(2,1)S(1)} %fusion.9), channel_id=1, source_target_pairs={{0,1},{1,0},{2,3},{3,2},{4,5},{5,4},{6,7},{7,6},{8,9},{9,8},{10,11... | collective-permute-start | bytes 2359304 | tf_op jit(solution)/shard_map/ppermute | solution.py:734
  409.8 17.9 %collective-permute-start.44 = (bf16[96,1536]{1,0:T(8,128)(2,1)S(1)}, bf16[96,1536]{1,0:T(8,128)(2,1)S(1)}, u32[]{:S(2)}, u32[]{:S(2)}) collective-permute-start(bf16[96,1536]{1,0:T(8,128)(2,1)S(1)} %slice_bitcast_fusion.4), channel_id=1, source_target_pairs={{0,2},{2,4},{4,6},{6,0},{1,3},{3,5},{5,7},{7,1},{8,10},{10,12},{12... | collective-permute-start | bytes 884744 | tf_op jit(solution)/shard_map/ppermute | solution.py:739
  410.7 18.4 %collective-permute-start.38 = (bf16[4,112,512]{2,1,0:T(8,128)(2,1)S(1)}, bf16[4,112,512]{2,1,0:T(8,128)(2,1)S(1)}, u32[]{:S(2)}, u32[]{:S(2)}) collective-permute-start(bf16[4,112,512]{2,1,0:T(8,128)(2,1)S(1)} %fusion.19.refs_1_), channel_id=1, source_target_pairs={{0,16},{8,24},{16,0},{24,8},{1,17},{9,25},{17,1},{25,9},{2,18},{10... | collective-permute-start | bytes 1376264 | tf_op jit(solution)/shard_map/ppermute | solution.py:730
  412.2 26.8 %collective-permute-start.37 = (bf16[256,1536]{1,0:T(8,128)(2,1)S(1)}, bf16[256,1536]{1,0:T(8,128)(2,1)S(1)}, u32[]{:S(2)}, u32[]{:S(2)}) collective-permute-start(bf16[256,1536]{1,0:T(8,128)(2,1)S(1)} %bitcast.107), channel_id=1, source_target_pairs={{0,1},{1,0},{2,3},{3,2},{4,5},{5,4},{6,7},{7,6},{8,9},{9,8},{10,11... | collective-permute-start | bytes 2359304 | tf_op jit(solution)/shard_map/ppermute | solution.py:734
  427.8 10.8 %collective-permute-start.45 = (bf16[96,1536]{1,0:T(8,128)(2,1)S(1)}, bf16[96,1536]{1,0:T(8,128)(2,1)S(1)}, u32[]{:S(2)}, u32[]{:S(2)}) collective-permute-start(bf16[96,1536]{1,0:T(8,128)(2,1)S(1)} %fusion.18), channel_id=1, source_target_pairs={{0,2},{2,4},{4,6},{6,0},{1,3},{3,5},{5,7},{7,1},{8,10},{10,12},{12... | collective-permute-start | bytes 884744 | tf_op jit(solution)/shard_map/ppermute | solution.py:739
  438.7 10.2 %collective-permute-start.46 = (bf16[96,1536]{1,0:T(8,128)(2,1)S(1)}, bf16[96,1536]{1,0:T(8,128)(2,1)S(1)}, u32[]{:S(2)}, u32[]{:S(2)}) collective-permute-start(bf16[96,1536]{1,0:T(8,128)(2,1)S(1)} %fusion.17), channel_id=1, source_target_pairs={{0,2},{2,4},{4,6},{6,0},{1,3},{3,5},{5,7},{7,1},{8,10},{10,12},{12... | collective-permute-start | bytes 884744 | tf_op jit(solution)/shard_map/ppermute | solution.py:739
  450.1 6.5 %collective-permute-start.39 = (bf16[112,512]{1,0:T(8,128)(2,1)S(1)}, bf16[112,512]{1,0:T(8,128)(2,1)S(1)}, u32[]{:S(2)}, u32[]{:S(2)}) collective-permute-start(bf16[112,512]{1,0:T(8,128)(2,1)S(1)} %get-tuple-element.102), channel_id=1, source_target_pairs={{0,6},{2,0},{4,2},{6,4},{1,7},{3,1},{5,3},{7,5},{8,14},{10,8},{12,... | collective-permute-start | bytes 344072 | tf_op jit(solution)/shard_map/ppermute | solution.py:770
  450.1 10.0 %collective-permute-start.40 = (bf16[112,512]{1,0:T(8,128)(2,1)S(1)}, bf16[112,512]{1,0:T(8,128)(2,1)S(1)}, u32[]{:S(2)}, u32[]{:S(2)}) collective-permute-start(bf16[112,512]{1,0:T(8,128)(2,1)S(1)} %get-tuple-element.104), channel_id=1, source_target_pairs={{0,4},{2,6},{4,0},{6,2},{1,5},{3,7},{5,1},{7,3},{8,12},{10,14},{12... | collective-permute-start | bytes 344072 | tf_op jit(solution)/shard_map/ppermute | solution.py:770
  450.2 9.9 %collective-permute-start.41 = (bf16[112,512]{1,0:T(8,128)(2,1)S(1)}, bf16[112,512]{1,0:T(8,128)(2,1)S(1)}, u32[]{:S(2)}, u32[]{:S(2)}) collective-permute-start(bf16[112,512]{1,0:T(8,128)(2,1)S(1)} %get-tuple-element.103), channel_id=1, source_target_pairs={{0,2},{2,4},{4,6},{6,0},{1,3},{3,5},{5,7},{7,1},{8,10},{10,12},{12... | collective-permute-start | bytes 344072 | tf_op jit(solution)/shard_map/ppermute | solution.py:770
  452.3 12.6 %collective-permute-start.47 = (bf16[3,96,864]{2,1,0:T(8,128)(2,1)S(1)}, bf16[3,96,864]{2,1,0:T(8,128)(2,1)S(1)}, u32[]{:S(2)}, u32[]{:S(2)}) collective-permute-start(bf16[3,96,864]{2,1,0:T(8,128)(2,1)S(1)} %bitcast.124), channel_id=1, source_target_pairs={{0,8},{8,0},{16,24},{24,16},{1,9},{9,1},{17,25},{25,17},{2,10},{10... | collective-permute-start | bytes 1493000 | tf_op jit(solution)/shard_map/ppermute | solution.py:730
  452.4 14.6 %collective-permute-start.48 = (bf16[3,96,864]{2,1,0:T(8,128)(2,1)S(1)}, bf16[3,96,864]{2,1,0:T(8,128)(2,1)S(1)}, u32[]{:S(2)}, u32[]{:S(2)}) collective-permute-start(bf16[3,96,864]{2,1,0:T(8,128)(2,1)S(1)} %bitcast.123), channel_id=1, source_target_pairs={{0,16},{8,24},{16,0},{24,8},{1,17},{9,25},{17,1},{25,9},{2,18},{10... | collective-permute-start | bytes 1493000 | tf_op jit(solution)/shard_map/ppermute | solution.py:730
  456.5 20.6 %collective-permute-start.49 = (bf16[3,96,864]{2,1,0:T(8,128)(2,1)S(1)}, bf16[3,96,864]{2,1,0:T(8,128)(2,1)S(1)}, u32[]{:S(2)}, u32[]{:S(2)}) collective-permute-start(bf16[3,96,864]{2,1,0:T(8,128)(2,1)S(1)} %bitcast.122), channel_id=1, source_target_pairs={{0,24},{8,16},{16,8},{24,0},{1,25},{9,17},{17,9},{25,1},{2,26},{10... | collective-permute-start | bytes 1493000 | tf_op jit(solution)/shard_map/ppermute | solution.py:730
  (45 other events, 315.2 us)
Sparse Core Ops, SparseCore 0:
  41.1 171.7 all-gather.1
  253.9 175.3 reduce-scatter.1

commit v2 on v1

--- a/solution.py
+++ b/solution.py
@@ -601,14 +601,16 @@
             )
 
         def block(i, carry):
-            m, part = i // parts, lax.rem(i, parts)
-            column = pl.multiple_of(part * tall, tall)
-            stage[i] = contract_rows(left[m // 2, :, pl.ds(column, tall)], right[m]).astype(LOW)
-            for c in range(size):
-                write(i, c).start()
+            m, half = i // 2, lax.rem(i, 2)
+            column = pl.multiple_of(half * 2 * tall, 2 * tall)
+            both = contract_rows(left[m // 2, :, pl.ds(column, 2 * tall)], right[m]).astype(LOW)
+            for j in range(2):
+                stage[2 * i + j] = both[j * tall : (j + 1) * tall]
+                for c in range(size):
+                    write(2 * i + j, c).start()
             return carry
 
-        lax.fori_loop(0, count * parts, block, 0)
+        lax.fori_loop(0, count * parts // 2, block, 0)
 
         def drain(i, carry):
             for c in range(size):
@@ -750,7 +752,7 @@
     return slots
 
 
-def ctx_sum(terms):
+def ctx_sum(terms, later=()):
     size = lax.axis_size("ctx")
     if size > LINE:
         return lax.psum_scatter(terms, "ctx", scatter_dimension=0, tiled=False).astype(jnp.float32)
@@ -758,6 +760,8 @@
     for step in range(1, size):
         total = turn(moving).astype(jnp.float32) + terms[(step + 1) % size].astype(jnp.float32)
         moving = total.astype(LOW)
+        if later and step == 1:
+            moving = collect([moving], later)[0]
     return total
 
 
@@ -815,11 +819,11 @@
     return pair_sum(*chip_sum(keep, send))
 
 
-def gather_all(where, slots, share, later=()):
+def gather_all(where, slots, share, later=(), pieces=1):
     own = collect(slots, later)
     across = flip(own, 2)
     both = flip(collect([own, across]), 1)
-    return arrange(where, [own, both, across], share, 1), across
+    return arrange(where, [own, both, across], share, pieces), across
 
 
 def scatter_hidden(terms):
@@ -871,14 +875,14 @@
         [part[0]] + [flip(part[bit], bit) for bit in range(1, parts)] for part in split
     ]
     kv_slots = ctx_slots(kv_block)
-    query_slots = ctx_slots(w_query)
-    output_slots = ctx_slots(w_output.T)
+    head_slots = ctx_slots(jnp.concatenate([w_query, w_output.T], axis=1))
     (full_kv, gain_rows), kv_across = gather_all(where, kv_slots, share)
-    (full_query,), query_across = gather_all(where, query_slots, share, [kv_across])
-    (full_output,), output_across = gather_all(where, output_slots, share, [query_across])
+    (full_query, full_output), output_across = gather_all(
+        where, head_slots, share, [kv_across], 2
+    )
     weights = []
     for chunk in traded:
-        block = collect(chunk, [kv_slots[-1]])
+        block = collect(chunk, [kv_slots[-1], head_slots[2]])
         weights.append(
             lax.all_gather(
                 block.reshape(-1, block.shape[-1]), "ctx", axis=0, tiled=True
@@ -935,11 +939,9 @@
     near, far = chip_sum(
         *head_grads(where, [normed, grad_hidden_low], [grad_query_low, mixed_low])
     )
-    heads_sum = ctx_sum(pair_sum(near, far).astype(LOW))
+    heads_terms = pair_sum(near, far).astype(LOW)
     moved = collect(key_terms[1:], [far])
     own_terms, _ = back_sum([key_terms[0]] + [moved[i] for i in range(size - 1)])
-    grad_query = heads_sum[:, :width]
-    grad_output = heads_sum[:, width:].T
     feed_part = group_sum(keep_out, collect([send_out], [grad_hidden_low])[0]).astype(LOW)
     feed = feed_part.astype(jnp.float32) + swap(feed_part).astype(jnp.float32)
     result = (hidden + feed).astype(LOW)[None]
@@ -964,6 +966,9 @@
     )
     kv_sum = pair_sum(near, far).astype(LOW)
     own_kv = ctx_sum_direct(collect([kv_sum], [hidden_sum])[0])
+    heads_sum = ctx_sum(heads_terms, [hidden_sum])
+    grad_query = heads_sum[:, :width]
+    grad_output = heads_sum[:, width:].T
     grad_key = own_kv[:share, :kv_width]
     grad_value = own_kv[:share, kv_width:]
     normed_low = collect([normed_low], [far])[0]

time: 495 us -> 474 us (0.958)
  waiting for transfers between devices: 267 us -> 255 us
  Pallas kernels: 110 us -> 102 us
    ppermute x12 -> x9, waiting for transfers between devices: 90.8 us -> 38.9 us  [turn(): return lax.ppermute(part, 'ctx', [(i, (i + 1) % size) for i in range(size)])]
    ppermute x24 -> x22, waiting for transfers between devices: 71.6 us -> 94.8 us  [flip(): return lax.ppermute(part, 'fsdp', [(i, i ^ bit) for i in range(size)])]
    ppermute x3, waiting for transfers between devices: 10.8 us -> 19.7 us  [back_slots(): lax.ppermute(part, 'ctx', [(i, i + step) for i in range(size - step)])]
    ppermute x5, waiting for transfers between devices: 30.9 us -> 37 us  [swap(): return lax.ppermute(part, 'tp', [(0, 1), (1, 0)])]
    ppermute x3, starting transfers between devices: 2.07 us -> 8.08 us  [ctx_sum_direct(): lax.ppermute(terms[step], 'ctx', [(i, (i - step) % size) for i in range(s...]
    pallas_call x3 -> x2, Pallas kernels: 13.6 us -> 9.93 us  [arrange(): pl.pallas_call(kernel, out_shape=tuple(shapes), in_specs=[SMEM] + [ANY] *...]
    pallas_call x14 -> x13, Pallas kernels: 17.6 us -> 14.8 us  [collect(): pl.pallas_call(kernel, out_shape=shaped((count,) + parts[0].shape, parts[...]
    ppermute x24 -> x22, starting transfers between devices: 17.1 us -> 16.1 us  [flip(): return lax.ppermute(part, 'fsdp', [(i, i ^ bit) for i in range(size)])]
  transfers between devices with their start and end apart: 52 -> 47, of which waited for: 32 -> 26; matrix products, arithmetic and copies ran while one was open for 7% -> 7% of each run, Pallas kernels for 12% -> 13%
where the time goes in v2:
time: 474 us; the launch traced here: 468 us
  waiting for transfers between devices  255 us (54%)
  Pallas kernels  102 us (22%)
  starting transfers between devices  52.4 us (11%)
  other arithmetic  24.1 us (5%)
  between operations  15.3 us (3%)
  local copies, waits for them, and re-layouts  11.5 us (2%)
  matrix products  8.26 us (2%)
    ppermute x22, waiting for transfers between devices, flip(): return lax.ppermute(part, 'fsdp', [(i, i ^ bit) for i in range(size)])  94.8 us
    ppermute x3, waiting for transfers between devices, back_sum(): lax.ppermute(terms[step], 'ctx', [(i, i - step) for i in range(step, size)])  44.8 us
    ppermute x9, waiting for transfers between devices, turn(): return lax.ppermute(part, 'ctx', [(i, (i + 1) % size) for i in range(size)])  38.9 us
    pallas_call x1, Pallas kernels, ffn(): pl.pallas_call(kernel, out_shape=(shaped((2, rows, model)),) * 4 + (shape...  38.7 us
    ppermute x5, waiting for transfers between devices, swap(): return lax.ppermute(part, 'tp', [(0, 1), (1, 0)])  37 us
    ppermute x3, waiting for transfers between devices, back_slots(): lax.ppermute(part, 'ctx', [(i, i + step) for i in range(size - step)])  19.7 us
    ppermute x22, starting transfers between devices, flip(): return lax.ppermute(part, 'fsdp', [(i, i ^ bit) for i in range(size)])  16.1 us
    pallas_call x13, Pallas kernels, collect(): pl.pallas_call(kernel, out_shape=shaped((count,) + parts[0].shape, parts[...  14.8 us
  transfers between devices with their start and end apart: 47, of which 26 were waited for; matrix products, arithmetic and copies ran while one was open for 7% of the time, Pallas kernels for 13%

profile of v2, /device:TPU:0, one launch (start us, length us, event | category | flops | bytes accessed | tf_op | source)
XLA Modules:
  0.0 468.4 jit_solution(3887219887130595147)
XLA Ops:
  8.2 3.1 collective-permute-start.5
  11.4 3.1 split_columns.1
  18.1 2.2 collective-permute-done.5.refs_1_
  20.3 3.4 collective-permute-done.refs_1_
  24.1 8.7 %collective-permute-done.1.refs_2_ = bf16[112,512]{1,0:T(8,128)(2,1)S(1)} collective-permute-done((bf16[112,512]{1,0:T(8,128)(2,1)S(1)}, bf16[112,512]{1,0:T(8,128)(2,1)S(1)}, u32[]{:S(2)}, u32[]{:S(2)}) %collective-permute-start.1) | collective-permute-done | bytes 114720 | tf_op jit(solution)/shard_map/ppermute | solution.py:741
  32.8 6.6 %collective-permute-done.2.refs_3_.refs_4_ = bf16[112,512]{1,0:T(8,128)(2,1)S(1)} collective-permute-done((bf16[112,512]{1,0:T(8,128)(2,1)S(1)}, bf16[112,512]{1,0:T(8,128)(2,1)S(1)}, u32[]{:S(2)}, u32[]{:S(2)}) %collective-permute-start.2) | collective-permute-done | bytes 114720 | tf_op jit(solution)/shard_map/ppermute | solution.py:741
  40.2 3.4 collect.20
  47.4 9.6 %collective-permute-done.3.refs_1_.refs_2_.refs_4_ = bf16[4,112,512]{2,1,0:T(8,128)(2,1)S(1)} collective-permute-done((bf16[4,112,512]{2,1,0:T(8,128)(2,1)S(1)}, bf16[4,112,512]{2,1,0:T(8,128)(2,1)S(1)}, u32[]{:S(2)}, u32[]{:S(2)}) %collective-permute-start.3) | collective-permute-done | bytes 458784 | tf_op jit(solution)/shard_map/ppermute | solution.py:732
  62.4 23.5 %collective-permute-done.8.refs_1_.refs_2_ = bf16[4,96,1536]{2,1,0:T(8,128)(2,1)} collective-permute-done((bf16[4,96,1536]{2,1,0:T(8,128)(2,1)}, bf16[4,96,1536]{2,1,0:T(8,128)(2,1)}, u32[]{:S(2)}, u32[]{:S(2)}) %collective-permute-start.8) | collective-permute-done | bytes 1179680 | tf_op jit(solution)/shard_map/ppermute | solution.py:732
  85.9 2.9 collect.16
  91.2 4.4 arrange.2
  98.8 3.5 collective-permute-start.10
  102.3 3.7 collective-permute-start.11
  106.1 2.0 collective-permute-start.12
  108.3 5.5 %arrange.3 = (bf16[1536,768]{1,0:T(8,128)(2,1)}, bf16[1536,768]{1,0:T(8,128)(2,1)}) custom-call(s32[6]{0:T(128)S(1)} %pad_add_fusion.where_ref, bf16[4,96,1536]{2,1,0:T(8,128)(2,1)S(1)} %copy-done.2, bf16[2,4,96,1536]{3,2,1,0:T(8,128)(2,1)} %collective-permute-done.9.refs_1_, bf16[4,96,1536]{2,1,0:T(8,128)(2,1)} %collective-permute-done.8.refs_1_.refs_2_), custom_call_target="tpu_custom_call" | custom-call | flops 1800000000 | bytes 2000000 | tf_op jit(solution)/shard_map/arrange/pallas_call | solution.py:493
  113.8 3.3 fusion.37.q_ref
  117.1 8.7 %collective-permute-done.11.refs_2_ = bf16[256,512]{1,0:T(8,128)(2,1)} collective-permute-done((bf16[256,512]{1,0:T(8,128)(2,1)S(1)}, bf16[256,512]{1,0:T(8,128)(2,1)}, u32[]{:S(2)}, u32[]{:S(2)}) %collective-permute-start.11) | collective-permute-done | bytes 262176 | tf_op jit(solution)/shard_map/ppermute | solution.py:786
  125.8 11.0 %collective-permute-done.12.refs_3_ = bf16[256,512]{1,0:T(8,128)(2,1)} collective-permute-done((bf16[256,512]{1,0:T(8,128)(2,1)S(1)}, bf16[256,512]{1,0:T(8,128)(2,1)}, u32[]{:S(2)}, u32[]{:S(2)}) %collective-permute-start.12) | collective-permute-done | bytes 262176 | tf_op jit(solution)/shard_map/ppermute | solution.py:786
  136.8 6.7 %attend.1 = (bf16[256,768]{1,0:T(8,128)(2,1)S(1)}, bf16[256,768]{1,0:T(8,128)(2,1)}, f32[4,128,768]{2,1,0:T(8,128)}) custom-call(s32[6]{0:T(128)S(1)} %pad_add_fusion.where_ref, s32[2]{0:T(128)S(1)} %bitcast.111, f32[256,768]{1,0:T(8,128)} %fusion.37.q_ref, bf16[256,512]{1,0:T(8,128)(2,1)S(1)} %keys.1.refs_0_, ...), custom_call_target="tpu_custom_call" | custom-call | flops 12600000512 | bytes 14000000 | tf_op jit(solution)/shard_map/attend/pallas_call | solution.py:272
  143.5 2.8 convolution_convert_fusion
  149.5 16.0 %collective-permute-done.13 = bf16[256,1536]{1,0:T(8,128)(2,1)} collective-permute-done((bf16[256,1536]{1,0:T(8,128)(2,1)}, bf16[256,1536]{1,0:T(8,128)(2,1)}, u32[]{:S(2)}, u32[]{:S(2)}) %collective-permute-start.13) | collective-permute-done | bytes 786464 | tf_op jit(solution)/shard_map/ppermute | solution.py:736
  165.5 1.8 multiply_reduce_fusion.2
  171.7 15.0 %collective-permute-done.14.refs_1_.refs_2_ = bf16[256,1536]{1,0:T(8,128)(2,1)S(1)} collective-permute-done((bf16[256,1536]{1,0:T(8,128)(2,1)S(1)}, bf16[256,1536]{1,0:T(8,128)(2,1)S(1)}, u32[]{:S(2)}, u32[]{:S(2)}) %collective-permute-start.14) | collective-permute-done | bytes 786464 | tf_op jit(solution)/shard_map/ppermute | solution.py:732
  188.3 3.7 collective-permute-done.15.refs_1_
  192.0 12.0 %all-gather.2.cloned.1.call-done = bf16[4608,864]{1,0:T(8,128)(2,1)} async-done(((bf16[1152,864]{1,0:T(8,128)(2,1)}), bf16[4608,864]{1,0:T(8,128)(2,1)}) %all-gather.2.cloned.1.call-update) | async-done | bytes 7962640 | tf_op jit(solution)/shard_map/all_gather | solution.py:887
  205.2 38.7 %ffn.1 = (bf16[2,256,1536]{2,1,0:T(8,128)(2,1)}, bf16[2,256,1536]{2,1,0:T(8,128)(2,1)}, bf16[2,256,1536]{2,1,0:T(8,128)(2,1)}, bf16[2,256,1536]{2,1,0:T(8,128)(2,1)}, bf16[4,4,3,96,864]{4,3,2,1,0:T(8,128)(2,1)}) custom-call(s32[6]{0:T(128)S(1)} %pad_add_fusion.where_ref, bf16[256,1536]{1,0:T(8,128)(2,1)S(1)} %multiply_convert_fusion.refs_0_, ...), custom_call_target="tpu_custom_call" | custom-call | flops 33300000768 | bytes 37000000 | tf_op jit(solution)/shard_map/ffn/pallas_call | solution.py:628
  244.0 3.7 collective-permute-done.21
  251.1 17.9 %collective-permute-done.22 = bf16[256,1536]{1,0:T(8,128)(2,1)S(1)} collective-permute-done((bf16[256,1536]{1,0:T(8,128)(2,1)S(1)}, bf16[256,1536]{1,0:T(8,128)(2,1)S(1)}, u32[]{:S(2)}, u32[]{:S(2)}) %collective-permute-start.22) | collective-permute-done | bytes 786464 | tf_op jit(solution)/shard_map/ppermute | solution.py:732
  272.1 17.2 %collective-permute-done.23 = bf16[256,1536]{1,0:T(8,128)(2,1)S(1)} collective-permute-done((bf16[256,1536]{1,0:T(8,128)(2,1)S(1)}, bf16[256,1536]{1,0:T(8,128)(2,1)S(1)}, u32[]{:S(2)}, u32[]{:S(2)}) %collective-permute-start.23) | collective-permute-done | bytes 786464 | tf_op jit(solution)/shard_map/ppermute | solution.py:736
  293.5 10.3 %attend_back.1 = (bf16[256,768]{1,0:T(8,128)(2,1)}, bf16[256,512]{1,0:T(8,128)(2,1)S(1)}, bf16[256,512]{1,0:T(8,128)(2,1)S(1)}, bf16[256,512]{1,0:T(8,128)(2,1)S...) custom-call(s32[6]{0:T(128)S(1)} %pad_add_fusion.where_ref, s32[2]{0:T(128)S(1)} %bitcast.112, ...), custom_call_target="tpu_custom_call" | custom-call | flops 15299999744 | bytes 17000000 | tf_op jit(solution)/shard_map/attend_back/pallas_call | solution.py:297
  304.7 5.7 %head_grads.2 = (bf16[2,4,96,1536]{3,2,1,0:T(8,128)(2,1)}, bf16[2,4,96,1536]{3,2,1,0:T(8,128)(2,1)}) custom-call(s32[6]{0:T(128)S(1)} %pad_add_fusion.where_ref, bf16[256,1536]{1,0:T(8,128)(2,1)S(1)} %fusion.3.refs_0_, bf16[256,1536]{1,0:T(8,128)(2,1)} %copy-done, bf16[256,768]{1,0:T(8,128)(2,1)S(1)} %copy-done.12, bf16[256,768]{1,0:T(8,128)(2,1)S(1)} %copy-done.11), custom_call_target="tpu_custom_call" | custom-call | flops 2700000000 | bytes 3000000 | tf_op jit(solution)/shard_map/head_grads/pallas_call | solution.py:715
  310.6 2.6 collect.21
  313.9 3.8 collective-permute-done.24
  317.7 2.4 fusion.15
  328.7 12.0 %collective-permute-done.25 = bf16[256,1536]{1,0:T(8,128)(2,1)S(1)} collective-permute-done((bf16[256,1536]{1,0:T(8,128)(2,1)}, bf16[256,1536]{1,0:T(8,128)(2,1)S(1)}, u32[]{:S(2)}, u32[]{:S(2)}) %collective-permute-start.25) | collective-permute-done | bytes 786464 | tf_op jit(solution)/shard_map/ppermute | solution.py:732
  343.9 11.9 %collective-permute-done.28 = bf16[256,512]{1,0:T(8,128)(2,1)S(1)} collective-permute-done((bf16[256,512]{1,0:T(8,128)(2,1)S(1)}, bf16[256,512]{1,0:T(8,128)(2,1)S(1)}, u32[]{:S(2)}, u32[]{:S(2)}) %collective-permute-start.28) | collective-permute-done | bytes 262176 | tf_op jit(solution)/shard_map/ppermute | solution.py:796
  355.8 32.9 %collective-permute-done.29 = bf16[256,512]{1,0:T(8,128)(2,1)S(1)} collective-permute-done((bf16[256,512]{1,0:T(8,128)(2,1)S(1)}, bf16[256,512]{1,0:T(8,128)(2,1)S(1)}, u32[]{:S(2)}, u32[]{:S(2)}) %collective-permute-start.29) | collective-permute-done | bytes 262176 | tf_op jit(solution)/shard_map/ppermute | solution.py:796
  389.8 3.6 normed_back.1
  393.4 4.1 head_grads.3
  397.6 1.8 fusion
  404.3 13.1 %collective-permute-done.39 = bf16[96,1536]{1,0:T(8,128)(2,1)S(1)} collective-permute-done((bf16[96,1536]{1,0:T(8,128)(2,1)S(1)}, bf16[96,1536]{1,0:T(8,128)(2,1)S(1)}, u32[]{:S(2)}, u32[]{:S(2)}) %collective-permute-start.39) | collective-permute-done | bytes 294944 | tf_op jit(solution)/shard_map/ppermute | solution.py:741
  417.7 2.4 collective-permute-done.32
  422.6 3.2 collective-permute-start.34
  425.8 4.8 %collective-permute-start.35 = (bf16[112,512]{1,0:T(8,128)(2,1)S(1)}, bf16[112,512]{1,0:T(8,128)(2,1)S(1)}, u32[]{:S(2)}, u32[]{:S(2)}) collective-permute-start(bf16[112,512]{1,0:T(8,128)(2,1)S(1)} %get-tuple-element.108), channel_id=1, source_target_pairs={{0,4},{2,6},{4,0},{6,2},{1,5},{3,7},{5,1},{7,3},{8,12},{10,14},{12... | collective-permute-start | bytes 344072 | tf_op jit(solution)/shard_map/ppermute | solution.py:774
  432.9 8.0 %collective-permute-done.35 = bf16[112,512]{1,0:T(8,128)(2,1)S(1)} collective-permute-done((bf16[112,512]{1,0:T(8,128)(2,1)S(1)}, bf16[112,512]{1,0:T(8,128)(2,1)S(1)}, u32[]{:S(2)}, u32[]{:S(2)}) %collective-permute-start.35) | collective-permute-done | bytes 114720 | tf_op jit(solution)/shard_map/ppermute | solution.py:774
  445.7 5.0 %collective-permute-done.40 = bf16[96,1536]{1,0:T(8,128)(2,1)S(1)} collective-permute-done((bf16[96,1536]{1,0:T(8,128)(2,1)S(1)}, bf16[96,1536]{1,0:T(8,128)(2,1)S(1)}, u32[]{:S(2)}, u32[]{:S(2)}) %collective-permute-start.40) | collective-permute-done | bytes 294944 | tf_op jit(solution)/shard_map/ppermute | solution.py:741
  450.8 4.9 %collective-permute-done.44.refs_3_ = bf16[3,96,864]{2,1,0:T(8,128)(2,1)S(1)} collective-permute-done((bf16[3,96,864]{2,1,0:T(8,128)(2,1)S(1)}, bf16[3,96,864]{2,1,0:T(8,128)(2,1)S(1)}, u32[]{:S(2)}, u32[]{:S(2)}) %collective-permute-start.44) | collective-permute-done | bytes 497696 | tf_op jit(solution)/shard_map/ppermute | solution.py:732
  456.5 3.7 join_columns.1
  (217 shorter events, 72.6 us)
Async XLA Ops:
  7.2 196.9 %all-gather.2.cloned.1.call-start = ((), (), s32[]{:S(2)}) async-start(), calls=%async_computation.1 | async-start | bytes 10321920 | tf_op jit(solution)/shard_map/all_gather | solution.py:887
  8.2 12.1 %collective-permute-start.5 = (bf16[96,1536]{1,0:T(8,128)(2,1)S(1)}, bf16[96,1536]{1,0:T(8,128)(2,1)S(1)}, u32[]{:S(2)}, u32[]{:S(2)}) collective-permute-start(bf16[96,1536]{1,0:T(8,128)(2,1)S(1)} %pad_maximum_fusion.refs_0_), channel_id=1, source_target_pairs={{0,2},{2,4},{4,6},{6,0},{1,3},{3,5},{5,7},{7,1},{8,10},{10,12},{12... | collective-permute-start | bytes 884744 | tf_op jit(solution)/shard_map/ppermute | solution.py:741
  14.5 24.9 %collective-permute-start.18 = (bf16[3,96,864]{2,1,0:T(8,128)(2,1)S(1)}, bf16[3,96,864]{2,1,0:T(8,128)(2,1)S(1)}, u32[]{:S(2)}, u32[]{:S(2)}) collective-permute-start(bf16[3,96,864]{2,1,0:T(8,128)(2,1)S(1)} %get-tuple-element.64), channel_id=1, source_target_pairs={{0,8},{8,0},{16,24},{24,16},{1,9},{9,1},{17,25},{25,17},{2,10},{10... | collective-permute-start | bytes 1493000 | tf_op jit(solution)/shard_map/ppermute | solution.py:732
  14.5 24.9 %collective-permute-start.19 = (bf16[3,96,864]{2,1,0:T(8,128)(2,1)S(1)}, bf16[3,96,864]{2,1,0:T(8,128)(2,1)S(1)}, u32[]{:S(2)}, u32[]{:S(2)}) collective-permute-start(bf16[3,96,864]{2,1,0:T(8,128)(2,1)S(1)} %get-tuple-element.65), channel_id=1, source_target_pairs={{0,16},{8,24},{16,0},{24,8},{1,17},{9,25},{17,1},{25,9},{2,18},{10... | collective-permute-start | bytes 1493000 | tf_op jit(solution)/shard_map/ppermute | solution.py:732
  16.0 23.4 %collective-permute-start.20 = (bf16[3,96,864]{2,1,0:T(8,128)(2,1)}, bf16[3,96,864]{2,1,0:T(8,128)(2,1)S(1)}, u32[]{:S(2)}, u32[]{:S(2)}) collective-permute-start(bf16[3,96,864]{2,1,0:T(8,128)(2,1)} %get-tuple-element.66), channel_id=1, source_target_pairs={{0,24},{8,16},{16,8},{24,0},{1,25},{9,17},{17,9},{25,1},{2,26},{10... | collective-permute-start | bytes 1493000 | tf_op jit(solution)/shard_map/ppermute | solution.py:732
  16.5 7.2 %collective-permute-start = (bf16[112,512]{1,0:T(8,128)(2,1)S(1)}, bf16[112,512]{1,0:T(8,128)(2,1)S(1)}, u32[]{:S(2)}, u32[]{:S(2)}) collective-permute-start(bf16[112,512]{1,0:T(8,128)(2,1)S(1)} %fusion.23.refs_0_), channel_id=1, source_target_pairs={{0,2},{2,4},{4,6},{6,0},{1,3},{3,5},{5,7},{7,1},{8,10},{10,12},{12... | collective-permute-start | bytes 344072 | tf_op jit(solution)/shard_map/ppermute | solution.py:741
  20.3 19.1 %collective-permute-start.6 = (bf16[96,1536]{1,0:T(8,128)(2,1)S(1)}, bf16[96,1536]{1,0:T(8,128)(2,1)S(1)}, u32[]{:S(2)}, u32[]{:S(2)}) collective-permute-start(bf16[96,1536]{1,0:T(8,128)(2,1)S(1)} %collective-permute-done.5.refs_1_), channel_id=1, source_target_pairs={{0,2},{2,4},{4,6},{6,0},{1,3},{3,5},{5,7},{7,1},{8,10},{10,12},{12... | collective-permute-start | bytes 884744 | tf_op jit(solution)/shard_map/ppermute | solution.py:741
  23.7 9.1 %collective-permute-start.1 = (bf16[112,512]{1,0:T(8,128)(2,1)S(1)}, bf16[112,512]{1,0:T(8,128)(2,1)S(1)}, u32[]{:S(2)}, u32[]{:S(2)}) collective-permute-start(bf16[112,512]{1,0:T(8,128)(2,1)S(1)} %collective-permute-done.refs_1_), channel_id=1, source_target_pairs={{0,2},{2,4},{4,6},{6,0},{1,3},{3,5},{5,7},{7,1},{8,10},{10,12},{12... | collective-permute-start | bytes 344072 | tf_op jit(solution)/shard_map/ppermute | solution.py:741
  32.8 6.6 %collective-permute-start.2 = (bf16[112,512]{1,0:T(8,128)(2,1)S(1)}, bf16[112,512]{1,0:T(8,128)(2,1)S(1)}, u32[]{:S(2)}, u32[]{:S(2)}) collective-permute-start(bf16[112,512]{1,0:T(8,128)(2,1)S(1)} %collective-permute-done.1.refs_2_), channel_id=1, source_target_pairs={{0,2},{2,4},{4,6},{6,0},{1,3},{3,5},{5,7},{7,1},{8,10},{10,12},{12... | collective-permute-start | bytes 344072 | tf_op jit(solution)/shard_map/ppermute | solution.py:741
  43.7 378.6 %reduce-scatter.2.cloned.1.call-start = ((), (), s32[]{:S(2)}) async-start(), calls=%async_computation.2 | async-start | bytes 10321920 | tf_op jit(solution)/shard_map/reduce_scatter | solution.py:831
  44.4 12.7 %collective-permute-start.3 = (bf16[4,112,512]{2,1,0:T(8,128)(2,1)S(1)}, bf16[4,112,512]{2,1,0:T(8,128)(2,1)S(1)}, u32[]{:S(2)}, u32[]{:S(2)}) collective-permute-start(bf16[4,112,512]{2,1,0:T(8,128)(2,1)S(1)} %collect.13.refs_0_), channel_id=1, source_target_pairs={{0,16},{8,24},{16,0},{24,8},{1,17},{9,25},{17,1},{25,9},{2,18},{10... | collective-permute-start | bytes 1376264 | tf_op jit(solution)/shard_map/ppermute | solution.py:732
  45.9 11.2 %collective-permute-start.7 = (bf16[96,1536]{1,0:T(8,128)(2,1)S(1)}, bf16[96,1536]{1,0:T(8,128)(2,1)S(1)}, u32[]{:S(2)}, u32[]{:S(2)}) collective-permute-start(bf16[96,1536]{1,0:T(8,128)(2,1)S(1)} %collective-permute-done.6.refs_2_.refs_5_), channel_id=1, source_target_pairs={{0,2},{2,4},{4,6},{6,0},{1,3},{3,5},{5,7},{7,1},{8,10},{10,12},{12... | collective-permute-start | bytes 884744 | tf_op jit(solution)/shard_map/ppermute | solution.py:741
  58.3 27.6 %collective-permute-start.8 = (bf16[4,96,1536]{2,1,0:T(8,128)(2,1)}, bf16[4,96,1536]{2,1,0:T(8,128)(2,1)}, u32[]{:S(2)}, u32[]{:S(2)}) collective-permute-start(bf16[4,96,1536]{2,1,0:T(8,128)(2,1)} %collect.15.refs_0_), channel_id=1, source_target_pairs={{0,16},{8,24},{16,0},{24,8},{1,17},{9,25},{17,1},{25,9},{2,18},{10... | collective-permute-start | bytes 3538952 | tf_op jit(solution)/shard_map/ppermute | solution.py:732
  62.3 27.9 %collective-permute-start.4 = (bf16[2,4,112,512]{3,2,1,0:T(8,128)(2,1)S(1)}, bf16[2,4,112,512]{3,2,1,0:T(8,128)(2,1)S(1)}, u32[]{:S(2)}, u32[]{:S(2)}) collective-permute-start(bf16[2,4,112,512]{3,2,1,0:T(8,128)(2,1)S(1)} %collect.14), channel_id=1, source_target_pairs={{0,8},{8,0},{16,24},{24,16},{1,9},{9,1},{17,25},{25,17},{2,10},{10... | collective-permute-start | bytes 2752520 | tf_op jit(solution)/shard_map/ppermute | solution.py:732
  88.9 19.4 %collective-permute-start.9 = (bf16[2,4,96,1536]{3,2,1,0:T(8,128)(2,1)}, bf16[2,4,96,1536]{3,2,1,0:T(8,128)(2,1)}, u32[]{:S(2)}, u32[]{:S(2)}) collective-permute-start(bf16[2,4,96,1536]{3,2,1,0:T(8,128)(2,1)} %collect.16), channel_id=1, source_target_pairs={{0,8},{8,0},{16,24},{24,16},{1,9},{9,1},{17,25},{25,17},{2,10},{10... | collective-permute-start | bytes 7077896 | tf_op jit(solution)/shard_map/ppermute | solution.py:732
  98.8 18.3 %collective-permute-start.10 = (bf16[256,512]{1,0:T(8,128)(2,1)S(1)}, bf16[256,512]{1,0:T(8,128)(2,1)S(1)}, u32[]{:S(2)}, u32[]{:S(2)}) collective-permute-start(bf16[256,512]{1,0:T(8,128)(2,1)S(1)} %keys.1.refs_0_), channel_id=1, source_target_pairs={{0,2},{2,4},{4,6},{1,3},{3,5},{5,7},{8,10},{10,12},{12,14},{9,11},... | collective-permute-start | bytes 786440 | tf_op jit(solution)/shard_map/ppermute | solution.py:786
  102.3 23.5 %collective-permute-start.11 = (bf16[256,512]{1,0:T(8,128)(2,1)S(1)}, bf16[256,512]{1,0:T(8,128)(2,1)}, u32[]{:S(2)}, u32[]{:S(2)}) collective-permute-start(bf16[256,512]{1,0:T(8,128)(2,1)S(1)} %keys.1.refs_0_), channel_id=1, source_target_pairs={{0,4},{2,6},{1,5},{3,7},{8,12},{10,14},{9,13},{11,15},{16,20},{18,... | collective-permute-start | bytes 786440 | tf_op jit(solution)/shard_map/ppermute | solution.py:786
  106.1 30.7 %collective-permute-start.12 = (bf16[256,512]{1,0:T(8,128)(2,1)S(1)}, bf16[256,512]{1,0:T(8,128)(2,1)}, u32[]{:S(2)}, u32[]{:S(2)}) collective-permute-start(bf16[256,512]{1,0:T(8,128)(2,1)S(1)} %keys.1.refs_0_), channel_id=1, source_target_pairs={{0,6},{1,7},{8,14},{9,15},{16,22},{17,23},{24,30},{25,31}} | collective-permute-start | bytes 786440 | tf_op jit(solution)/shard_map/ppermute | solution.py:786
  146.3 19.2 %collective-permute-start.13 = (bf16[256,1536]{1,0:T(8,128)(2,1)}, bf16[256,1536]{1,0:T(8,128)(2,1)}, u32[]{:S(2)}, u32[]{:S(2)}) collective-permute-start(bf16[256,1536]{1,0:T(8,128)(2,1)} %convolution_convert_fusion), channel_id=1, source_target_pairs={{0,1},{1,0},{2,3},{3,2},{4,5},{5,4},{6,7},{7,6},{8,9},{9,8},{10,11... | collective-permute-start | bytes 2359304 | tf_op jit(solution)/shard_map/ppermute | solution.py:736
  148.0 22.3 %collective-permute-start.16 = (bf16[256,1536]{1,0:T(8,128)(2,1)S(1)}, bf16[256,1536]{1,0:T(8,128)(2,1)S(1)}, u32[]{:S(2)}, u32[]{:S(2)}) collective-permute-start(bf16[256,1536]{1,0:T(8,128)(2,1)S(1)} %bitcast.113), channel_id=1, source_target_pairs={{0,16},{8,24},{16,0},{24,8},{1,17},{9,25},{17,1},{25,9},{2,18},{10... | collective-permute-start | bytes 2359304 | tf_op jit(solution)/shard_map/ppermute | solution.py:732
  168.7 18.0 %collective-permute-start.14 = (bf16[256,1536]{1,0:T(8,128)(2,1)S(1)}, bf16[256,1536]{1,0:T(8,128)(2,1)S(1)}, u32[]{:S(2)}, u32[]{:S(2)}) collective-permute-start(bf16[256,1536]{1,0:T(8,128)(2,1)S(1)} %multiply_convert_fusion.refs_0_), channel_id=1, source_target_pairs={{0,16},{8,24},{16,0},{24,8},{1,17},{9,25},{17,1},{25,9},{2,18},{10... | collective-permute-start | bytes 2359304 | tf_op jit(solution)/shard_map/ppermute | solution.py:732
  171.7 16.6 %collective-permute-start.17 = (bf16[2,256,1536]{2,1,0:T(8,128)(2,1)}, bf16[2,256,1536]{2,1,0:T(8,128)(2,1)}, u32[]{:S(2)}, u32[]{:S(2)}) collective-permute-start(bf16[2,256,1536]{2,1,0:T(8,128)(2,1)} %collect.19), channel_id=1, source_target_pairs={{0,8},{8,0},{16,24},{24,16},{1,9},{9,1},{17,25},{25,17},{2,10},{10... | collective-permute-start | bytes 4718600 | tf_op jit(solution)/shard_map/ppermute | solution.py:732
  188.2 3.8 collective-permute-start.15
  243.9 3.8 collective-permute-start.21
  249.3 40.0 %copy-start.16 = (f32[256,1536]{1,0:T(8,128)S(1)}, f32[256,1536]{1,0:T(8,128)}, u32[]{:S(2)}) copy-start(f32[256,1536]{1,0:T(8,128)} %copy-done.15) | copy-start | bytes 4718596
  249.3 19.6 %collective-permute-start.22 = (bf16[256,1536]{1,0:T(8,128)(2,1)S(1)}, bf16[256,1536]{1,0:T(8,128)(2,1)S(1)}, u32[]{:S(2)}, u32[]{:S(2)}) collective-permute-start(bf16[256,1536]{1,0:T(8,128)(2,1)S(1)} %fusion.14), channel_id=1, source_target_pairs={{0,16},{8,24},{16,0},{24,8},{1,17},{9,25},{17,1},{25,9},{2,18},{10... | collective-permute-start | bytes 2359304 | tf_op jit(solution)/shard_map/ppermute | solution.py:732
  270.4 18.9 %collective-permute-start.23 = (bf16[256,1536]{1,0:T(8,128)(2,1)S(1)}, bf16[256,1536]{1,0:T(8,128)(2,1)S(1)}, u32[]{:S(2)}, u32[]{:S(2)}) collective-permute-start(bf16[256,1536]{1,0:T(8,128)(2,1)S(1)} %fusion.10), channel_id=1, source_target_pairs={{0,1},{1,0},{2,3},{3,2},{4,5},{5,4},{6,7},{7,6},{8,9},{9,8},{10,11... | collective-permute-start | bytes 2359304 | tf_op jit(solution)/shard_map/ppermute | solution.py:736
  310.5 11.3 %collective-permute-start.27 = (bf16[2,4,96,1536]{3,2,1,0:T(8,128)(2,1)}, bf16[2,4,96,1536]{3,2,1,0:T(8,128)(2,1)}, u32[]{:S(2)}, u32[]{:S(2)}) collective-permute-start(bf16[2,4,96,1536]{3,2,1,0:T(8,128)(2,1)} %get-tuple-element.80), channel_id=1, source_target_pairs={{0,8},{8,0},{16,24},{24,16},{1,9},{9,1},{17,25},{25,17},{2,10},{10... | collective-permute-start | bytes 7077896 | tf_op jit(solution)/shard_map/ppermute | solution.py:732
  313.2 4.5 collective-permute-start.24
  320.1 20.6 %collective-permute-start.25 = (bf16[256,1536]{1,0:T(8,128)(2,1)}, bf16[256,1536]{1,0:T(8,128)(2,1)S(1)}, u32[]{:S(2)}, u32[]{:S(2)}) collective-permute-start(bf16[256,1536]{1,0:T(8,128)(2,1)} %fusion.15), channel_id=1, source_target_pairs={{0,16},{8,24},{16,0},{24,8},{1,17},{9,25},{17,1},{25,9},{2,18},{10... | collective-permute-start | bytes 2359304 | tf_op jit(solution)/shard_map/ppermute | solution.py:732
  323.5 74.1 %collective-permute-start.38 = (bf16[4,96,1536]{2,1,0:T(8,128)(2,1)S(1)}, bf16[4,96,1536]{2,1,0:T(8,128)(2,1)S(1)}, u32[]{:S(2)}, u32[]{:S(2)}) collective-permute-start(bf16[4,96,1536]{2,1,0:T(8,128)(2,1)S(1)} %fusion.12.refs_3_), channel_id=1, source_target_pairs={{0,16},{8,24},{16,0},{24,8},{1,17},{9,25},{17,1},{25,9},{2,18},{10... | collective-permute-start | bytes 3538952 | tf_op jit(solution)/shard_map/ppermute | solution.py:732
  324.7 31.1 %collective-permute-start.28 = (bf16[256,512]{1,0:T(8,128)(2,1)S(1)}, bf16[256,512]{1,0:T(8,128)(2,1)S(1)}, u32[]{:S(2)}, u32[]{:S(2)}) collective-permute-start(bf16[256,512]{1,0:T(8,128)(2,1)S(1)} %get-tuple-element.101), channel_id=1, source_target_pairs={{2,0},{4,2},{6,4},{3,1},{5,3},{7,5},{10,8},{12,10},{14,12},{11,9},... | collective-permute-start | bytes 786440 | tf_op jit(solution)/shard_map/ppermute | solution.py:796
  326.1 62.6 %collective-permute-start.29 = (bf16[256,512]{1,0:T(8,128)(2,1)S(1)}, bf16[256,512]{1,0:T(8,128)(2,1)S(1)}, u32[]{:S(2)}, u32[]{:S(2)}) collective-permute-start(bf16[256,512]{1,0:T(8,128)(2,1)S(1)} %get-tuple-element.103), channel_id=1, source_target_pairs={{4,0},{6,2},{5,1},{7,3},{12,8},{14,10},{13,9},{15,11},{20,16},{22,... | collective-permute-start | bytes 786440 | tf_op jit(solution)/shard_map/ppermute | solution.py:796
  327.4 61.3 %collective-permute-start.30 = (bf16[256,512]{1,0:T(8,128)(2,1)S(1)}, bf16[256,512]{1,0:T(8,128)(2,1)S(1)}, u32[]{:S(2)}, u32[]{:S(2)}) collective-permute-start(bf16[256,512]{1,0:T(8,128)(2,1)S(1)} %get-tuple-element.102), channel_id=1, source_target_pairs={{6,0},{7,1},{14,8},{15,9},{22,16},{23,17},{30,24},{31,25}} | collective-permute-start | bytes 786440 | tf_op jit(solution)/shard_map/ppermute | solution.py:796
  342.2 59.8 %collective-permute-start.26 = (bf16[256,1536]{1,0:T(8,128)(2,1)S(1)}, bf16[256,1536]{1,0:T(8,128)(2,1)S(1)}, u32[]{:S(2)}, u32[]{:S(2)}) collective-permute-start(bf16[256,1536]{1,0:T(8,128)(2,1)S(1)} %fusion.9), channel_id=1, source_target_pairs={{0,1},{1,0},{2,3},{3,2},{4,5},{5,4},{6,7},{7,6},{8,9},{9,8},{10,11... | collective-permute-start | bytes 2359304 | tf_op jit(solution)/shard_map/ppermute | solution.py:736
  397.5 2.7 collective-permute-start.31
  399.4 18.0 %collective-permute-start.39 = (bf16[96,1536]{1,0:T(8,128)(2,1)S(1)}, bf16[96,1536]{1,0:T(8,128)(2,1)S(1)}, u32[]{:S(2)}, u32[]{:S(2)}) collective-permute-start(bf16[96,1536]{1,0:T(8,128)(2,1)S(1)} %slice_bitcast_fusion.4), channel_id=1, source_target_pairs={{0,2},{2,4},{4,6},{6,0},{1,3},{3,5},{5,7},{7,1},{8,10},{10,12},{12... | collective-permute-start | bytes 884744 | tf_op jit(solution)/shard_map/ppermute | solution.py:741
  400.4 19.6 %collective-permute-start.32 = (bf16[256,1536]{1,0:T(8,128)(2,1)S(1)}, bf16[256,1536]{1,0:T(8,128)(2,1)S(1)}, u32[]{:S(2)}, u32[]{:S(2)}) collective-permute-start(bf16[256,1536]{1,0:T(8,128)(2,1)S(1)} %bitcast.108), channel_id=1, source_target_pairs={{0,1},{1,0},{2,3},{3,2},{4,5},{5,4},{6,7},{7,6},{8,9},{9,8},{10,11... | collective-permute-start | bytes 2359304 | tf_op jit(solution)/shard_map/ppermute | solution.py:736
  403.2 14.3 %collective-permute-start.33 = (bf16[4,112,512]{2,1,0:T(8,128)(2,1)S(1)}, bf16[4,112,512]{2,1,0:T(8,128)(2,1)S(1)}, u32[]{:S(2)}, u32[]{:S(2)}) collective-permute-start(bf16[4,112,512]{2,1,0:T(8,128)(2,1)S(1)} %fusion.19.refs_1_), channel_id=1, source_target_pairs={{0,16},{8,24},{16,0},{24,8},{1,17},{9,25},{17,1},{25,9},{2,18},{10... | collective-permute-start | bytes 1376264 | tf_op jit(solution)/shard_map/ppermute | solution.py:732
  422.6 9.9 %collective-permute-start.34 = (bf16[112,512]{1,0:T(8,128)(2,1)S(1)}, bf16[112,512]{1,0:T(8,128)(2,1)S(1)}, u32[]{:S(2)}, u32[]{:S(2)}) collective-permute-start(bf16[112,512]{1,0:T(8,128)(2,1)S(1)} %get-tuple-element.106), channel_id=1, source_target_pairs={{0,6},{2,0},{4,2},{6,4},{1,7},{3,1},{5,3},{7,5},{8,14},{10,8},{12,... | collective-permute-start | bytes 344072 | tf_op jit(solution)/shard_map/ppermute | solution.py:774
  425.8 15.1 %collective-permute-start.35 = (bf16[112,512]{1,0:T(8,128)(2,1)S(1)}, bf16[112,512]{1,0:T(8,128)(2,1)S(1)}, u32[]{:S(2)}, u32[]{:S(2)}) collective-permute-start(bf16[112,512]{1,0:T(8,128)(2,1)S(1)} %get-tuple-element.108), channel_id=1, source_target_pairs={{0,4},{2,6},{4,0},{6,2},{1,5},{3,7},{5,1},{7,3},{8,12},{10,14},{12... | collective-permute-start | bytes 344072 | tf_op jit(solution)/shard_map/ppermute | solution.py:774
  430.7 10.3 %collective-permute-start.36 = (bf16[112,512]{1,0:T(8,128)(2,1)S(1)}, bf16[112,512]{1,0:T(8,128)(2,1)S(1)}, u32[]{:S(2)}, u32[]{:S(2)}) collective-permute-start(bf16[112,512]{1,0:T(8,128)(2,1)S(1)} %get-tuple-element.107), channel_id=1, source_target_pairs={{0,2},{2,4},{4,6},{6,0},{1,3},{3,5},{5,7},{7,1},{8,10},{10,12},{12... | collective-permute-start | bytes 344072 | tf_op jit(solution)/shard_map/ppermute | solution.py:774
  430.8 20.0 %collective-permute-start.42 = (bf16[3,96,864]{2,1,0:T(8,128)(2,1)S(1)}, bf16[3,96,864]{2,1,0:T(8,128)(2,1)S(1)}, u32[]{:S(2)}, u32[]{:S(2)}) collective-permute-start(bf16[3,96,864]{2,1,0:T(8,128)(2,1)S(1)} %bitcast.125), channel_id=1, source_target_pairs={{0,8},{8,0},{16,24},{24,16},{1,9},{9,1},{17,25},{25,17},{2,10},{10... | collective-permute-start | bytes 1493000 | tf_op jit(solution)/shard_map/ppermute | solution.py:732
  430.9 19.9 %collective-permute-start.43 = (bf16[3,96,864]{2,1,0:T(8,128)(2,1)S(1)}, bf16[3,96,864]{2,1,0:T(8,128)(2,1)S(1)}, u32[]{:S(2)}, u32[]{:S(2)}) collective-permute-start(bf16[3,96,864]{2,1,0:T(8,128)(2,1)S(1)} %bitcast.124), channel_id=1, source_target_pairs={{0,16},{8,24},{16,0},{24,8},{1,17},{9,25},{17,1},{25,9},{2,18},{10... | collective-permute-start | bytes 1493000 | tf_op jit(solution)/shard_map/ppermute | solution.py:732
  432.5 23.1 %collective-permute-start.44 = (bf16[3,96,864]{2,1,0:T(8,128)(2,1)S(1)}, bf16[3,96,864]{2,1,0:T(8,128)(2,1)S(1)}, u32[]{:S(2)}, u32[]{:S(2)}) collective-permute-start(bf16[3,96,864]{2,1,0:T(8,128)(2,1)S(1)} %bitcast.123), channel_id=1, source_target_pairs={{0,24},{8,16},{16,8},{24,0},{1,25},{9,17},{17,9},{25,1},{2,26},{10... | collective-permute-start | bytes 1493000 | tf_op jit(solution)/shard_map/ppermute | solution.py:732
  440.9 9.7 %collective-permute-start.40 = (bf16[96,1536]{1,0:T(8,128)(2,1)S(1)}, bf16[96,1536]{1,0:T(8,128)(2,1)S(1)}, u32[]{:S(2)}, u32[]{:S(2)}) collective-permute-start(bf16[96,1536]{1,0:T(8,128)(2,1)S(1)} %bitcast.116), channel_id=1, source_target_pairs={{0,2},{2,4},{4,6},{6,0},{1,3},{3,5},{5,7},{7,1},{8,10},{10,12},{12... | collective-permute-start | bytes 884744 | tf_op jit(solution)/shard_map/ppermute | solution.py:741
  441.0 3.6 collective-permute-start.37
  450.7 9.4 %collective-permute-start.41 = (bf16[96,1536]{1,0:T(8,128)(2,1)S(1)}, bf16[96,1536]{1,0:T(8,128)(2,1)S(1)}, u32[]{:S(2)}, u32[]{:S(2)}) collective-permute-start(bf16[96,1536]{1,0:T(8,128)(2,1)S(1)} %fusion.17), channel_id=1, source_target_pairs={{0,2},{2,4},{4,6},{6,0},{1,3},{3,5},{5,7},{7,1},{8,10},{10,12},{12... | collective-permute-start | bytes 884744 | tf_op jit(solution)/shard_map/ppermute | solution.py:741
  (38 other events, 263.6 us)
Sparse Core Ops, SparseCore 0:
  43.8 160.2 all-gather.1
  244.1 177.6 reduce-scatter.1

commit v3 on v2

--- a/solution.py
+++ b/solution.py
@@ -503,11 +503,10 @@
 
 
 def token_copies(refs, whole, sems):
-    own, both, across = refs
-    rows = own.shape[0]
-    pairs = ((own, 0), (both.at[0], 1), (across, 2), (both.at[1], 3))
+    rows = refs[0].shape[0]
     return [
-        pltpu.make_async_copy(ref, whole.at[pl.ds(i * rows, rows)], sems.at[i]) for ref, i in pairs
+        pltpu.make_async_copy(ref, whole.at[pl.ds(i * rows, rows)], sems.at[i])
+        for i, ref in enumerate(refs)
     ]
 
 
@@ -533,15 +532,15 @@
     tall = model // parts
 
     def kernel(where_ref, *refs):
-        weights_ref = refs[6]
-        sums, grads = refs[7:11], refs[11]
-        left, w_gate, w_up, w_down, right, back, stage = refs[12:19]
-        sem_h, sem_c, sem_g, sem_u, sem_d, sem_s, sem_o = refs[19:]
+        weights_ref = refs[8]
+        sums, grads = refs[9:13], refs[13]
+        left, w_gate, w_up, w_down, right, back, stage = refs[14:21]
+        sem_h, sem_c, sem_g, sem_u, sem_d, sem_s, sem_o = refs[21:]
         me = where_ref[size + 1]
         gates = weight_copies(where_ref, weights_ref, 0, w_gate, sem_g)
-        reads = token_copies(refs[:3], left.at[0], sem_h)
+        reads = token_copies(refs[:4], left.at[0], sem_h)
         ups = weight_copies(where_ref, weights_ref, 1, w_up, sem_u)
-        pulls = token_copies(refs[3:6], left.at[1], sem_c)
+        pulls = token_copies(refs[4:8], left.at[1], sem_c)
         downs = weight_copies(where_ref, weights_ref, 2, w_down, sem_d)
         for copies in (gates, reads, ups, pulls, downs):
             begin(copies)
@@ -628,7 +627,7 @@
     return pl.pallas_call(
         kernel,
         out_shape=(shaped((2, rows, model)),) * 4 + (shaped((size, parts, count, share, width)),),
-        in_specs=[SMEM] + [ANY] * 7,
+        in_specs=[SMEM] + [ANY] * 9,
         out_specs=(ANY,) * 5,
         scratch_shapes=[pltpu.VMEM((2, total, model), LOW)]
         + [pltpu.VMEM((model, width), LOW)] * 3
@@ -801,7 +800,7 @@
 
 def group_tokens(part):
     across = flip(part, 2)
-    return (part, flip(collect([part, across]), 1), across)
+    return (part, flip(part, 1), across, flip(across, 1))
 
 
 def chip_sum(keep, send):

time: 474 us -> 471 us (level)
    pallas_call x13 -> x11, Pallas kernels: 14.8 us -> 12 us  [collect(): pl.pallas_call(kernel, out_shape=shaped((count,) + parts[0].shape, parts[...]
    ppermute x22 -> x24, waiting for transfers between devices: 94.8 us -> 92.3 us  [flip(): return lax.ppermute(part, 'fsdp', [(i, i ^ bit) for i in range(size)])]
    ppermute x22 -> x24, starting transfers between devices: 16.1 us -> 16.1 us  [flip(): return lax.ppermute(part, 'fsdp', [(i, i ^ bit) for i in range(size)])]
  transfers between devices with their start and end apart: 47 -> 49, of which waited for: 26 -> 27; matrix products, arithmetic and copies ran while one was open for 7% -> 7% of each run, Pallas kernels for 13% -> 12%
where the time goes in v3:
time: 471 us; the launch traced here: 465 us
  waiting for transfers between devices  257 us (55%)
  Pallas kernels  98.5 us (21%)
  starting transfers between devices  48.8 us (10%)
  other arithmetic  24.1 us (5%)
  between operations  15.4 us (3%)
  local copies, waits for them, and re-layouts  12.5 us (3%)
  matrix products  8.26 us (2%)
    ppermute x24, waiting for transfers between devices, flip(): return lax.ppermute(part, 'fsdp', [(i, i ^ bit) for i in range(size)])  92.3 us
    ppermute x3, waiting for transfers between devices, back_sum(): lax.ppermute(terms[step], 'ctx', [(i, i - step) for i in range(step, size)])  44.7 us
    ppermute x9, waiting for transfers between devices, turn(): return lax.ppermute(part, 'ctx', [(i, (i + 1) % size) for i in range(size)])  38.8 us
    pallas_call x1, Pallas kernels, ffn(): pl.pallas_call(kernel, out_shape=(shaped((2, rows, model)),) * 4 + (shape...  38.6 us
    ppermute x5, waiting for transfers between devices, swap(): return lax.ppermute(part, 'tp', [(0, 1), (1, 0)])  37.1 us
    ppermute x3, waiting for transfers between devices, back_slots(): lax.ppermute(part, 'ctx', [(i, i + step) for i in range(size - step)])  19.8 us
    all_gather x1, waiting for transfers between devices, body(): lax.all_gather(block.reshape(-1, block.shape[-1]), 'ctx', axis=0, tiled=T...  16.1 us
    ppermute x24, starting transfers between devices, flip(): return lax.ppermute(part, 'fsdp', [(i, i ^ bit) for i in range(size)])  16.1 us
  transfers between devices with their start and end apart: 49, of which 27 were waited for; matrix products, arithmetic and copies ran while one was open for 7% of the time, Pallas kernels for 12%

profile of v3, /device:TPU:0, one launch (start us, length us, event | category | flops | bytes accessed | tf_op | source)
XLA Modules:
  0.0 464.5 jit_solution(7801060747065712178)
XLA Ops:
  8.2 3.1 collective-permute-start.5
  11.4 3.1 split_columns.1
  18.1 2.2 collective-permute-done.5.refs_1_
  20.3 3.4 collective-permute-done.refs_1_
  24.1 8.7 %collective-permute-done.1.refs_2_ = bf16[112,512]{1,0:T(8,128)(2,1)S(1)} collective-permute-done((bf16[112,512]{1,0:T(8,128)(2,1)S(1)}, bf16[112,512]{1,0:T(8,128)(2,1)S(1)}, u32[]{:S(2)}, u32[]{:S(2)}) %collective-permute-start.1) | collective-permute-done | bytes 114720 | tf_op jit(solution)/shard_map/ppermute | solution.py:740
  32.8 6.6 %collective-permute-done.2.refs_3_.refs_4_ = bf16[112,512]{1,0:T(8,128)(2,1)S(1)} collective-permute-done((bf16[112,512]{1,0:T(8,128)(2,1)S(1)}, bf16[112,512]{1,0:T(8,128)(2,1)S(1)}, u32[]{:S(2)}, u32[]{:S(2)}) %collective-permute-start.2) | collective-permute-done | bytes 114720 | tf_op jit(solution)/shard_map/ppermute | solution.py:740
  40.2 3.4 collect.16
  47.4 9.6 %collective-permute-done.3.refs_1_.refs_2_.refs_4_ = bf16[4,112,512]{2,1,0:T(8,128)(2,1)S(1)} collective-permute-done((bf16[4,112,512]{2,1,0:T(8,128)(2,1)S(1)}, bf16[4,112,512]{2,1,0:T(8,128)(2,1)S(1)}, u32[]{:S(2)}, u32[]{:S(2)}) %collective-permute-start.3) | collective-permute-done | bytes 458784 | tf_op jit(solution)/shard_map/ppermute | solution.py:731
  62.4 23.5 %collective-permute-done.8.refs_1_.refs_2_ = bf16[4,96,1536]{2,1,0:T(8,128)(2,1)} collective-permute-done((bf16[4,96,1536]{2,1,0:T(8,128)(2,1)}, bf16[4,96,1536]{2,1,0:T(8,128)(2,1)}, u32[]{:S(2)}, u32[]{:S(2)}) %collective-permute-start.8) | collective-permute-done | bytes 1179680 | tf_op jit(solution)/shard_map/ppermute | solution.py:731
  85.9 2.9 collect.14
  91.1 4.4 arrange.2
  98.7 3.5 collective-permute-start.10
  102.3 3.7 collective-permute-start.11
  106.0 2.1 collective-permute-start.12
  108.3 5.3 %arrange.3 = (bf16[1536,768]{1,0:T(8,128)(2,1)}, bf16[1536,768]{1,0:T(8,128)(2,1)}) custom-call(s32[6]{0:T(128)S(1)} %pad_add_fusion.where_ref, bf16[4,96,1536]{2,1,0:T(8,128)(2,1)S(1)} %copy-done.2, bf16[2,4,96,1536]{3,2,1,0:T(8,128)(2,1)} %collective-permute-done.9.refs_1_, bf16[4,96,1536]{2,1,0:T(8,128)(2,1)} %collective-permute-done.8.refs_1_.refs_2_), custom_call_target="tpu_custom_call" | custom-call | flops 1800000000 | bytes 2000000 | tf_op jit(solution)/shard_map/arrange/pallas_call | solution.py:493
  113.7 3.3 fusion.37.q_ref
  117.0 8.7 %collective-permute-done.11.refs_2_ = bf16[256,512]{1,0:T(8,128)(2,1)} collective-permute-done((bf16[256,512]{1,0:T(8,128)(2,1)S(1)}, bf16[256,512]{1,0:T(8,128)(2,1)}, u32[]{:S(2)}, u32[]{:S(2)}) %collective-permute-start.11) | collective-permute-done | bytes 262176 | tf_op jit(solution)/shard_map/ppermute | solution.py:785
  125.7 11.0 %collective-permute-done.12.refs_3_ = bf16[256,512]{1,0:T(8,128)(2,1)} collective-permute-done((bf16[256,512]{1,0:T(8,128)(2,1)S(1)}, bf16[256,512]{1,0:T(8,128)(2,1)}, u32[]{:S(2)}, u32[]{:S(2)}) %collective-permute-start.12) | collective-permute-done | bytes 262176 | tf_op jit(solution)/shard_map/ppermute | solution.py:785
  136.8 6.6 %attend.1 = (bf16[256,768]{1,0:T(8,128)(2,1)S(1)}, bf16[256,768]{1,0:T(8,128)(2,1)}, f32[4,128,768]{2,1,0:T(8,128)}) custom-call(s32[6]{0:T(128)S(1)} %pad_add_fusion.where_ref, s32[2]{0:T(128)S(1)} %bitcast.111, f32[256,768]{1,0:T(8,128)} %fusion.37.q_ref, bf16[256,512]{1,0:T(8,128)(2,1)S(1)} %keys.1.refs_0_, ...), custom_call_target="tpu_custom_call" | custom-call | flops 12600000512 | bytes 14000000 | tf_op jit(solution)/shard_map/attend/pallas_call | solution.py:272
  143.4 2.8 convolution_convert_fusion
  149.4 16.0 %collective-permute-done.13 = bf16[256,1536]{1,0:T(8,128)(2,1)} collective-permute-done((bf16[256,1536]{1,0:T(8,128)(2,1)}, bf16[256,1536]{1,0:T(8,128)(2,1)}, u32[]{:S(2)}, u32[]{:S(2)}) %collective-permute-start.13) | collective-permute-done | bytes 786464 | tf_op jit(solution)/shard_map/ppermute | solution.py:735
  165.5 1.8 multiply_reduce_fusion.2
  169.7 15.8 %collective-permute-done.15.refs_2_ = bf16[256,1536]{1,0:T(8,128)(2,1)S(1)} collective-permute-done((bf16[256,1536]{1,0:T(8,128)(2,1)S(1)}, bf16[256,1536]{1,0:T(8,128)(2,1)S(1)}, u32[]{:S(2)}, u32[]{:S(2)}) %collective-permute-start.15) | collective-permute-done | bytes 786464 | tf_op jit(solution)/shard_map/ppermute | solution.py:731
  188.0 16.1 %all-gather.2.cloned.1.call-done = bf16[4608,864]{1,0:T(8,128)(2,1)} async-done(((bf16[1152,864]{1,0:T(8,128)(2,1)}), bf16[4608,864]{1,0:T(8,128)(2,1)}) %all-gather.2.cloned.1.call-update) | async-done | bytes 7962640 | tf_op jit(solution)/shard_map/all_gather | solution.py:886
  205.2 38.6 %ffn.1 = (bf16[2,256,1536]{2,1,0:T(8,128)(2,1)}, bf16[2,256,1536]{2,1,0:T(8,128)(2,1)}, bf16[2,256,1536]{2,1,0:T(8,128)(2,1)}, bf16[2,256,1536]{2,1,0:T(8,128)(2,1)}, bf16[4,4,3,96,864]{4,3,2,1,0:T(8,128)(2,1)}) custom-call(s32[6]{0:T(128)S(1)} %pad_add_fusion.where_ref, bf16[256,1536]{1,0:T(8,128)(2,1)S(1)} %multiply_convert_fusion.refs_0_, ...), custom_call_target="tpu_custom_call" | custom-call | flops 33300000768 | bytes 37000000 | tf_op jit(solution)/shard_map/ffn/pallas_call | solution.py:627
  243.9 3.7 collective-permute-done.23
  250.9 17.9 %collective-permute-done.24 = bf16[256,1536]{1,0:T(8,128)(2,1)S(1)} collective-permute-done((bf16[256,1536]{1,0:T(8,128)(2,1)S(1)}, bf16[256,1536]{1,0:T(8,128)(2,1)S(1)}, u32[]{:S(2)}, u32[]{:S(2)}) %collective-permute-start.24) | collective-permute-done | bytes 786464 | tf_op jit(solution)/shard_map/ppermute | solution.py:731
  272.0 17.2 %collective-permute-done.25 = bf16[256,1536]{1,0:T(8,128)(2,1)S(1)} collective-permute-done((bf16[256,1536]{1,0:T(8,128)(2,1)S(1)}, bf16[256,1536]{1,0:T(8,128)(2,1)S(1)}, u32[]{:S(2)}, u32[]{:S(2)}) %collective-permute-start.25) | collective-permute-done | bytes 786464 | tf_op jit(solution)/shard_map/ppermute | solution.py:735
  289.9 1.8 fusion.29
  293.2 10.5 %attend_back.1 = (bf16[256,768]{1,0:T(8,128)(2,1)}, bf16[256,512]{1,0:T(8,128)(2,1)S(1)}, bf16[256,512]{1,0:T(8,128)(2,1)S(1)}, bf16[256,512]{1,0:T(8,128)(2,1)S...) custom-call(s32[6]{0:T(128)S(1)} %pad_add_fusion.where_ref, s32[2]{0:T(128)S(1)} %bitcast.112, ...), custom_call_target="tpu_custom_call" | custom-call | flops 15299999744 | bytes 17000000 | tf_op jit(solution)/shard_map/attend_back/pallas_call | solution.py:297
  304.7 5.5 %head_grads.2 = (bf16[2,4,96,1536]{3,2,1,0:T(8,128)(2,1)}, bf16[2,4,96,1536]{3,2,1,0:T(8,128)(2,1)}) custom-call(s32[6]{0:T(128)S(1)} %pad_add_fusion.where_ref, bf16[256,1536]{1,0:T(8,128)(2,1)S(1)} %fusion.3.refs_0_, bf16[256,1536]{1,0:T(8,128)(2,1)} %copy-done, bf16[256,768]{1,0:T(8,128)(2,1)S(1)} %copy-done.11, bf16[256,768]{1,0:T(8,128)(2,1)S(1)} %copy-done.10), custom_call_target="tpu_custom_call" | custom-call | flops 2700000000 | bytes 3000000 | tf_op jit(solution)/shard_map/head_grads/pallas_call | solution.py:714
  310.4 2.6 collect.17
  313.8 3.7 collective-permute-done.26
  317.5 2.5 fusion.15
  328.5 12.0 %collective-permute-done.27 = bf16[256,1536]{1,0:T(8,128)(2,1)S(1)} collective-permute-done((bf16[256,1536]{1,0:T(8,128)(2,1)}, bf16[256,1536]{1,0:T(8,128)(2,1)S(1)}, u32[]{:S(2)}, u32[]{:S(2)}) %collective-permute-start.27) | collective-permute-done | bytes 786464 | tf_op jit(solution)/shard_map/ppermute | solution.py:731
  342.0 1.7 collective-permute-start.28
  343.8 10.6 %collective-permute-done.30 = bf16[256,512]{1,0:T(8,128)(2,1)S(1)} collective-permute-done((bf16[256,512]{1,0:T(8,128)(2,1)S(1)}, bf16[256,512]{1,0:T(8,128)(2,1)S(1)}, u32[]{:S(2)}, u32[]{:S(2)}) %collective-permute-start.30) | collective-permute-done | bytes 262176 | tf_op jit(solution)/shard_map/ppermute | solution.py:795
  354.3 34.1 %collective-permute-done.31 = bf16[256,512]{1,0:T(8,128)(2,1)S(1)} collective-permute-done((bf16[256,512]{1,0:T(8,128)(2,1)S(1)}, bf16[256,512]{1,0:T(8,128)(2,1)S(1)}, u32[]{:S(2)}, u32[]{:S(2)}) %collective-permute-start.31) | collective-permute-done | bytes 262176 | tf_op jit(solution)/shard_map/ppermute | solution.py:795
  389.6 3.6 normed_back.1
  393.1 4.1 head_grads.3
  397.3 1.8 fusion
  404.1 13.0 %collective-permute-done.41 = bf16[96,1536]{1,0:T(8,128)(2,1)S(1)} collective-permute-done((bf16[96,1536]{1,0:T(8,128)(2,1)S(1)}, bf16[96,1536]{1,0:T(8,128)(2,1)S(1)}, u32[]{:S(2)}, u32[]{:S(2)}) %collective-permute-start.41) | collective-permute-done | bytes 294944 | tf_op jit(solution)/shard_map/ppermute | solution.py:740
  417.4 2.4 collective-permute-done.34
  422.3 3.2 collective-permute-start.36
  429.1 7.6 %collective-permute-done.37 = bf16[112,512]{1,0:T(8,128)(2,1)S(1)} collective-permute-done((bf16[112,512]{1,0:T(8,128)(2,1)S(1)}, bf16[112,512]{1,0:T(8,128)(2,1)S(1)}, u32[]{:S(2)}, u32[]{:S(2)}) %collective-permute-start.37) | collective-permute-done | bytes 114720 | tf_op jit(solution)/shard_map/ppermute | solution.py:773
  441.5 5.0 %collective-permute-done.42 = bf16[96,1536]{1,0:T(8,128)(2,1)S(1)} collective-permute-done((bf16[96,1536]{1,0:T(8,128)(2,1)S(1)}, bf16[96,1536]{1,0:T(8,128)(2,1)S(1)}, u32[]{:S(2)}, u32[]{:S(2)}) %collective-permute-start.42) | collective-permute-done | bytes 294944 | tf_op jit(solution)/shard_map/ppermute | solution.py:740
  446.7 5.1 %collective-permute-done.46.refs_3_ = bf16[3,96,864]{2,1,0:T(8,128)(2,1)S(1)} collective-permute-done((bf16[3,96,864]{2,1,0:T(8,128)(2,1)S(1)}, bf16[3,96,864]{2,1,0:T(8,128)(2,1)S(1)}, u32[]{:S(2)}, u32[]{:S(2)}) %collective-permute-start.46) | collective-permute-done | bytes 497696 | tf_op jit(solution)/shard_map/ppermute | solution.py:731
  452.6 3.7 join_columns.1
  (225 shorter events, 69.3 us)
Async XLA Ops:
  7.2 196.8 %all-gather.2.cloned.1.call-start = ((), (), s32[]{:S(2)}) async-start(), calls=%async_computation.1 | async-start | bytes 10321920 | tf_op jit(solution)/shard_map/all_gather | solution.py:886
  8.2 12.1 %collective-permute-start.5 = (bf16[96,1536]{1,0:T(8,128)(2,1)S(1)}, bf16[96,1536]{1,0:T(8,128)(2,1)S(1)}, u32[]{:S(2)}, u32[]{:S(2)}) collective-permute-start(bf16[96,1536]{1,0:T(8,128)(2,1)S(1)} %pad_maximum_fusion.refs_0_), channel_id=1, source_target_pairs={{0,2},{2,4},{4,6},{6,0},{1,3},{3,5},{5,7},{7,1},{8,10},{10,12},{12... | collective-permute-start | bytes 884744 | tf_op jit(solution)/shard_map/ppermute | solution.py:740
  14.5 24.9 %collective-permute-start.20 = (bf16[3,96,864]{2,1,0:T(8,128)(2,1)S(1)}, bf16[3,96,864]{2,1,0:T(8,128)(2,1)S(1)}, u32[]{:S(2)}, u32[]{:S(2)}) collective-permute-start(bf16[3,96,864]{2,1,0:T(8,128)(2,1)S(1)} %get-tuple-element.64), channel_id=1, source_target_pairs={{0,8},{8,0},{16,24},{24,16},{1,9},{9,1},{17,25},{25,17},{2,10},{10... | collective-permute-start | bytes 1493000 | tf_op jit(solution)/shard_map/ppermute | solution.py:731
  14.5 24.9 %collective-permute-start.21 = (bf16[3,96,864]{2,1,0:T(8,128)(2,1)S(1)}, bf16[3,96,864]{2,1,0:T(8,128)(2,1)S(1)}, u32[]{:S(2)}, u32[]{:S(2)}) collective-permute-start(bf16[3,96,864]{2,1,0:T(8,128)(2,1)S(1)} %get-tuple-element.65), channel_id=1, source_target_pairs={{0,16},{8,24},{16,0},{24,8},{1,17},{9,25},{17,1},{25,9},{2,18},{10... | collective-permute-start | bytes 1493000 | tf_op jit(solution)/shard_map/ppermute | solution.py:731
  16.0 23.4 %collective-permute-start.22 = (bf16[3,96,864]{2,1,0:T(8,128)(2,1)}, bf16[3,96,864]{2,1,0:T(8,128)(2,1)S(1)}, u32[]{:S(2)}, u32[]{:S(2)}) collective-permute-start(bf16[3,96,864]{2,1,0:T(8,128)(2,1)} %get-tuple-element.66), channel_id=1, source_target_pairs={{0,24},{8,16},{16,8},{24,0},{1,25},{9,17},{17,9},{25,1},{2,26},{10... | collective-permute-start | bytes 1493000 | tf_op jit(solution)/shard_map/ppermute | solution.py:731
  16.5 7.2 %collective-permute-start = (bf16[112,512]{1,0:T(8,128)(2,1)S(1)}, bf16[112,512]{1,0:T(8,128)(2,1)S(1)}, u32[]{:S(2)}, u32[]{:S(2)}) collective-permute-start(bf16[112,512]{1,0:T(8,128)(2,1)S(1)} %fusion.23.refs_0_), channel_id=1, source_target_pairs={{0,2},{2,4},{4,6},{6,0},{1,3},{3,5},{5,7},{7,1},{8,10},{10,12},{12... | collective-permute-start | bytes 344072 | tf_op jit(solution)/shard_map/ppermute | solution.py:740
  20.3 19.1 %collective-permute-start.6 = (bf16[96,1536]{1,0:T(8,128)(2,1)S(1)}, bf16[96,1536]{1,0:T(8,128)(2,1)S(1)}, u32[]{:S(2)}, u32[]{:S(2)}) collective-permute-start(bf16[96,1536]{1,0:T(8,128)(2,1)S(1)} %collective-permute-done.5.refs_1_), channel_id=1, source_target_pairs={{0,2},{2,4},{4,6},{6,0},{1,3},{3,5},{5,7},{7,1},{8,10},{10,12},{12... | collective-permute-start | bytes 884744 | tf_op jit(solution)/shard_map/ppermute | solution.py:740
  23.7 9.1 %collective-permute-start.1 = (bf16[112,512]{1,0:T(8,128)(2,1)S(1)}, bf16[112,512]{1,0:T(8,128)(2,1)S(1)}, u32[]{:S(2)}, u32[]{:S(2)}) collective-permute-start(bf16[112,512]{1,0:T(8,128)(2,1)S(1)} %collective-permute-done.refs_1_), channel_id=1, source_target_pairs={{0,2},{2,4},{4,6},{6,0},{1,3},{3,5},{5,7},{7,1},{8,10},{10,12},{12... | collective-permute-start | bytes 344072 | tf_op jit(solution)/shard_map/ppermute | solution.py:740
  32.8 6.6 %collective-permute-start.2 = (bf16[112,512]{1,0:T(8,128)(2,1)S(1)}, bf16[112,512]{1,0:T(8,128)(2,1)S(1)}, u32[]{:S(2)}, u32[]{:S(2)}) collective-permute-start(bf16[112,512]{1,0:T(8,128)(2,1)S(1)} %collective-permute-done.1.refs_2_), channel_id=1, source_target_pairs={{0,2},{2,4},{4,6},{6,0},{1,3},{3,5},{5,7},{7,1},{8,10},{10,12},{12... | collective-permute-start | bytes 344072 | tf_op jit(solution)/shard_map/ppermute | solution.py:740
  43.6 378.4 %reduce-scatter.2.cloned.1.call-start = ((), (), s32[]{:S(2)}) async-start(), calls=%async_computation.2 | async-start | bytes 10321920 | tf_op jit(solution)/shard_map/reduce_scatter | solution.py:830
  44.3 12.7 %collective-permute-start.3 = (bf16[4,112,512]{2,1,0:T(8,128)(2,1)S(1)}, bf16[4,112,512]{2,1,0:T(8,128)(2,1)S(1)}, u32[]{:S(2)}, u32[]{:S(2)}) collective-permute-start(bf16[4,112,512]{2,1,0:T(8,128)(2,1)S(1)} %collect.11.refs_0_), channel_id=1, source_target_pairs={{0,16},{8,24},{16,0},{24,8},{1,17},{9,25},{17,1},{25,9},{2,18},{10... | collective-permute-start | bytes 1376264 | tf_op jit(solution)/shard_map/ppermute | solution.py:731
  45.8 11.2 %collective-permute-start.7 = (bf16[96,1536]{1,0:T(8,128)(2,1)S(1)}, bf16[96,1536]{1,0:T(8,128)(2,1)S(1)}, u32[]{:S(2)}, u32[]{:S(2)}) collective-permute-start(bf16[96,1536]{1,0:T(8,128)(2,1)S(1)} %collective-permute-done.6.refs_2_.refs_5_), channel_id=1, source_target_pairs={{0,2},{2,4},{4,6},{6,0},{1,3},{3,5},{5,7},{7,1},{8,10},{10,12},{12... | collective-permute-start | bytes 884744 | tf_op jit(solution)/shard_map/ppermute | solution.py:740
  58.3 27.6 %collective-permute-start.8 = (bf16[4,96,1536]{2,1,0:T(8,128)(2,1)}, bf16[4,96,1536]{2,1,0:T(8,128)(2,1)}, u32[]{:S(2)}, u32[]{:S(2)}) collective-permute-start(bf16[4,96,1536]{2,1,0:T(8,128)(2,1)} %collect.13.refs_0_), channel_id=1, source_target_pairs={{0,16},{8,24},{16,0},{24,8},{1,17},{9,25},{17,1},{25,9},{2,18},{10... | collective-permute-start | bytes 3538952 | tf_op jit(solution)/shard_map/ppermute | solution.py:731
  62.3 27.9 %collective-permute-start.4 = (bf16[2,4,112,512]{3,2,1,0:T(8,128)(2,1)S(1)}, bf16[2,4,112,512]{3,2,1,0:T(8,128)(2,1)S(1)}, u32[]{:S(2)}, u32[]{:S(2)}) collective-permute-start(bf16[2,4,112,512]{3,2,1,0:T(8,128)(2,1)S(1)} %collect.12), channel_id=1, source_target_pairs={{0,8},{8,0},{16,24},{24,16},{1,9},{9,1},{17,25},{25,17},{2,10},{10... | collective-permute-start | bytes 2752520 | tf_op jit(solution)/shard_map/ppermute | solution.py:731
  88.8 19.5 %collective-permute-start.9 = (bf16[2,4,96,1536]{3,2,1,0:T(8,128)(2,1)}, bf16[2,4,96,1536]{3,2,1,0:T(8,128)(2,1)}, u32[]{:S(2)}, u32[]{:S(2)}) collective-permute-start(bf16[2,4,96,1536]{3,2,1,0:T(8,128)(2,1)} %collect.14), channel_id=1, source_target_pairs={{0,8},{8,0},{16,24},{24,16},{1,9},{9,1},{17,25},{25,17},{2,10},{10... | collective-permute-start | bytes 7077896 | tf_op jit(solution)/shard_map/ppermute | solution.py:731
  98.7 18.3 %collective-permute-start.10 = (bf16[256,512]{1,0:T(8,128)(2,1)S(1)}, bf16[256,512]{1,0:T(8,128)(2,1)S(1)}, u32[]{:S(2)}, u32[]{:S(2)}) collective-permute-start(bf16[256,512]{1,0:T(8,128)(2,1)S(1)} %keys.1.refs_0_), channel_id=1, source_target_pairs={{0,2},{2,4},{4,6},{1,3},{3,5},{5,7},{8,10},{10,12},{12,14},{9,11},... | collective-permute-start | bytes 786440 | tf_op jit(solution)/shard_map/ppermute | solution.py:785
  102.3 23.5 %collective-permute-start.11 = (bf16[256,512]{1,0:T(8,128)(2,1)S(1)}, bf16[256,512]{1,0:T(8,128)(2,1)}, u32[]{:S(2)}, u32[]{:S(2)}) collective-permute-start(bf16[256,512]{1,0:T(8,128)(2,1)S(1)} %keys.1.refs_0_), channel_id=1, source_target_pairs={{0,4},{2,6},{1,5},{3,7},{8,12},{10,14},{9,13},{11,15},{16,20},{18,... | collective-permute-start | bytes 786440 | tf_op jit(solution)/shard_map/ppermute | solution.py:785
  106.0 30.8 %collective-permute-start.12 = (bf16[256,512]{1,0:T(8,128)(2,1)S(1)}, bf16[256,512]{1,0:T(8,128)(2,1)}, u32[]{:S(2)}, u32[]{:S(2)}) collective-permute-start(bf16[256,512]{1,0:T(8,128)(2,1)S(1)} %keys.1.refs_0_), channel_id=1, source_target_pairs={{0,6},{1,7},{8,14},{9,15},{16,22},{17,23},{24,30},{25,31}} | collective-permute-start | bytes 786440 | tf_op jit(solution)/shard_map/ppermute | solution.py:785
  146.3 19.2 %collective-permute-start.13 = (bf16[256,1536]{1,0:T(8,128)(2,1)}, bf16[256,1536]{1,0:T(8,128)(2,1)}, u32[]{:S(2)}, u32[]{:S(2)}) collective-permute-start(bf16[256,1536]{1,0:T(8,128)(2,1)} %convolution_convert_fusion), channel_id=1, source_target_pairs={{0,1},{1,0},{2,3},{3,2},{4,5},{5,4},{6,7},{7,6},{8,9},{9,8},{10,11... | collective-permute-start | bytes 2359304 | tf_op jit(solution)/shard_map/ppermute | solution.py:735
  147.9 21.1 %collective-permute-start.18 = (bf16[256,1536]{1,0:T(8,128)(2,1)S(1)}, bf16[256,1536]{1,0:T(8,128)(2,1)S(1)}, u32[]{:S(2)}, u32[]{:S(2)}) collective-permute-start(bf16[256,1536]{1,0:T(8,128)(2,1)S(1)} %bitcast.113), channel_id=1, source_target_pairs={{0,16},{8,24},{16,0},{24,8},{1,17},{9,25},{17,1},{25,9},{2,18},{10... | collective-permute-start | bytes 2359304 | tf_op jit(solution)/shard_map/ppermute | solution.py:731
  167.5 18.0 %collective-permute-start.15 = (bf16[256,1536]{1,0:T(8,128)(2,1)S(1)}, bf16[256,1536]{1,0:T(8,128)(2,1)S(1)}, u32[]{:S(2)}, u32[]{:S(2)}) collective-permute-start(bf16[256,1536]{1,0:T(8,128)(2,1)S(1)} %multiply_convert_fusion.refs_0_), channel_id=1, source_target_pairs={{0,16},{8,24},{16,0},{24,8},{1,17},{9,25},{17,1},{25,9},{2,18},{10... | collective-permute-start | bytes 2359304 | tf_op jit(solution)/shard_map/ppermute | solution.py:731
  169.0 16.5 %collective-permute-start.17 = (bf16[256,1536]{1,0:T(8,128)(2,1)S(1)}, bf16[256,1536]{1,0:T(8,128)(2,1)S(1)}, u32[]{:S(2)}, u32[]{:S(2)}) collective-permute-start(bf16[256,1536]{1,0:T(8,128)(2,1)S(1)} %bitcast.114), channel_id=1, source_target_pairs={{0,8},{8,0},{16,24},{24,16},{1,9},{9,1},{17,25},{25,17},{2,10},{10... | collective-permute-start | bytes 2359304 | tf_op jit(solution)/shard_map/ppermute | solution.py:731
  169.1 16.5 %collective-permute-start.19 = (bf16[256,1536]{1,0:T(8,128)(2,1)S(1)}, bf16[256,1536]{1,0:T(8,128)(2,1)S(1)}, u32[]{:S(2)}, u32[]{:S(2)}) collective-permute-start(bf16[256,1536]{1,0:T(8,128)(2,1)S(1)} %collective-permute-done.18.refs_6_), channel_id=1, source_target_pairs={{0,8},{8,0},{16,24},{24,16},{1,9},{9,1},{17,25},{25,17},{2,10},{10... | collective-permute-start | bytes 2359304 | tf_op jit(solution)/shard_map/ppermute | solution.py:731
  169.6 16.0 %collective-permute-start.14 = (bf16[256,1536]{1,0:T(8,128)(2,1)S(1)}, bf16[256,1536]{1,0:T(8,128)(2,1)S(1)}, u32[]{:S(2)}, u32[]{:S(2)}) collective-permute-start(bf16[256,1536]{1,0:T(8,128)(2,1)S(1)} %multiply_convert_fusion.refs_0_), channel_id=1, source_target_pairs={{0,8},{8,0},{16,24},{24,16},{1,9},{9,1},{17,25},{25,17},{2,10},{10... | collective-permute-start | bytes 2359304 | tf_op jit(solution)/shard_map/ppermute | solution.py:731
  243.8 3.8 collective-permute-start.23
  249.2 19.6 %collective-permute-start.24 = (bf16[256,1536]{1,0:T(8,128)(2,1)S(1)}, bf16[256,1536]{1,0:T(8,128)(2,1)S(1)}, u32[]{:S(2)}, u32[]{:S(2)}) collective-permute-start(bf16[256,1536]{1,0:T(8,128)(2,1)S(1)} %fusion.14), channel_id=1, source_target_pairs={{0,16},{8,24},{16,0},{24,8},{1,17},{9,25},{17,1},{25,9},{2,18},{10... | collective-permute-start | bytes 2359304 | tf_op jit(solution)/shard_map/ppermute | solution.py:731
  270.2 18.9 %collective-permute-start.25 = (bf16[256,1536]{1,0:T(8,128)(2,1)S(1)}, bf16[256,1536]{1,0:T(8,128)(2,1)S(1)}, u32[]{:S(2)}, u32[]{:S(2)}) collective-permute-start(bf16[256,1536]{1,0:T(8,128)(2,1)S(1)} %fusion.10), channel_id=1, source_target_pairs={{0,1},{1,0},{2,3},{3,2},{4,5},{5,4},{6,7},{7,6},{8,9},{9,8},{10,11... | collective-permute-start | bytes 2359304 | tf_op jit(solution)/shard_map/ppermute | solution.py:735
  310.3 11.3 %collective-permute-start.29 = (bf16[2,4,96,1536]{3,2,1,0:T(8,128)(2,1)}, bf16[2,4,96,1536]{3,2,1,0:T(8,128)(2,1)}, u32[]{:S(2)}, u32[]{:S(2)}) collective-permute-start(bf16[2,4,96,1536]{3,2,1,0:T(8,128)(2,1)} %get-tuple-element.80), channel_id=1, source_target_pairs={{0,8},{8,0},{16,24},{24,16},{1,9},{9,1},{17,25},{25,17},{2,10},{10... | collective-permute-start | bytes 7077896 | tf_op jit(solution)/shard_map/ppermute | solution.py:731
  313.0 4.5 collective-permute-start.26
  319.9 20.6 %collective-permute-start.27 = (bf16[256,1536]{1,0:T(8,128)(2,1)}, bf16[256,1536]{1,0:T(8,128)(2,1)S(1)}, u32[]{:S(2)}, u32[]{:S(2)}) collective-permute-start(bf16[256,1536]{1,0:T(8,128)(2,1)} %fusion.15), channel_id=1, source_target_pairs={{0,16},{8,24},{16,0},{24,8},{1,17},{9,25},{17,1},{25,9},{2,18},{10... | collective-permute-start | bytes 2359304 | tf_op jit(solution)/shard_map/ppermute | solution.py:731
  323.3 74.0 %collective-permute-start.40 = (bf16[4,96,1536]{2,1,0:T(8,128)(2,1)S(1)}, bf16[4,96,1536]{2,1,0:T(8,128)(2,1)S(1)}, u32[]{:S(2)}, u32[]{:S(2)}) collective-permute-start(bf16[4,96,1536]{2,1,0:T(8,128)(2,1)S(1)} %fusion.12.refs_3_), channel_id=1, source_target_pairs={{0,16},{8,24},{16,0},{24,8},{1,17},{9,25},{17,1},{25,9},{2,18},{10... | collective-permute-start | bytes 3538952 | tf_op jit(solution)/shard_map/ppermute | solution.py:731
  324.5 29.9 %collective-permute-start.30 = (bf16[256,512]{1,0:T(8,128)(2,1)S(1)}, bf16[256,512]{1,0:T(8,128)(2,1)S(1)}, u32[]{:S(2)}, u32[]{:S(2)}) collective-permute-start(bf16[256,512]{1,0:T(8,128)(2,1)S(1)} %get-tuple-element.101), channel_id=1, source_target_pairs={{2,0},{4,2},{6,4},{3,1},{5,3},{7,5},{10,8},{12,10},{14,12},{11,9},... | collective-permute-start | bytes 786440 | tf_op jit(solution)/shard_map/ppermute | solution.py:795
  325.9 62.5 %collective-permute-start.31 = (bf16[256,512]{1,0:T(8,128)(2,1)S(1)}, bf16[256,512]{1,0:T(8,128)(2,1)S(1)}, u32[]{:S(2)}, u32[]{:S(2)}) collective-permute-start(bf16[256,512]{1,0:T(8,128)(2,1)S(1)} %get-tuple-element.103), channel_id=1, source_target_pairs={{4,0},{6,2},{5,1},{7,3},{12,8},{14,10},{13,9},{15,11},{20,16},{22,... | collective-permute-start | bytes 786440 | tf_op jit(solution)/shard_map/ppermute | solution.py:795
  327.2 61.3 %collective-permute-start.32 = (bf16[256,512]{1,0:T(8,128)(2,1)S(1)}, bf16[256,512]{1,0:T(8,128)(2,1)S(1)}, u32[]{:S(2)}, u32[]{:S(2)}) collective-permute-start(bf16[256,512]{1,0:T(8,128)(2,1)S(1)} %get-tuple-element.102), channel_id=1, source_target_pairs={{6,0},{7,1},{14,8},{15,9},{22,16},{23,17},{30,24},{31,25}} | collective-permute-start | bytes 786440 | tf_op jit(solution)/shard_map/ppermute | solution.py:795
  342.0 59.7 %collective-permute-start.28 = (bf16[256,1536]{1,0:T(8,128)(2,1)S(1)}, bf16[256,1536]{1,0:T(8,128)(2,1)S(1)}, u32[]{:S(2)}, u32[]{:S(2)}) collective-permute-start(bf16[256,1536]{1,0:T(8,128)(2,1)S(1)} %fusion.9), channel_id=1, source_target_pairs={{0,1},{1,0},{2,3},{3,2},{4,5},{5,4},{6,7},{7,6},{8,9},{9,8},{10,11... | collective-permute-start | bytes 2359304 | tf_op jit(solution)/shard_map/ppermute | solution.py:735
  397.2 2.7 collective-permute-start.33
  399.2 17.9 %collective-permute-start.41 = (bf16[96,1536]{1,0:T(8,128)(2,1)S(1)}, bf16[96,1536]{1,0:T(8,128)(2,1)S(1)}, u32[]{:S(2)}, u32[]{:S(2)}) collective-permute-start(bf16[96,1536]{1,0:T(8,128)(2,1)S(1)} %slice_bitcast_fusion.4), channel_id=1, source_target_pairs={{0,2},{2,4},{4,6},{6,0},{1,3},{3,5},{5,7},{7,1},{8,10},{10,12},{12... | collective-permute-start | bytes 884744 | tf_op jit(solution)/shard_map/ppermute | solution.py:740
  400.2 19.6 %collective-permute-start.34 = (bf16[256,1536]{1,0:T(8,128)(2,1)S(1)}, bf16[256,1536]{1,0:T(8,128)(2,1)S(1)}, u32[]{:S(2)}, u32[]{:S(2)}) collective-permute-start(bf16[256,1536]{1,0:T(8,128)(2,1)S(1)} %bitcast.108), channel_id=1, source_target_pairs={{0,1},{1,0},{2,3},{3,2},{4,5},{5,4},{6,7},{7,6},{8,9},{9,8},{10,11... | collective-permute-start | bytes 2359304 | tf_op jit(solution)/shard_map/ppermute | solution.py:735
  402.9 14.3 %collective-permute-start.35 = (bf16[4,112,512]{2,1,0:T(8,128)(2,1)S(1)}, bf16[4,112,512]{2,1,0:T(8,128)(2,1)S(1)}, u32[]{:S(2)}, u32[]{:S(2)}) collective-permute-start(bf16[4,112,512]{2,1,0:T(8,128)(2,1)S(1)} %fusion.19.refs_1_), channel_id=1, source_target_pairs={{0,16},{8,24},{16,0},{24,8},{1,17},{9,25},{17,1},{25,9},{2,18},{10... | collective-permute-start | bytes 1376264 | tf_op jit(solution)/shard_map/ppermute | solution.py:731
  422.3 6.8 %collective-permute-start.36 = (bf16[112,512]{1,0:T(8,128)(2,1)S(1)}, bf16[112,512]{1,0:T(8,128)(2,1)S(1)}, u32[]{:S(2)}, u32[]{:S(2)}) collective-permute-start(bf16[112,512]{1,0:T(8,128)(2,1)S(1)} %get-tuple-element.106), channel_id=1, source_target_pairs={{0,6},{2,0},{4,2},{6,4},{1,7},{3,1},{5,3},{7,5},{8,14},{10,8},{12,... | collective-permute-start | bytes 344072 | tf_op jit(solution)/shard_map/ppermute | solution.py:773
  425.5 11.2 %collective-permute-start.37 = (bf16[112,512]{1,0:T(8,128)(2,1)S(1)}, bf16[112,512]{1,0:T(8,128)(2,1)S(1)}, u32[]{:S(2)}, u32[]{:S(2)}) collective-permute-start(bf16[112,512]{1,0:T(8,128)(2,1)S(1)} %get-tuple-element.108), channel_id=1, source_target_pairs={{0,4},{2,6},{4,0},{6,2},{1,5},{3,7},{5,1},{7,3},{8,12},{10,14},{12... | collective-permute-start | bytes 344072 | tf_op jit(solution)/shard_map/ppermute | solution.py:773
  426.5 10.3 %collective-permute-start.38 = (bf16[112,512]{1,0:T(8,128)(2,1)S(1)}, bf16[112,512]{1,0:T(8,128)(2,1)S(1)}, u32[]{:S(2)}, u32[]{:S(2)}) collective-permute-start(bf16[112,512]{1,0:T(8,128)(2,1)S(1)} %get-tuple-element.107), channel_id=1, source_target_pairs={{0,2},{2,4},{4,6},{6,0},{1,3},{3,5},{5,7},{7,1},{8,10},{10,12},{12... | collective-permute-start | bytes 344072 | tf_op jit(solution)/shard_map/ppermute | solution.py:773
  426.9 19.7 %collective-permute-start.44 = (bf16[3,96,864]{2,1,0:T(8,128)(2,1)S(1)}, bf16[3,96,864]{2,1,0:T(8,128)(2,1)S(1)}, u32[]{:S(2)}, u32[]{:S(2)}) collective-permute-start(bf16[3,96,864]{2,1,0:T(8,128)(2,1)S(1)} %bitcast.125), channel_id=1, source_target_pairs={{0,8},{8,0},{16,24},{24,16},{1,9},{9,1},{17,25},{25,17},{2,10},{10... | collective-permute-start | bytes 1493000 | tf_op jit(solution)/shard_map/ppermute | solution.py:731
  427.0 19.7 %collective-permute-start.45 = (bf16[3,96,864]{2,1,0:T(8,128)(2,1)S(1)}, bf16[3,96,864]{2,1,0:T(8,128)(2,1)S(1)}, u32[]{:S(2)}, u32[]{:S(2)}) collective-permute-start(bf16[3,96,864]{2,1,0:T(8,128)(2,1)S(1)} %bitcast.124), channel_id=1, source_target_pairs={{0,16},{8,24},{16,0},{24,8},{1,17},{9,25},{17,1},{25,9},{2,18},{10... | collective-permute-start | bytes 1493000 | tf_op jit(solution)/shard_map/ppermute | solution.py:731
  429.1 22.7 %collective-permute-start.46 = (bf16[3,96,864]{2,1,0:T(8,128)(2,1)S(1)}, bf16[3,96,864]{2,1,0:T(8,128)(2,1)S(1)}, u32[]{:S(2)}, u32[]{:S(2)}) collective-permute-start(bf16[3,96,864]{2,1,0:T(8,128)(2,1)S(1)} %bitcast.123), channel_id=1, source_target_pairs={{0,24},{8,16},{16,8},{24,0},{1,25},{9,17},{17,9},{25,1},{2,26},{10... | collective-permute-start | bytes 1493000 | tf_op jit(solution)/shard_map/ppermute | solution.py:731
  436.8 9.8 %collective-permute-start.42 = (bf16[96,1536]{1,0:T(8,128)(2,1)S(1)}, bf16[96,1536]{1,0:T(8,128)(2,1)S(1)}, u32[]{:S(2)}, u32[]{:S(2)}) collective-permute-start(bf16[96,1536]{1,0:T(8,128)(2,1)S(1)} %bitcast.116), channel_id=1, source_target_pairs={{0,2},{2,4},{4,6},{6,0},{1,3},{3,5},{5,7},{7,1},{8,10},{10,12},{12... | collective-permute-start | bytes 884744 | tf_op jit(solution)/shard_map/ppermute | solution.py:740
  436.9 3.6 collective-permute-start.39
  446.6 9.7 %collective-permute-start.43 = (bf16[96,1536]{1,0:T(8,128)(2,1)S(1)}, bf16[96,1536]{1,0:T(8,128)(2,1)S(1)}, u32[]{:S(2)}, u32[]{:S(2)}) collective-permute-start(bf16[96,1536]{1,0:T(8,128)(2,1)S(1)} %fusion.17), channel_id=1, source_target_pairs={{0,2},{2,4},{4,6},{6,0},{1,3},{3,5},{5,7},{7,1},{8,10},{10,12},{12... | collective-permute-start | bytes 884744 | tf_op jit(solution)/shard_map/ppermute | solution.py:740
  (43 other events, 319.4 us)
Sparse Core Ops, SparseCore 0:
  43.7 160.2 all-gather.1
  244.0 173.0 reduce-scatter.1

commit v4 on v3

--- a/solution.py
+++ b/solution.py
@@ -764,17 +764,6 @@
     return total
 
 
-def ctx_sum_direct(terms):
-    size = lax.axis_size("ctx")
-    if size > LINE:
-        return ctx_sum(terms)
-    total = terms[0].astype(jnp.float32)
-    for step in range(1, size):
-        part = lax.ppermute(terms[step], "ctx", [(i, (i - step) % size) for i in range(size)])
-        total = total + part.astype(jnp.float32)
-    return total
-
-
 def back_slots(part):
     size = lax.axis_size("ctx")
     if size > LINE:
@@ -964,7 +953,7 @@
         )
     )
     kv_sum = pair_sum(near, far).astype(LOW)
-    own_kv = ctx_sum_direct(collect([kv_sum], [hidden_sum])[0])
+    own_kv = ctx_sum(collect([kv_sum], [hidden_sum])[0])
     heads_sum = ctx_sum(heads_terms, [hidden_sum])
     grad_query = heads_sum[:, :width]
     grad_output = heads_sum[:, width:].T

time: 471 us -> 473 us (level)
    ppermute x9 -> x12, waiting for transfers between devices: 38.8 us -> 49.1 us  [turn(): return lax.ppermute(part, 'ctx', [(i, (i + 1) % size) for i in range(size)])]
    ppermute x3 -> x0, waiting for transfers between devices: 8.15 us -> none  [ctx_sum_direct(): lax.ppermute(terms[step], 'ctx', [(i, (i - step) % size) for i in range(s...]
    ppermute x9 -> x12, starting transfers between devices: 6.83 us -> 14.3 us  [turn(): return lax.ppermute(part, 'ctx', [(i, (i + 1) % size) for i in range(size)])]
  transfers between devices with their start and end apart: 49 -> 49, of which waited for: 27 -> 26; matrix products, arithmetic and copies ran while one was open for 7% -> 7% of each run, Pallas kernels for 12% -> 12%
where the time goes in v4:
time: 473 us; the launch traced here: 468 us
  waiting for transfers between devices  257 us (54%)
  Pallas kernels  98.4 us (21%)
  starting transfers between devices  52.5 us (11%)
  other arithmetic  22.9 us (5%)
  between operations  15.4 us (3%)
  local copies, waits for them, and re-layouts  13.5 us (3%)
  matrix products  8.26 us (2%)
    ppermute x24, waiting for transfers between devices, flip(): return lax.ppermute(part, 'fsdp', [(i, i ^ bit) for i in range(size)])  89.5 us
    ppermute x12, waiting for transfers between devices, turn(): return lax.ppermute(part, 'ctx', [(i, (i + 1) % size) for i in range(size)])  49.1 us
    ppermute x3, waiting for transfers between devices, back_sum(): lax.ppermute(terms[step], 'ctx', [(i, i - step) for i in range(step, size)])  45 us
    pallas_call x1, Pallas kernels, ffn(): pl.pallas_call(kernel, out_shape=(shaped((2, rows, model)),) * 4 + (shape...  38.5 us
    ppermute x5, waiting for transfers between devices, swap(): return lax.ppermute(part, 'tp', [(0, 1), (1, 0)])  37.1 us
    ppermute x3, waiting for transfers between devices, back_slots(): lax.ppermute(part, 'ctx', [(i, i + step) for i in range(size - step)])  19.8 us
    ppermute x24, starting transfers between devices, flip(): return lax.ppermute(part, 'fsdp', [(i, i ^ bit) for i in range(size)])  16.7 us
    all_gather x1, waiting for transfers between devices, body(): lax.all_gather(block.reshape(-1, block.shape[-1]), 'ctx', axis=0, tiled=T...  16.1 us
  transfers between devices with their start and end apart: 49, of which 26 were waited for; matrix products, arithmetic and copies ran while one was open for 7% of the time, Pallas kernels for 12%

profile of v4, /device:TPU:0, one launch (start us, length us, event | category | flops | bytes accessed | tf_op | source)
XLA Modules:
  0.0 467.6 jit_solution(17140700611538536718)
XLA Ops:
  8.2 3.1 collective-permute-start.5
  11.4 3.1 split_columns.1
  18.1 2.2 collective-permute-done.5.refs_1_
  20.3 3.4 collective-permute-done.refs_1_
  24.1 8.7 %collective-permute-done.1.refs_2_ = bf16[112,512]{1,0:T(8,128)(2,1)S(1)} collective-permute-done((bf16[112,512]{1,0:T(8,128)(2,1)S(1)}, bf16[112,512]{1,0:T(8,128)(2,1)S(1)}, u32[]{:S(2)}, u32[]{:S(2)}) %collective-permute-start.1) | collective-permute-done | bytes 114720 | tf_op jit(solution)/shard_map/ppermute | solution.py:740
  32.8 6.6 %collective-permute-done.2.refs_3_.refs_4_ = bf16[112,512]{1,0:T(8,128)(2,1)S(1)} collective-permute-done((bf16[112,512]{1,0:T(8,128)(2,1)S(1)}, bf16[112,512]{1,0:T(8,128)(2,1)S(1)}, u32[]{:S(2)}, u32[]{:S(2)}) %collective-permute-start.2) | collective-permute-done | bytes 114720 | tf_op jit(solution)/shard_map/ppermute | solution.py:740
  40.2 3.4 collect.16
  47.4 9.6 %collective-permute-done.3.refs_1_.refs_2_.refs_4_ = bf16[4,112,512]{2,1,0:T(8,128)(2,1)S(1)} collective-permute-done((bf16[4,112,512]{2,1,0:T(8,128)(2,1)S(1)}, bf16[4,112,512]{2,1,0:T(8,128)(2,1)S(1)}, u32[]{:S(2)}, u32[]{:S(2)}) %collective-permute-start.3) | collective-permute-done | bytes 458784 | tf_op jit(solution)/shard_map/ppermute | solution.py:731
  62.4 23.5 %collective-permute-done.8.refs_1_.refs_2_ = bf16[4,96,1536]{2,1,0:T(8,128)(2,1)} collective-permute-done((bf16[4,96,1536]{2,1,0:T(8,128)(2,1)}, bf16[4,96,1536]{2,1,0:T(8,128)(2,1)}, u32[]{:S(2)}, u32[]{:S(2)}) %collective-permute-start.8) | collective-permute-done | bytes 1179680 | tf_op jit(solution)/shard_map/ppermute | solution.py:731
  85.9 2.9 collect.14
  91.1 4.4 arrange.2
  98.7 3.5 collective-permute-start.10
  102.3 3.7 collective-permute-start.11
  106.0 2.1 collective-permute-start.12
  108.3 5.3 %arrange.3 = (bf16[1536,768]{1,0:T(8,128)(2,1)}, bf16[1536,768]{1,0:T(8,128)(2,1)}) custom-call(s32[6]{0:T(128)S(1)} %pad_add_fusion.where_ref, bf16[4,96,1536]{2,1,0:T(8,128)(2,1)S(1)} %copy-done.2, bf16[2,4,96,1536]{3,2,1,0:T(8,128)(2,1)} %collective-permute-done.9.refs_1_, bf16[4,96,1536]{2,1,0:T(8,128)(2,1)} %collective-permute-done.8.refs_1_.refs_2_), custom_call_target="tpu_custom_call" | custom-call | flops 1800000000 | bytes 2000000 | tf_op jit(solution)/shard_map/arrange/pallas_call | solution.py:493
  113.6 3.3 fusion.37.q_ref
  117.0 8.8 %collective-permute-done.11.refs_2_ = bf16[256,512]{1,0:T(8,128)(2,1)} collective-permute-done((bf16[256,512]{1,0:T(8,128)(2,1)S(1)}, bf16[256,512]{1,0:T(8,128)(2,1)}, u32[]{:S(2)}, u32[]{:S(2)}) %collective-permute-start.11) | collective-permute-done | bytes 262176 | tf_op jit(solution)/shard_map/ppermute | solution.py:774
  125.7 11.0 %collective-permute-done.12.refs_3_ = bf16[256,512]{1,0:T(8,128)(2,1)} collective-permute-done((bf16[256,512]{1,0:T(8,128)(2,1)S(1)}, bf16[256,512]{1,0:T(8,128)(2,1)}, u32[]{:S(2)}, u32[]{:S(2)}) %collective-permute-start.12) | collective-permute-done | bytes 262176 | tf_op jit(solution)/shard_map/ppermute | solution.py:774
  136.8 6.6 %attend.1 = (bf16[256,768]{1,0:T(8,128)(2,1)S(1)}, bf16[256,768]{1,0:T(8,128)(2,1)}, f32[4,128,768]{2,1,0:T(8,128)}) custom-call(s32[6]{0:T(128)S(1)} %pad_add_fusion.where_ref, s32[2]{0:T(128)S(1)} %bitcast.117, f32[256,768]{1,0:T(8,128)} %fusion.37.q_ref, bf16[256,512]{1,0:T(8,128)(2,1)S(1)} %keys.1.refs_0_, ...), custom_call_target="tpu_custom_call" | custom-call | flops 12600000512 | bytes 14000000 | tf_op jit(solution)/shard_map/attend/pallas_call | solution.py:272
  143.4 2.8 convolution_convert_fusion
  149.4 16.0 %collective-permute-done.13 = bf16[256,1536]{1,0:T(8,128)(2,1)} collective-permute-done((bf16[256,1536]{1,0:T(8,128)(2,1)}, bf16[256,1536]{1,0:T(8,128)(2,1)}, u32[]{:S(2)}, u32[]{:S(2)}) %collective-permute-start.13) | collective-permute-done | bytes 786464 | tf_op jit(solution)/shard_map/ppermute | solution.py:735
  165.5 1.8 multiply_reduce_fusion.2
  169.7 15.8 %collective-permute-done.15.refs_2_ = bf16[256,1536]{1,0:T(8,128)(2,1)S(1)} collective-permute-done((bf16[256,1536]{1,0:T(8,128)(2,1)S(1)}, bf16[256,1536]{1,0:T(8,128)(2,1)S(1)}, u32[]{:S(2)}, u32[]{:S(2)}) %collective-permute-start.15) | collective-permute-done | bytes 786464 | tf_op jit(solution)/shard_map/ppermute | solution.py:731
  188.0 16.1 %all-gather.2.cloned.1.call-done = bf16[4608,864]{1,0:T(8,128)(2,1)} async-done(((bf16[1152,864]{1,0:T(8,128)(2,1)}), bf16[4608,864]{1,0:T(8,128)(2,1)}) %all-gather.2.cloned.1.call-update) | async-done | bytes 7962640 | tf_op jit(solution)/shard_map/all_gather | solution.py:875
  205.2 38.5 %ffn.1 = (bf16[2,256,1536]{2,1,0:T(8,128)(2,1)}, bf16[2,256,1536]{2,1,0:T(8,128)(2,1)}, bf16[2,256,1536]{2,1,0:T(8,128)(2,1)}, bf16[2,256,1536]{2,1,0:T(8,128)(2,1)}, bf16[4,4,3,96,864]{4,3,2,1,0:T(8,128)(2,1)}) custom-call(s32[6]{0:T(128)S(1)} %pad_add_fusion.where_ref, bf16[256,1536]{1,0:T(8,128)(2,1)S(1)} %multiply_convert_fusion.refs_0_, ...), custom_call_target="tpu_custom_call" | custom-call | flops 33300000768 | bytes 37000000 | tf_op jit(solution)/shard_map/ffn/pallas_call | solution.py:627
  243.8 3.6 collective-permute-done.23
  248.8 1.8 collective-permute-start.24
  250.6 17.9 %collective-permute-done.24 = bf16[256,1536]{1,0:T(8,128)(2,1)S(1)} collective-permute-done((bf16[256,1536]{1,0:T(8,128)(2,1)S(1)}, bf16[256,1536]{1,0:T(8,128)(2,1)S(1)}, u32[]{:S(2)}, u32[]{:S(2)}) %collective-permute-start.24) | collective-permute-done | bytes 786464 | tf_op jit(solution)/shard_map/ppermute | solution.py:731
  270.5 17.2 %collective-permute-done.25 = bf16[256,1536]{1,0:T(8,128)(2,1)S(1)} collective-permute-done((bf16[256,1536]{1,0:T(8,128)(2,1)S(1)}, bf16[256,1536]{1,0:T(8,128)(2,1)S(1)}, u32[]{:S(2)}, u32[]{:S(2)}) %collective-permute-start.25) | collective-permute-done | bytes 786464 | tf_op jit(solution)/shard_map/ppermute | solution.py:735
  288.4 1.8 fusion.29
  291.7 10.6 %attend_back.1 = (bf16[256,768]{1,0:T(8,128)(2,1)}, bf16[256,512]{1,0:T(8,128)(2,1)S(1)}, bf16[256,512]{1,0:T(8,128)(2,1)S(1)}, bf16[256,512]{1,0:T(8,128)(2,1)S...) custom-call(s32[6]{0:T(128)S(1)} %pad_add_fusion.where_ref, s32[2]{0:T(128)S(1)} %bitcast.118, ...), custom_call_target="tpu_custom_call" | custom-call | flops 15299999744 | bytes 17000000 | tf_op jit(solution)/shard_map/attend_back/pallas_call | solution.py:297
  303.3 5.5 %head_grads.2 = (bf16[2,4,96,1536]{3,2,1,0:T(8,128)(2,1)}, bf16[2,4,96,1536]{3,2,1,0:T(8,128)(2,1)}) custom-call(s32[6]{0:T(128)S(1)} %pad_add_fusion.where_ref, bf16[256,1536]{1,0:T(8,128)(2,1)S(1)} %fusion.3.refs_0_, bf16[256,1536]{1,0:T(8,128)(2,1)} %copy-done, bf16[256,768]{1,0:T(8,128)(2,1)S(1)} %copy-done.11, bf16[256,768]{1,0:T(8,128)(2,1)S(1)} %copy-done.10), custom_call_target="tpu_custom_call" | custom-call | flops 2700000000 | bytes 3000000 | tf_op jit(solution)/shard_map/head_grads/pallas_call | solution.py:714
  308.9 2.6 collect.17
  312.2 3.8 collective-permute-done.26
  316.0 2.6 fusion.15
  327.2 12.0 %collective-permute-done.27 = bf16[256,1536]{1,0:T(8,128)(2,1)S(1)} collective-permute-done((bf16[256,1536]{1,0:T(8,128)(2,1)}, bf16[256,1536]{1,0:T(8,128)(2,1)S(1)}, u32[]{:S(2)}, u32[]{:S(2)}) %collective-permute-start.27) | collective-permute-done | bytes 786464 | tf_op jit(solution)/shard_map/ppermute | solution.py:731
  342.5 11.1 %collective-permute-done.30 = bf16[256,512]{1,0:T(8,128)(2,1)S(1)} collective-permute-done((bf16[256,512]{1,0:T(8,128)(2,1)S(1)}, bf16[256,512]{1,0:T(8,128)(2,1)S(1)}, u32[]{:S(2)}, u32[]{:S(2)}) %collective-permute-start.30) | collective-permute-done | bytes 262176 | tf_op jit(solution)/shard_map/ppermute | solution.py:784
  353.6 34.0 %collective-permute-done.31 = bf16[256,512]{1,0:T(8,128)(2,1)S(1)} collective-permute-done((bf16[256,512]{1,0:T(8,128)(2,1)S(1)}, bf16[256,512]{1,0:T(8,128)(2,1)S(1)}, u32[]{:S(2)}, u32[]{:S(2)}) %collective-permute-start.31) | collective-permute-done | bytes 262176 | tf_op jit(solution)/shard_map/ppermute | solution.py:784
  388.7 3.6 normed_back.1
  392.2 4.1 head_grads.3
  396.4 1.8 fusion
  403.4 12.8 %collective-permute-done.41 = bf16[96,1536]{1,0:T(8,128)(2,1)S(1)} collective-permute-done((bf16[96,1536]{1,0:T(8,128)(2,1)S(1)}, bf16[96,1536]{1,0:T(8,128)(2,1)S(1)}, u32[]{:S(2)}, u32[]{:S(2)}) %collective-permute-start.41) | collective-permute-done | bytes 294944 | tf_op jit(solution)/shard_map/ppermute | solution.py:740
  416.5 2.4 collective-permute-done.34
  420.6 4.2 collective-permute-start.36
  431.9 7.8 %collective-permute-done.37 = bf16[112,512]{1,0:T(8,128)(2,1)S(1)} collective-permute-done((bf16[112,512]{1,0:T(8,128)(2,1)S(1)}, bf16[112,512]{1,0:T(8,128)(2,1)S(1)}, u32[]{:S(2)}, u32[]{:S(2)}) %collective-permute-start.37) | collective-permute-done | bytes 114720 | tf_op jit(solution)/shard_map/ppermute | solution.py:740
  440.0 7.7 %collective-permute-done.38 = bf16[112,512]{1,0:T(8,128)(2,1)S(1)} collective-permute-done((bf16[112,512]{1,0:T(8,128)(2,1)S(1)}, bf16[112,512]{1,0:T(8,128)(2,1)S(1)}, u32[]{:S(2)}, u32[]{:S(2)}) %collective-permute-start.38) | collective-permute-done | bytes 114720 | tf_op jit(solution)/shard_map/ppermute | solution.py:740
  452.4 2.4 collective-permute-done.46.refs_3_
  455.6 3.7 join_columns.1
  (231 shorter events, 71.0 us)
Async XLA Ops:
  7.2 196.9 %all-gather.2.cloned.1.call-start = ((), (), s32[]{:S(2)}) async-start(), calls=%async_computation.1 | async-start | bytes 10321920 | tf_op jit(solution)/shard_map/all_gather | solution.py:875
  8.2 12.1 %collective-permute-start.5 = (bf16[96,1536]{1,0:T(8,128)(2,1)S(1)}, bf16[96,1536]{1,0:T(8,128)(2,1)S(1)}, u32[]{:S(2)}, u32[]{:S(2)}) collective-permute-start(bf16[96,1536]{1,0:T(8,128)(2,1)S(1)} %pad_maximum_fusion.refs_0_), channel_id=1, source_target_pairs={{0,2},{2,4},{4,6},{6,0},{1,3},{3,5},{5,7},{7,1},{8,10},{10,12},{12... | collective-permute-start | bytes 884744 | tf_op jit(solution)/shard_map/ppermute | solution.py:740
  14.5 24.9 %collective-permute-start.20 = (bf16[3,96,864]{2,1,0:T(8,128)(2,1)S(1)}, bf16[3,96,864]{2,1,0:T(8,128)(2,1)S(1)}, u32[]{:S(2)}, u32[]{:S(2)}) collective-permute-start(bf16[3,96,864]{2,1,0:T(8,128)(2,1)S(1)} %get-tuple-element.64), channel_id=1, source_target_pairs={{0,8},{8,0},{16,24},{24,16},{1,9},{9,1},{17,25},{25,17},{2,10},{10... | collective-permute-start | bytes 1493000 | tf_op jit(solution)/shard_map/ppermute | solution.py:731
  14.5 24.9 %collective-permute-start.21 = (bf16[3,96,864]{2,1,0:T(8,128)(2,1)S(1)}, bf16[3,96,864]{2,1,0:T(8,128)(2,1)S(1)}, u32[]{:S(2)}, u32[]{:S(2)}) collective-permute-start(bf16[3,96,864]{2,1,0:T(8,128)(2,1)S(1)} %get-tuple-element.65), channel_id=1, source_target_pairs={{0,16},{8,24},{16,0},{24,8},{1,17},{9,25},{17,1},{25,9},{2,18},{10... | collective-permute-start | bytes 1493000 | tf_op jit(solution)/shard_map/ppermute | solution.py:731
  16.0 23.4 %collective-permute-start.22 = (bf16[3,96,864]{2,1,0:T(8,128)(2,1)}, bf16[3,96,864]{2,1,0:T(8,128)(2,1)S(1)}, u32[]{:S(2)}, u32[]{:S(2)}) collective-permute-start(bf16[3,96,864]{2,1,0:T(8,128)(2,1)} %get-tuple-element.66), channel_id=1, source_target_pairs={{0,24},{8,16},{16,8},{24,0},{1,25},{9,17},{17,9},{25,1},{2,26},{10... | collective-permute-start | bytes 1493000 | tf_op jit(solution)/shard_map/ppermute | solution.py:731
  16.5 7.2 %collective-permute-start = (bf16[112,512]{1,0:T(8,128)(2,1)S(1)}, bf16[112,512]{1,0:T(8,128)(2,1)S(1)}, u32[]{:S(2)}, u32[]{:S(2)}) collective-permute-start(bf16[112,512]{1,0:T(8,128)(2,1)S(1)} %fusion.23.refs_0_), channel_id=1, source_target_pairs={{0,2},{2,4},{4,6},{6,0},{1,3},{3,5},{5,7},{7,1},{8,10},{10,12},{12... | collective-permute-start | bytes 344072 | tf_op jit(solution)/shard_map/ppermute | solution.py:740
  20.3 19.1 %collective-permute-start.6 = (bf16[96,1536]{1,0:T(8,128)(2,1)S(1)}, bf16[96,1536]{1,0:T(8,128)(2,1)S(1)}, u32[]{:S(2)}, u32[]{:S(2)}) collective-permute-start(bf16[96,1536]{1,0:T(8,128)(2,1)S(1)} %collective-permute-done.5.refs_1_), channel_id=1, source_target_pairs={{0,2},{2,4},{4,6},{6,0},{1,3},{3,5},{5,7},{7,1},{8,10},{10,12},{12... | collective-permute-start | bytes 884744 | tf_op jit(solution)/shard_map/ppermute | solution.py:740
  23.7 9.1 %collective-permute-start.1 = (bf16[112,512]{1,0:T(8,128)(2,1)S(1)}, bf16[112,512]{1,0:T(8,128)(2,1)S(1)}, u32[]{:S(2)}, u32[]{:S(2)}) collective-permute-start(bf16[112,512]{1,0:T(8,128)(2,1)S(1)} %collective-permute-done.refs_1_), channel_id=1, source_target_pairs={{0,2},{2,4},{4,6},{6,0},{1,3},{3,5},{5,7},{7,1},{8,10},{10,12},{12... | collective-permute-start | bytes 344072 | tf_op jit(solution)/shard_map/ppermute | solution.py:740
  32.8 6.6 %collective-permute-start.2 = (bf16[112,512]{1,0:T(8,128)(2,1)S(1)}, bf16[112,512]{1,0:T(8,128)(2,1)S(1)}, u32[]{:S(2)}, u32[]{:S(2)}) collective-permute-start(bf16[112,512]{1,0:T(8,128)(2,1)S(1)} %collective-permute-done.1.refs_2_), channel_id=1, source_target_pairs={{0,2},{2,4},{4,6},{6,0},{1,3},{3,5},{5,7},{7,1},{8,10},{10,12},{12... | collective-permute-start | bytes 344072 | tf_op jit(solution)/shard_map/ppermute | solution.py:740
  43.6 376.6 %reduce-scatter.2.cloned.1.call-start = ((), (), s32[]{:S(2)}) async-start(), calls=%async_computation.2 | async-start | bytes 10321920 | tf_op jit(solution)/shard_map/reduce_scatter | solution.py:819
  44.3 12.7 %collective-permute-start.3 = (bf16[4,112,512]{2,1,0:T(8,128)(2,1)S(1)}, bf16[4,112,512]{2,1,0:T(8,128)(2,1)S(1)}, u32[]{:S(2)}, u32[]{:S(2)}) collective-permute-start(bf16[4,112,512]{2,1,0:T(8,128)(2,1)S(1)} %collect.11.refs_0_), channel_id=1, source_target_pairs={{0,16},{8,24},{16,0},{24,8},{1,17},{9,25},{17,1},{25,9},{2,18},{10... | collective-permute-start | bytes 1376264 | tf_op jit(solution)/shard_map/ppermute | solution.py:731
  45.8 11.2 %collective-permute-start.7 = (bf16[96,1536]{1,0:T(8,128)(2,1)S(1)}, bf16[96,1536]{1,0:T(8,128)(2,1)S(1)}, u32[]{:S(2)}, u32[]{:S(2)}) collective-permute-start(bf16[96,1536]{1,0:T(8,128)(2,1)S(1)} %collective-permute-done.6.refs_2_.refs_5_), channel_id=1, source_target_pairs={{0,2},{2,4},{4,6},{6,0},{1,3},{3,5},{5,7},{7,1},{8,10},{10,12},{12... | collective-permute-start | bytes 884744 | tf_op jit(solution)/shard_map/ppermute | solution.py:740
  58.3 27.6 %collective-permute-start.8 = (bf16[4,96,1536]{2,1,0:T(8,128)(2,1)}, bf16[4,96,1536]{2,1,0:T(8,128)(2,1)}, u32[]{:S(2)}, u32[]{:S(2)}) collective-permute-start(bf16[4,96,1536]{2,1,0:T(8,128)(2,1)} %collect.13.refs_0_), channel_id=1, source_target_pairs={{0,16},{8,24},{16,0},{24,8},{1,17},{9,25},{17,1},{25,9},{2,18},{10... | collective-permute-start | bytes 3538952 | tf_op jit(solution)/shard_map/ppermute | solution.py:731
  62.3 27.9 %collective-permute-start.4 = (bf16[2,4,112,512]{3,2,1,0:T(8,128)(2,1)S(1)}, bf16[2,4,112,512]{3,2,1,0:T(8,128)(2,1)S(1)}, u32[]{:S(2)}, u32[]{:S(2)}) collective-permute-start(bf16[2,4,112,512]{3,2,1,0:T(8,128)(2,1)S(1)} %collect.12), channel_id=1, source_target_pairs={{0,8},{8,0},{16,24},{24,16},{1,9},{9,1},{17,25},{25,17},{2,10},{10... | collective-permute-start | bytes 2752520 | tf_op jit(solution)/shard_map/ppermute | solution.py:731
  88.8 19.5 %collective-permute-start.9 = (bf16[2,4,96,1536]{3,2,1,0:T(8,128)(2,1)}, bf16[2,4,96,1536]{3,2,1,0:T(8,128)(2,1)}, u32[]{:S(2)}, u32[]{:S(2)}) collective-permute-start(bf16[2,4,96,1536]{3,2,1,0:T(8,128)(2,1)} %collect.14), channel_id=1, source_target_pairs={{0,8},{8,0},{16,24},{24,16},{1,9},{9,1},{17,25},{25,17},{2,10},{10... | collective-permute-start | bytes 7077896 | tf_op jit(solution)/shard_map/ppermute | solution.py:731
  98.7 18.2 %collective-permute-start.10 = (bf16[256,512]{1,0:T(8,128)(2,1)S(1)}, bf16[256,512]{1,0:T(8,128)(2,1)S(1)}, u32[]{:S(2)}, u32[]{:S(2)}) collective-permute-start(bf16[256,512]{1,0:T(8,128)(2,1)S(1)} %keys.1.refs_0_), channel_id=1, source_target_pairs={{0,2},{2,4},{4,6},{1,3},{3,5},{5,7},{8,10},{10,12},{12,14},{9,11},... | collective-permute-start | bytes 786440 | tf_op jit(solution)/shard_map/ppermute | solution.py:774
  102.3 23.5 %collective-permute-start.11 = (bf16[256,512]{1,0:T(8,128)(2,1)S(1)}, bf16[256,512]{1,0:T(8,128)(2,1)}, u32[]{:S(2)}, u32[]{:S(2)}) collective-permute-start(bf16[256,512]{1,0:T(8,128)(2,1)S(1)} %keys.1.refs_0_), channel_id=1, source_target_pairs={{0,4},{2,6},{1,5},{3,7},{8,12},{10,14},{9,13},{11,15},{16,20},{18,... | collective-permute-start | bytes 786440 | tf_op jit(solution)/shard_map/ppermute | solution.py:774
  106.0 30.8 %collective-permute-start.12 = (bf16[256,512]{1,0:T(8,128)(2,1)S(1)}, bf16[256,512]{1,0:T(8,128)(2,1)}, u32[]{:S(2)}, u32[]{:S(2)}) collective-permute-start(bf16[256,512]{1,0:T(8,128)(2,1)S(1)} %keys.1.refs_0_), channel_id=1, source_target_pairs={{0,6},{1,7},{8,14},{9,15},{16,22},{17,23},{24,30},{25,31}} | collective-permute-start | bytes 786440 | tf_op jit(solution)/shard_map/ppermute | solution.py:774
  146.3 19.2 %collective-permute-start.13 = (bf16[256,1536]{1,0:T(8,128)(2,1)}, bf16[256,1536]{1,0:T(8,128)(2,1)}, u32[]{:S(2)}, u32[]{:S(2)}) collective-permute-start(bf16[256,1536]{1,0:T(8,128)(2,1)} %convolution_convert_fusion), channel_id=1, source_target_pairs={{0,1},{1,0},{2,3},{3,2},{4,5},{5,4},{6,7},{7,6},{8,9},{9,8},{10,11... | collective-permute-start | bytes 2359304 | tf_op jit(solution)/shard_map/ppermute | solution.py:735
  147.9 21.1 %collective-permute-start.18 = (bf16[256,1536]{1,0:T(8,128)(2,1)S(1)}, bf16[256,1536]{1,0:T(8,128)(2,1)S(1)}, u32[]{:S(2)}, u32[]{:S(2)}) collective-permute-start(bf16[256,1536]{1,0:T(8,128)(2,1)S(1)} %bitcast.119), channel_id=1, source_target_pairs={{0,16},{8,24},{16,0},{24,8},{1,17},{9,25},{17,1},{25,9},{2,18},{10... | collective-permute-start | bytes 2359304 | tf_op jit(solution)/shard_map/ppermute | solution.py:731
  167.5 18.0 %collective-permute-start.15 = (bf16[256,1536]{1,0:T(8,128)(2,1)S(1)}, bf16[256,1536]{1,0:T(8,128)(2,1)S(1)}, u32[]{:S(2)}, u32[]{:S(2)}) collective-permute-start(bf16[256,1536]{1,0:T(8,128)(2,1)S(1)} %multiply_convert_fusion.refs_0_), channel_id=1, source_target_pairs={{0,16},{8,24},{16,0},{24,8},{1,17},{9,25},{17,1},{25,9},{2,18},{10... | collective-permute-start | bytes 2359304 | tf_op jit(solution)/shard_map/ppermute | solution.py:731
  169.1 16.5 %collective-permute-start.17 = (bf16[256,1536]{1,0:T(8,128)(2,1)S(1)}, bf16[256,1536]{1,0:T(8,128)(2,1)S(1)}, u32[]{:S(2)}, u32[]{:S(2)}) collective-permute-start(bf16[256,1536]{1,0:T(8,128)(2,1)S(1)} %bitcast.120), channel_id=1, source_target_pairs={{0,8},{8,0},{16,24},{24,16},{1,9},{9,1},{17,25},{25,17},{2,10},{10... | collective-permute-start | bytes 2359304 | tf_op jit(solution)/shard_map/ppermute | solution.py:731
  169.1 16.5 %collective-permute-start.19 = (bf16[256,1536]{1,0:T(8,128)(2,1)S(1)}, bf16[256,1536]{1,0:T(8,128)(2,1)S(1)}, u32[]{:S(2)}, u32[]{:S(2)}) collective-permute-start(bf16[256,1536]{1,0:T(8,128)(2,1)S(1)} %collective-permute-done.18.refs_6_), channel_id=1, source_target_pairs={{0,8},{8,0},{16,24},{24,16},{1,9},{9,1},{17,25},{25,17},{2,10},{10... | collective-permute-start | bytes 2359304 | tf_op jit(solution)/shard_map/ppermute | solution.py:731
  169.6 16.0 %collective-permute-start.14 = (bf16[256,1536]{1,0:T(8,128)(2,1)S(1)}, bf16[256,1536]{1,0:T(8,128)(2,1)S(1)}, u32[]{:S(2)}, u32[]{:S(2)}) collective-permute-start(bf16[256,1536]{1,0:T(8,128)(2,1)S(1)} %multiply_convert_fusion.refs_0_), channel_id=1, source_target_pairs={{0,8},{8,0},{16,24},{24,16},{1,9},{9,1},{17,25},{25,17},{2,10},{10... | collective-permute-start | bytes 2359304 | tf_op jit(solution)/shard_map/ppermute | solution.py:731
  243.8 3.7 collective-permute-start.23
  248.8 19.6 %collective-permute-start.24 = (bf16[256,1536]{1,0:T(8,128)(2,1)S(1)}, bf16[256,1536]{1,0:T(8,128)(2,1)S(1)}, u32[]{:S(2)}, u32[]{:S(2)}) collective-permute-start(bf16[256,1536]{1,0:T(8,128)(2,1)S(1)} %fusion.14), channel_id=1, source_target_pairs={{0,16},{8,24},{16,0},{24,8},{1,17},{9,25},{17,1},{25,9},{2,18},{10... | collective-permute-start | bytes 2359304 | tf_op jit(solution)/shard_map/ppermute | solution.py:731
  268.7 18.9 %collective-permute-start.25 = (bf16[256,1536]{1,0:T(8,128)(2,1)S(1)}, bf16[256,1536]{1,0:T(8,128)(2,1)S(1)}, u32[]{:S(2)}, u32[]{:S(2)}) collective-permute-start(bf16[256,1536]{1,0:T(8,128)(2,1)S(1)} %fusion.10), channel_id=1, source_target_pairs={{0,1},{1,0},{2,3},{3,2},{4,5},{5,4},{6,7},{7,6},{8,9},{9,8},{10,11... | collective-permute-start | bytes 2359304 | tf_op jit(solution)/shard_map/ppermute | solution.py:735
  308.8 11.5 %collective-permute-start.29 = (bf16[2,4,96,1536]{3,2,1,0:T(8,128)(2,1)}, bf16[2,4,96,1536]{3,2,1,0:T(8,128)(2,1)}, u32[]{:S(2)}, u32[]{:S(2)}) collective-permute-start(bf16[2,4,96,1536]{3,2,1,0:T(8,128)(2,1)} %get-tuple-element.80), channel_id=1, source_target_pairs={{0,8},{8,0},{16,24},{24,16},{1,9},{9,1},{17,25},{25,17},{2,10},{10... | collective-permute-start | bytes 7077896 | tf_op jit(solution)/shard_map/ppermute | solution.py:731
  311.5 4.5 collective-permute-start.26
  318.6 20.6 %collective-permute-start.27 = (bf16[256,1536]{1,0:T(8,128)(2,1)}, bf16[256,1536]{1,0:T(8,128)(2,1)S(1)}, u32[]{:S(2)}, u32[]{:S(2)}) collective-permute-start(bf16[256,1536]{1,0:T(8,128)(2,1)} %fusion.15), channel_id=1, source_target_pairs={{0,16},{8,24},{16,0},{24,8},{1,17},{9,25},{17,1},{25,9},{2,18},{10... | collective-permute-start | bytes 2359304 | tf_op jit(solution)/shard_map/ppermute | solution.py:731
  322.0 74.4 %collective-permute-start.40 = (bf16[4,96,1536]{2,1,0:T(8,128)(2,1)S(1)}, bf16[4,96,1536]{2,1,0:T(8,128)(2,1)S(1)}, u32[]{:S(2)}, u32[]{:S(2)}) collective-permute-start(bf16[4,96,1536]{2,1,0:T(8,128)(2,1)S(1)} %fusion.12.refs_3_), channel_id=1, source_target_pairs={{0,16},{8,24},{16,0},{24,8},{1,17},{9,25},{17,1},{25,9},{2,18},{10... | collective-permute-start | bytes 3538952 | tf_op jit(solution)/shard_map/ppermute | solution.py:731
  323.2 30.4 %collective-permute-start.30 = (bf16[256,512]{1,0:T(8,128)(2,1)S(1)}, bf16[256,512]{1,0:T(8,128)(2,1)S(1)}, u32[]{:S(2)}, u32[]{:S(2)}) collective-permute-start(bf16[256,512]{1,0:T(8,128)(2,1)S(1)} %get-tuple-element.101), channel_id=1, source_target_pairs={{2,0},{4,2},{6,4},{3,1},{5,3},{7,5},{10,8},{12,10},{14,12},{11,9},... | collective-permute-start | bytes 786440 | tf_op jit(solution)/shard_map/ppermute | solution.py:784
  324.6 62.9 %collective-permute-start.31 = (bf16[256,512]{1,0:T(8,128)(2,1)S(1)}, bf16[256,512]{1,0:T(8,128)(2,1)S(1)}, u32[]{:S(2)}, u32[]{:S(2)}) collective-permute-start(bf16[256,512]{1,0:T(8,128)(2,1)S(1)} %get-tuple-element.103), channel_id=1, source_target_pairs={{4,0},{6,2},{5,1},{7,3},{12,8},{14,10},{13,9},{15,11},{20,16},{22,... | collective-permute-start | bytes 786440 | tf_op jit(solution)/shard_map/ppermute | solution.py:784
  325.9 61.6 %collective-permute-start.32 = (bf16[256,512]{1,0:T(8,128)(2,1)S(1)}, bf16[256,512]{1,0:T(8,128)(2,1)S(1)}, u32[]{:S(2)}, u32[]{:S(2)}) collective-permute-start(bf16[256,512]{1,0:T(8,128)(2,1)S(1)} %get-tuple-element.102), channel_id=1, source_target_pairs={{6,0},{7,1},{14,8},{15,9},{22,16},{23,17},{30,24},{31,25}} | collective-permute-start | bytes 786440 | tf_op jit(solution)/shard_map/ppermute | solution.py:784
  340.7 60.1 %collective-permute-start.28 = (bf16[256,1536]{1,0:T(8,128)(2,1)S(1)}, bf16[256,1536]{1,0:T(8,128)(2,1)S(1)}, u32[]{:S(2)}, u32[]{:S(2)}) collective-permute-start(bf16[256,1536]{1,0:T(8,128)(2,1)S(1)} %fusion.9), channel_id=1, source_target_pairs={{0,1},{1,0},{2,3},{3,2},{4,5},{5,4},{6,7},{7,6},{8,9},{9,8},{10,11... | collective-permute-start | bytes 2359304 | tf_op jit(solution)/shard_map/ppermute | solution.py:735
  396.3 2.7 collective-permute-start.33
  398.3 17.9 %collective-permute-start.41 = (bf16[96,1536]{1,0:T(8,128)(2,1)S(1)}, bf16[96,1536]{1,0:T(8,128)(2,1)S(1)}, u32[]{:S(2)}, u32[]{:S(2)}) collective-permute-start(bf16[96,1536]{1,0:T(8,128)(2,1)S(1)} %slice_bitcast_fusion.4), channel_id=1, source_target_pairs={{0,2},{2,4},{4,6},{6,0},{1,3},{3,5},{5,7},{7,1},{8,10},{10,12},{12... | collective-permute-start | bytes 884744 | tf_op jit(solution)/shard_map/ppermute | solution.py:740
  399.3 19.6 %collective-permute-start.34 = (bf16[256,1536]{1,0:T(8,128)(2,1)S(1)}, bf16[256,1536]{1,0:T(8,128)(2,1)S(1)}, u32[]{:S(2)}, u32[]{:S(2)}) collective-permute-start(bf16[256,1536]{1,0:T(8,128)(2,1)S(1)} %bitcast.114), channel_id=1, source_target_pairs={{0,1},{1,0},{2,3},{3,2},{4,5},{5,4},{6,7},{7,6},{8,9},{9,8},{10,11... | collective-permute-start | bytes 2359304 | tf_op jit(solution)/shard_map/ppermute | solution.py:735
  402.0 14.3 %collective-permute-start.35 = (bf16[4,112,512]{2,1,0:T(8,128)(2,1)S(1)}, bf16[4,112,512]{2,1,0:T(8,128)(2,1)S(1)}, u32[]{:S(2)}, u32[]{:S(2)}) collective-permute-start(bf16[4,112,512]{2,1,0:T(8,128)(2,1)S(1)} %fusion.19.refs_1_), channel_id=1, source_target_pairs={{0,16},{8,24},{16,0},{24,8},{1,17},{9,25},{17,1},{25,9},{2,18},{10... | collective-permute-start | bytes 1376264 | tf_op jit(solution)/shard_map/ppermute | solution.py:731
  420.6 7.6 %collective-permute-start.36 = (bf16[112,512]{1,0:T(8,128)(2,1)S(1)}, bf16[112,512]{1,0:T(8,128)(2,1)S(1)}, u32[]{:S(2)}, u32[]{:S(2)}) collective-permute-start(bf16[112,512]{1,0:T(8,128)(2,1)S(1)} %slice_bitcast_fusion.11), channel_id=1, source_target_pairs={{0,2},{2,4},{4,6},{6,0},{1,3},{3,5},{5,7},{7,1},{8,10},{10,12},{12... | collective-permute-start | bytes 344072 | tf_op jit(solution)/shard_map/ppermute | solution.py:740
  426.6 13.2 %collective-permute-start.42 = (bf16[96,1536]{1,0:T(8,128)(2,1)S(1)}, bf16[96,1536]{1,0:T(8,128)(2,1)S(1)}, u32[]{:S(2)}, u32[]{:S(2)}) collective-permute-start(bf16[96,1536]{1,0:T(8,128)(2,1)S(1)} %bitcast.122), channel_id=1, source_target_pairs={{0,2},{2,4},{4,6},{6,0},{1,3},{3,5},{5,7},{7,1},{8,10},{10,12},{12... | collective-permute-start | bytes 884744 | tf_op jit(solution)/shard_map/ppermute | solution.py:740
  428.2 11.5 %collective-permute-start.37 = (bf16[112,512]{1,0:T(8,128)(2,1)S(1)}, bf16[112,512]{1,0:T(8,128)(2,1)S(1)}, u32[]{:S(2)}, u32[]{:S(2)}) collective-permute-start(bf16[112,512]{1,0:T(8,128)(2,1)S(1)} %fusion.21), channel_id=1, source_target_pairs={{0,2},{2,4},{4,6},{6,0},{1,3},{3,5},{5,7},{7,1},{8,10},{10,12},{12... | collective-permute-start | bytes 344072 | tf_op jit(solution)/shard_map/ppermute | solution.py:740
  430.0 22.4 %collective-permute-start.44 = (bf16[3,96,864]{2,1,0:T(8,128)(2,1)S(1)}, bf16[3,96,864]{2,1,0:T(8,128)(2,1)S(1)}, u32[]{:S(2)}, u32[]{:S(2)}) collective-permute-start(bf16[3,96,864]{2,1,0:T(8,128)(2,1)S(1)} %bitcast.131), channel_id=1, source_target_pairs={{0,8},{8,0},{16,24},{24,16},{1,9},{9,1},{17,25},{25,17},{2,10},{10... | collective-permute-start | bytes 1493000 | tf_op jit(solution)/shard_map/ppermute | solution.py:731
  430.1 22.4 %collective-permute-start.45 = (bf16[3,96,864]{2,1,0:T(8,128)(2,1)S(1)}, bf16[3,96,864]{2,1,0:T(8,128)(2,1)S(1)}, u32[]{:S(2)}, u32[]{:S(2)}) collective-permute-start(bf16[3,96,864]{2,1,0:T(8,128)(2,1)S(1)} %bitcast.130), channel_id=1, source_target_pairs={{0,16},{8,24},{16,0},{24,8},{1,17},{9,25},{17,1},{25,9},{2,18},{10... | collective-permute-start | bytes 1493000 | tf_op jit(solution)/shard_map/ppermute | solution.py:731
  431.6 23.2 %collective-permute-start.46 = (bf16[3,96,864]{2,1,0:T(8,128)(2,1)S(1)}, bf16[3,96,864]{2,1,0:T(8,128)(2,1)S(1)}, u32[]{:S(2)}, u32[]{:S(2)}) collective-permute-start(bf16[3,96,864]{2,1,0:T(8,128)(2,1)S(1)} %bitcast.129), channel_id=1, source_target_pairs={{0,24},{8,16},{16,8},{24,0},{1,25},{9,17},{17,9},{25,1},{2,26},{10... | collective-permute-start | bytes 1493000 | tf_op jit(solution)/shard_map/ppermute | solution.py:731
  439.8 7.9 %collective-permute-start.38 = (bf16[112,512]{1,0:T(8,128)(2,1)S(1)}, bf16[112,512]{1,0:T(8,128)(2,1)S(1)}, u32[]{:S(2)}, u32[]{:S(2)}) collective-permute-start(bf16[112,512]{1,0:T(8,128)(2,1)S(1)} %fusion.20), channel_id=1, source_target_pairs={{0,2},{2,4},{4,6},{6,0},{1,3},{3,5},{5,7},{7,1},{8,10},{10,12},{12... | collective-permute-start | bytes 344072 | tf_op jit(solution)/shard_map/ppermute | solution.py:740
  439.9 19.4 %collective-permute-start.43 = (bf16[96,1536]{1,0:T(8,128)(2,1)S(1)}, bf16[96,1536]{1,0:T(8,128)(2,1)S(1)}, u32[]{:S(2)}, u32[]{:S(2)}) collective-permute-start(bf16[96,1536]{1,0:T(8,128)(2,1)S(1)} %fusion.17), channel_id=1, source_target_pairs={{0,2},{2,4},{4,6},{6,0},{1,3},{3,5},{5,7},{7,1},{8,10},{10,12},{12... | collective-permute-start | bytes 884744 | tf_op jit(solution)/shard_map/ppermute | solution.py:740
  447.7 3.6 collective-permute-start.39
  (45 other events, 324.9 us)
Sparse Core Ops, SparseCore 0:
  43.7 160.2 all-gather.1
  243.9 173.5 reduce-scatter.1
